TPU v7x, 32 devices: a whole 2x2x4 slice. The times are simulated.
32 devices in a mesh: dp: 16 (over z, y, x), tensor: 2 (over core).
Axes of the slice: x: 2, y: 2, z: 4, core: 2. Of those that a mesh axis runs over, the one named last changes fastest.
Arguments:
- latents: float32 [32, 16, 256], P('dp', None, 'tensor'), may hold values from -6 to 6
- gaussian: float32 [32, 16, 256], P('dp', None, 'tensor'), may hold values from -6 to 6
- velocity: float32 [32, 16, 256], P('dp', None, 'tensor'), may hold values from -6 to 6
- time_ids: int32 [32], P('dp'), may hold values from 0 to 999, as said below
- labels: int32 [32], P('dp'), may hold values from 0 to 1000
- small_w: float32 [288, 768], replicated
- small_m: float32 [288, 768], replicated, may hold values from -0.0009765625 to 0.0009765625
- small_v: float32 [288, 768], replicated, may hold values from 1.904297e-09 to 7.629395e-09
- cond_w: float32 [1769, 768], P(None, 'dp')
- cond_m: float32 [1769, 768], P(None, 'dp'), may hold values from -0.0009765625 to 0.0009765625
- cond_v: float32 [1769, 768], P(None, 'dp'), as said below
- mod_w: float32 [768, 10752], P('dp')
- mod_m: float32 [768, 10752], P('dp'), may hold values from -0.0009765625 to 0.0009765625
- mod_v: float32 [768, 10752], P('dp'), as said below
- qkv_w: float32 [2, 768, 3, 768], P(None, 'dp', None, 'tensor')
- qkv_m: float32 [2, 768, 3, 768], P(None, 'dp', None, 'tensor'), may hold values from -0.0009765625 to 0.0009765625
- qkv_v: float32 [2, 768, 3, 768], P(None, 'dp', None, 'tensor'), as said below
- proj_w: float32 [2, 768, 768], P(None, 'tensor', 'dp')
- proj_m: float32 [2, 768, 768], P(None, 'tensor', 'dp'), may hold values from -0.0009765625 to 0.0009765625
- proj_v: float32 [2, 768, 768], P(None, 'tensor', 'dp'), as said below
- up_w: float32 [2, 768, 3072], P(None, 'dp', 'tensor')
- up_m: float32 [2, 768, 3072], P(None, 'dp', 'tensor'), may hold values from -0.0009765625 to 0.0009765625
- up_v: float32 [2, 768, 3072], P(None, 'dp', 'tensor'), as said below
- down_w: float32 [2, 3072, 768], P(None, 'tensor', 'dp')
- down_m: float32 [2, 3072, 768], P(None, 'tensor', 'dp'), may hold values from -0.0009765625 to 0.0009765625
- down_v: float32 [2, 3072, 768], P(None, 'tensor', 'dp'), as said below
Outputs:
- small_new: float32 [288, 768], replicated
- small_m_new: float32 [288, 768], replicated
- small_v_new: float32 [288, 768], replicated
- cond_new: float32 [1769, 768], P(None, 'dp')
- cond_m_new: float32 [1769, 768], P(None, 'dp')
- cond_v_new: float32 [1769, 768], P(None, 'dp')
- mod_new: float32 [768, 10752], P('dp')
- mod_m_new: float32 [768, 10752], P('dp')
- mod_v_new: float32 [768, 10752], P('dp')
- qkv_new: float32 [2, 768, 3, 768], P(None, 'dp', None, 'tensor')
- qkv_m_new: float32 [2, 768, 3, 768], P(None, 'dp', None, 'tensor')
- qkv_v_new: float32 [2, 768, 3, 768], P(None, 'dp', None, 'tensor')
- proj_new: float32 [2, 768, 768], P(None, 'tensor', 'dp')
- proj_m_new: float32 [2, 768, 768], P(None, 'tensor', 'dp')
- proj_v_new: float32 [2, 768, 768], P(None, 'tensor', 'dp')
- up_new: float32 [2, 768, 3072], P(None, 'dp', 'tensor')
- up_m_new: float32 [2, 768, 3072], P(None, 'dp', 'tensor')
- up_v_new: float32 [2, 768, 3072], P(None, 'dp', 'tensor')
- down_new: float32 [2, 3072, 768], P(None, 'tensor', 'dp')
- down_m_new: float32 [2, 3072, 768], P(None, 'tensor', 'dp')
- down_v_new: float32 [2, 3072, 768], P(None, 'tensor', 'dp')
- loss_sum: float32 [], replicated
- norms: float32 [2, 11], replicated
Inputs may be any that keep to these rules, and one draw needn't show every extreme that they name: time_ids[b] is at least b * 1000 // 32 and less than that plus max(2, 31). `cond_v`: positive. `mod_v`: positive. `qkv_v`: positive. `proj_v`: positive. `up_v`: positive. `down_v`: positive.
All inputs are finite; a program needn't handle non-finite values.
Results may differ from a plain program's by a relative error of at most 0.015.
The roundings to bfloat16 on the way count: a program that leaves them out, or rounds other values in their place, can miss the bound.
Values may be sent and summed in bfloat16 or wider, within the bound.
A program may use at most 256 MiB of HBM per device.

v0:
```python
import math

import jax
import jax.numpy as jnp
from jax import lax
from jax.sharding import PartitionSpec as P

HDIM = 64
PATCH = 16
GRID = 16
FREQ = 256
CLASSES = 1001
TSTEPS = 1000
STEP = 10


HIGHEST_PREC = lax.Precision.HIGHEST
BETA_ONE = 0.9
BETA_TWO = 0.999
EPS_ADAM = 1e-06
EPS_LAYER = 1e-06
EPS_NORM = 1e-12
WEIGHT_DECAY = 0.01
LEARN_RATE = 0.25


def time_features(moment):
    half_freq = FREQ // 2
    frequency = jnp.exp(-math.log(10000.0) * jnp.arange(half_freq).astype(jnp.float32) / half_freq)
    angles = (1000.0 * moment)[:, None] * frequency[None, :]
    return jnp.concatenate([jnp.cos(angles), jnp.sin(angles)], axis=1)


def position_table(token_index, model_width):
    quarter = model_width // 4
    omega_rate = 1.0 / 10000.0 ** (jnp.arange(quarter).astype(jnp.float32) / quarter)
    grid_row = (token_index // GRID).astype(jnp.float32)[:, None] * omega_rate[None, :]
    grid_col = (token_index % GRID).astype(jnp.float32)[:, None] * omega_rate[None, :]
    return jnp.concatenate(
        [jnp.sin(grid_col), jnp.cos(grid_col), jnp.sin(grid_row), jnp.cos(grid_row)], axis=1
    )


def modulated_norm(hidden_in, shift_vec, scale_vec):
    centre = hidden_in - jnp.mean(hidden_in, axis=-1, keepdims=True)
    spread = jnp.mean(centre * centre, axis=-1, keepdims=True)
    return (
        centre * lax.rsqrt(spread + EPS_LAYER) * (1.0 + scale_vec[:, None, :])
        + shift_vec[:, None, :]
    )


def lamb_parts(weight, first, second, grad):
    first_new = BETA_ONE * first + (1.0 - BETA_ONE) * grad
    second_new = BETA_TWO * second + (1.0 - BETA_TWO) * grad * grad
    update = (
        first_new
        / (1.0 - BETA_ONE**STEP)
        / (jnp.sqrt(second_new / (1.0 - BETA_TWO**STEP)) + EPS_ADAM)
        + WEIGHT_DECAY * weight
    )
    return (first_new, second_new, update)


def gelu_tanh(values_in):
    return jax.nn.gelu(values_in, approximate=True)


def spread_rows(part_rows):
    return lax.all_gather(part_rows, "tensor", axis=1, tiled=True)


def fold_rows(term_rows):
    return lax.psum_scatter(
        term_rows.astype(jnp.bfloat16), "tensor", scatter_dimension=1, tiled=True
    ).astype(jnp.float32)


def fetch_layer(qkv_w, proj_w, up_w, down_w, layer_id):
    return (
        lax.all_gather(qkv_w[layer_id].astype(jnp.bfloat16), "dp", axis=0, tiled=True),
        lax.all_gather(proj_w[layer_id].astype(jnp.bfloat16), "dp", axis=1, tiled=True),
        lax.all_gather(up_w[layer_id].astype(jnp.bfloat16), "dp", axis=0, tiled=True),
        lax.all_gather(down_w[layer_id].astype(jnp.bfloat16), "dp", axis=1, tiled=True),
    )


def split_heads(gathered, w_qkv):
    mixed = jnp.einsum("bnd,dte->bnte", gathered, w_qkv, preferred_element_type=jnp.float32).astype(
        jnp.bfloat16
    )
    shaped = mixed.reshape(mixed.shape[0], mixed.shape[1], 3, -1, HDIM)
    return (shaped[:, :, 0], shaped[:, :, 1], shaped[:, :, 2])


def score_block(queries, key_heads):
    return jnp.einsum(
        "bnhe,bmhe->bhnm", queries, key_heads, preferred_element_type=jnp.float32
    ) * HDIM ** (-0.5)


def block_forward(hidden, layer_mod, weights):
    w_qkv, w_proj, w_up, w_down = weights
    normed = modulated_norm(hidden, layer_mod[:, 0], layer_mod[:, 1]).astype(jnp.bfloat16)
    gathered = spread_rows(normed)
    queries, key_heads, values = split_heads(gathered, w_qkv)
    scores = score_block(queries, key_heads)
    row_top = jnp.max(scores, axis=-1, keepdims=True)
    logsum = row_top + jnp.log(jnp.sum(jnp.exp(scores - row_top), axis=-1, keepdims=True))
    softmax_w = jnp.exp(scores - logsum).astype(jnp.bfloat16)
    attended = jnp.einsum(
        "bhnm,bmhe->bnhe", softmax_w, values, preferred_element_type=jnp.float32
    ).astype(jnp.bfloat16)
    attended = attended.reshape(attended.shape[0], attended.shape[1], -1)
    branch = fold_rows(
        jnp.einsum("bne,ed->bnd", attended, w_proj, preferred_element_type=jnp.float32)
    )
    middle = hidden + layer_mod[:, 2][:, None, :] * branch
    normed_two = modulated_norm(middle, layer_mod[:, 3], layer_mod[:, 4]).astype(jnp.bfloat16)
    gathered_two = spread_rows(normed_two)
    inner_pre = jnp.einsum("bnd,df->bnf", gathered_two, w_up, preferred_element_type=jnp.float32)
    activ = gelu_tanh(inner_pre).astype(jnp.bfloat16)
    outer_out = fold_rows(
        jnp.einsum("bnf,fd->bnd", activ, w_down, preferred_element_type=jnp.float32)
    )
    output = middle + layer_mod[:, 5][:, None, :] * outer_out
    saved_state = (
        hidden,
        gathered,
        queries,
        key_heads,
        values,
        attended,
        logsum,
        branch,
        middle,
        gathered_two,
        inner_pre,
        outer_out,
    )
    return (output, saved_state)


def block_backward(grad_out, layer_mod, weights, saved_state):
    (
        hidden,
        gathered,
        queries,
        key_heads,
        values,
        attended,
        logsum,
        branch,
        middle,
        gathered_two,
        inner_pre,
        outer_out,
    ) = saved_state
    w_qkv, w_proj, w_up, w_down = weights
    grad_gate_m = jnp.sum(grad_out * outer_out, axis=1)
    grad_outer = spread_rows((layer_mod[:, 5][:, None, :] * grad_out).astype(jnp.bfloat16))
    activ = gelu_tanh(inner_pre).astype(jnp.bfloat16)
    grad_down = jnp.einsum("bnf,bnd->fd", activ, grad_outer, preferred_element_type=jnp.float32)
    grad_activ = jnp.einsum("bnd,fd->bnf", grad_outer, w_down, preferred_element_type=jnp.float32)
    _, gelu_back = jax.vjp(gelu_tanh, inner_pre)
    grad_inner = gelu_back(grad_activ)[0].astype(jnp.bfloat16)
    grad_up = jnp.einsum(
        "bnd,bnf->df", gathered_two, grad_inner, preferred_element_type=jnp.float32
    )
    grad_normed_two = fold_rows(
        jnp.einsum("bnf,df->bnd", grad_inner, w_up, preferred_element_type=jnp.float32)
    )
    _, norm_back = jax.vjp(modulated_norm, middle, layer_mod[:, 3], layer_mod[:, 4])
    grad_middle, grad_shift_m, grad_scale_m = norm_back(grad_normed_two)
    grad_middle = grad_middle + grad_out
    grad_gate_a = jnp.sum(grad_middle * branch, axis=1)
    grad_branch = spread_rows((layer_mod[:, 2][:, None, :] * grad_middle).astype(jnp.bfloat16))
    grad_proj = jnp.einsum("bne,bnd->ed", attended, grad_branch, preferred_element_type=jnp.float32)
    grad_att = jnp.einsum(
        "bnd,ed->bne", grad_branch, w_proj, preferred_element_type=jnp.float32
    ).astype(jnp.bfloat16)
    grad_att = grad_att.reshape(queries.shape)
    scores = score_block(queries, key_heads)
    soft_float = jnp.exp(scores - logsum)
    softmax_w = soft_float.astype(jnp.bfloat16)
    grad_values = jnp.einsum(
        "bhnm,bnhe->bmhe", softmax_w, grad_att, preferred_element_type=jnp.float32
    ).astype(jnp.bfloat16)
    grad_soft = jnp.einsum("bnhe,bmhe->bhnm", grad_att, values, preferred_element_type=jnp.float32)
    row_delta = jnp.sum(soft_float * grad_soft, axis=-1, keepdims=True)
    grad_scores = (soft_float * (grad_soft - row_delta)).astype(jnp.bfloat16)
    grad_queries = (
        jnp.einsum("bhnm,bmhe->bnhe", grad_scores, key_heads, preferred_element_type=jnp.float32)
        * HDIM ** (-0.5)
    ).astype(jnp.bfloat16)
    grad_keys = (
        jnp.einsum("bhnm,bnhe->bmhe", grad_scores, queries, preferred_element_type=jnp.float32)
        * HDIM ** (-0.5)
    ).astype(jnp.bfloat16)
    grad_mixed = jnp.stack([grad_queries, grad_keys, grad_values], axis=2)
    grad_mixed = grad_mixed.reshape(grad_mixed.shape[0], grad_mixed.shape[1], 3, -1)
    grad_qkv = jnp.einsum("bnd,bnte->dte", gathered, grad_mixed, preferred_element_type=jnp.float32)
    grad_normed = fold_rows(
        jnp.einsum("bnte,dte->bnd", grad_mixed, w_qkv, preferred_element_type=jnp.float32)
    )
    _, norm_back_two = jax.vjp(modulated_norm, hidden, layer_mod[:, 0], layer_mod[:, 1])
    grad_hidden, grad_shift_a, grad_scale_a = norm_back_two(grad_normed)
    grad_hidden = grad_hidden + grad_middle
    grad_layer_mod = jnp.stack(
        [grad_shift_a, grad_scale_a, grad_gate_a, grad_shift_m, grad_scale_m, grad_gate_m], axis=1
    )
    return (grad_hidden, grad_layer_mod, (grad_qkv, grad_proj, grad_up, grad_down))


def local(
    latents,
    gaussian,
    velocity,
    time_ids,
    labels,
    small_w,
    small_m,
    small_v,
    cond_w,
    cond_m,
    cond_v,
    mod_w,
    mod_m,
    mod_v,
    qkv_w,
    qkv_m,
    qkv_v,
    proj_w,
    proj_m,
    proj_v,
    up_w,
    up_m,
    up_v,
    down_w,
    down_m,
    down_v,
):
    layer_count = qkv_w.shape[0]
    model_width = mod_w.shape[1] // (6 * layer_count + 2)
    dp_count = lax.axis_size("dp")
    tensor_count = lax.axis_size("tensor")
    samples = latents.shape[0]
    half_rows = latents.shape[2]
    shares = [1.0 / (dp_count * tensor_count), 1.0 / tensor_count, 1.0 / tensor_count] + [1.0] * (
        4 * layer_count
    )
    weights_list = (
        [small_w, cond_w, mod_w]
        + [qkv_w[i] for i in range(layer_count)]
        + [proj_w[i] for i in range(layer_count)]
        + [up_w[i] for i in range(layer_count)]
        + [down_w[i] for i in range(layer_count)]
    )
    firsts_list = (
        [small_m, cond_m, mod_m]
        + [qkv_m[i] for i in range(layer_count)]
        + [proj_m[i] for i in range(layer_count)]
        + [up_m[i] for i in range(layer_count)]
        + [down_m[i] for i in range(layer_count)]
    )
    seconds_list = (
        [small_v, cond_v, mod_v]
        + [qkv_v[i] for i in range(layer_count)]
        + [proj_v[i] for i in range(layer_count)]
        + [up_v[i] for i in range(layer_count)]
        + [down_v[i] for i in range(layer_count)]
    )

    def squares(arrays):
        return jnp.stack([jnp.sum(a * a) * f for a, f in zip(arrays, shares)])

    weight_sq = lax.psum(squares(weights_list), ("dp", "tensor"))
    cond_full, mod_full = (
        lax.all_gather(cond_w.astype(jnp.bfloat16), "dp", axis=1, tiled=True),
        lax.all_gather(mod_w.astype(jnp.bfloat16), "dp", axis=0, tiled=True),
    )
    small_low = small_w.astype(jnp.bfloat16)
    patch_rows = small_low[:PATCH]
    time_rows = small_low[PATCH : PATCH + FREQ]
    head_rows = small_low[PATCH + FREQ :]
    moment = (time_ids.astype(jnp.float32) + 0.5) / TSTEPS
    features = time_features(moment).astype(jnp.bfloat16)
    time_pre = jnp.dot(features, time_rows, preferred_element_type=jnp.float32)
    time_act = jax.nn.silu(time_pre).astype(jnp.bfloat16)
    time_emb = jnp.dot(time_act, cond_full[:model_width], preferred_element_type=jnp.float32)
    onehot = (labels[:, None] == jnp.arange(CLASSES)[None, :]).astype(jnp.bfloat16)
    cond = time_emb + jnp.dot(onehot, cond_full[model_width:], preferred_element_type=jnp.float32)
    cond_act = jax.nn.silu(cond).astype(jnp.bfloat16)
    modulation = jnp.dot(cond_act, mod_full, preferred_element_type=jnp.float32)
    blended = ((1.0 - moment)[:, None, None] * latents + moment[:, None, None] * gaussian).astype(
        jnp.bfloat16
    )
    token_index = lax.axis_index("tensor") * half_rows + jnp.arange(half_rows)
    hidden = (
        jnp.einsum("bpn,pd->bnd", blended, patch_rows, preferred_element_type=jnp.float32)
        + position_table(token_index, model_width)[None]
    )
    saved_list = []
    fetched = []
    for layer_id in range(layer_count):
        weights = fetch_layer(qkv_w, proj_w, up_w, down_w, layer_id)
        layer_mod = modulation[
            :, 6 * layer_id * model_width : (6 * layer_id + 6) * model_width
        ].reshape(samples, 6, model_width)
        hidden, saved_state = block_forward(hidden, layer_mod, weights)
        saved_list.append(saved_state)
        fetched.append(weights)
    final_mod = modulation[:, 6 * layer_count * model_width :].reshape(samples, 2, model_width)
    final_normed = modulated_norm(hidden, final_mod[:, 0], final_mod[:, 1]).astype(jnp.bfloat16)
    predicted = jnp.einsum(
        "bnd,pd->bpn", final_normed, head_rows, preferred_element_type=jnp.float32
    )
    time_weight = 0.5 + moment
    error = predicted - velocity
    loss_part = jnp.sum(time_weight[:, None, None] * error * error)
    total_count = samples * dp_count * half_rows * tensor_count * PATCH
    grad_pred = (time_weight[:, None, None] * (2.0 * error) / total_count).astype(jnp.bfloat16)
    grad_head = jnp.einsum(
        "bpn,bnd->pd", grad_pred, final_normed, preferred_element_type=jnp.float32
    )
    grad_final = jnp.einsum("bpn,pd->bnd", grad_pred, head_rows, preferred_element_type=jnp.float32)
    _, final_back = jax.vjp(modulated_norm, hidden, final_mod[:, 0], final_mod[:, 1])
    grad_hidden, grad_fshift, grad_fscale = final_back(grad_final)
    mod_grads = [None] * layer_count
    layer_grads = [None] * layer_count
    for layer_id in reversed(range(layer_count)):
        weights = fetch_layer(qkv_w, proj_w, up_w, down_w, layer_id)
        layer_mod = modulation[
            :, 6 * layer_id * model_width : (6 * layer_id + 6) * model_width
        ].reshape(samples, 6, model_width)
        grad_hidden, grad_layer_mod, grads = block_backward(
            grad_hidden, layer_mod, weights, saved_list[layer_id]
        )
        layer_grads[layer_id] = (
            lax.psum_scatter(grads[0], "dp", scatter_dimension=0, tiled=True),
            lax.psum_scatter(grads[1], "dp", scatter_dimension=1, tiled=True),
            lax.psum_scatter(grads[2], "dp", scatter_dimension=0, tiled=True),
            lax.psum_scatter(grads[3], "dp", scatter_dimension=1, tiled=True),
        )
        mod_grads[layer_id] = grad_layer_mod.reshape(samples, 6 * model_width)
    grad_patch = jnp.einsum(
        "bpn,bnd->pd", blended, grad_hidden.astype(jnp.bfloat16), preferred_element_type=jnp.float32
    )
    all_mods = jnp.concatenate(
        mod_grads
        + [jnp.stack([grad_fshift, grad_fscale], axis=1).reshape(samples, 2 * model_width)],
        axis=1,
    )
    grad_mods = lax.psum(all_mods.astype(jnp.bfloat16), "tensor")
    grad_cond_act = jnp.einsum("be,de->bd", grad_mods, mod_full, preferred_element_type=jnp.float32)
    _, silu_back = jax.vjp(jax.nn.silu, cond)
    grad_cond = silu_back(grad_cond_act)[0]
    grad_temb = grad_cond.astype(jnp.bfloat16)
    grad_time_act = jnp.einsum(
        "be,de->bd", grad_temb, cond_full[:model_width], preferred_element_type=jnp.float32
    )
    _, silu_back_two = jax.vjp(jax.nn.silu, time_pre)
    grad_pre = silu_back_two(grad_time_act)[0].astype(jnp.bfloat16)
    grad_time_one = jnp.einsum("bf,bd->fd", features, grad_pre, preferred_element_type=jnp.float32)
    grad_modw = jnp.einsum("bd,be->de", cond_act, grad_mods, preferred_element_type=jnp.float32)
    grad_table = jnp.einsum(
        "bc,bd->cd", onehot.astype(jnp.float32), grad_cond, precision=HIGHEST_PREC
    )
    grad_time_two = jnp.einsum("bd,be->de", time_act, grad_temb, preferred_element_type=jnp.float32)
    grad_cond_full = jnp.concatenate([grad_time_two, grad_table], axis=0)
    grad_cond_w, grad_mod_w = (
        lax.psum_scatter(grad_cond_full, "dp", scatter_dimension=1, tiled=True),
        lax.psum_scatter(grad_modw, "dp", scatter_dimension=0, tiled=True),
    )
    grad_small_local = jnp.concatenate(
        [grad_patch, grad_time_one / tensor_count, grad_head], axis=0
    )
    grad_small, loss_sum = lax.psum((grad_small_local, loss_part), ("dp", "tensor"))
    grads_list = (
        [grad_small, grad_cond_w, grad_mod_w]
        + [layer_grads[i][0] for i in range(layer_count)]
        + [layer_grads[i][1] for i in range(layer_count)]
        + [layer_grads[i][2] for i in range(layer_count)]
        + [layer_grads[i][3] for i in range(layer_count)]
    )
    results = [
        lamb_parts(weights_list[i], firsts_list[i], seconds_list[i], grads_list[i])
        for i in range(len(weights_list))
    ]
    updates = [r[2] for r in results]
    update_sq = lax.psum(squares(updates), ("dp", "tensor"))
    weight_norm = jnp.sqrt(weight_sq + EPS_NORM)
    update_norm = jnp.sqrt(update_sq + EPS_NORM)
    renewed = [
        weights_list[i] - LEARN_RATE * (weight_norm[i] / update_norm[i]) * updates[i]
        for i in range(len(weights_list))
    ]
    firsts_new = [r[0] for r in results]
    seconds_new = [r[1] for r in results]
    span_list = [[0], [1], [2]] + [
        [3 + kind_id * layer_count + l for l in range(layer_count)] for kind_id in range(4)
    ]
    outputs = []
    for kind_id, span_ids in enumerate(span_list):
        for source in (renewed, firsts_new, seconds_new):
            picked = [source[i] for i in span_ids]
            outputs.append(picked[0] if kind_id < 3 else jnp.stack(picked))
    norms = jnp.stack([weight_norm, update_norm])
    return tuple(outputs) + (loss_sum, norms)


def solution(mesh):
    return jax.shard_map(
        local,
        mesh=mesh,
        in_specs=(
            P("dp", None, "tensor"),
            P("dp", None, "tensor"),
            P("dp", None, "tensor"),
            P("dp"),
            P("dp"),
            P(),
            P(),
            P(),
            P(None, "dp"),
            P(None, "dp"),
            P(None, "dp"),
            P("dp", None),
            P("dp", None),
            P("dp", None),
            P(None, "dp", None, "tensor"),
            P(None, "dp", None, "tensor"),
            P(None, "dp", None, "tensor"),
            P(None, "tensor", "dp"),
            P(None, "tensor", "dp"),
            P(None, "tensor", "dp"),
            P(None, "dp", "tensor"),
            P(None, "dp", "tensor"),
            P(None, "dp", "tensor"),
            P(None, "tensor", "dp"),
            P(None, "tensor", "dp"),
            P(None, "tensor", "dp"),
        ),
        out_specs=(
            P(),
            P(),
            P(),
            P(None, "dp"),
            P(None, "dp"),
            P(None, "dp"),
            P("dp", None),
            P("dp", None),
            P("dp", None),
            P(None, "dp", None, "tensor"),
            P(None, "dp", None, "tensor"),
            P(None, "dp", None, "tensor"),
            P(None, "tensor", "dp"),
            P(None, "tensor", "dp"),
            P(None, "tensor", "dp"),
            P(None, "dp", "tensor"),
            P(None, "dp", "tensor"),
            P(None, "dp", "tensor"),
            P(None, "tensor", "dp"),
            P(None, "tensor", "dp"),
            P(None, "tensor", "dp"),
            P(),
            P(),
        ),
        check_vma=False,
    )
```

profile of v0, /device:TPU:1, one launch (start us, length us, event | category | flops | bytes accessed | tf_op | source)
XLA Modules:
  0.0 2839.6 jit_solution(17756244202729900690)
XLA Ops:
  14.5 41.8 %all_gather.66 = bf16[384,768]{0,1:T(8,128)(2,1)} all-gather(bf16[384,48]{0,1:T(8,128)(2,1)S(1)} %get-tuple-element.230), channel_id=1, replica_groups=mesh['dp'=16,'tensor'=2] {'dp'}, dimensions={1}, use_global_device_ids=true | all-gather | bytes 626688 | tf_op jit(solution)/shard_map/all_gather | solution.py:82
  57.0 23.3 all-gather.9.cloned.1.call-done
  84.0 188.6 %all-gather.11.cloned.1.call-done = bf16[768,10752]{1,0:T(8,128)(2,1)} async-done(((bf16[48,10752]{1,0:T(8,128)(2,1)}), bf16[768,10752]{1,0:T(8,128)(2,1)}) %all-gather.11.cloned.1.call-update) | async-done | bytes 16515088 | tf_op jit(solution)/shard_map/all_gather | solution.py:280
  284.0 48.2 %all-gather.13.cloned.1.call-done = bf16[768,3,384]{2,0,1:T(8,128)(2,1)} async-done(((bf16[48,3,384]{2,0,1:T(8,128)(2,1)}), bf16[768,3,384]{2,0,1:T(8,128)(2,1)}) %all-gather.13.cloned.1.call-update) | async-done | bytes 1769488 | tf_op jit(solution)/shard_map/all_gather | solution.py:81
  356.4 61.1 %all-gather.15.cloned.1.call-done = bf16[768,1536]{1,0:T(8,128)(2,1)} async-done(((bf16[48,1536]{1,0:T(8,128)(2,1)}), bf16[768,1536]{1,0:T(8,128)(2,1)}) %all-gather.15.cloned.1.call-update) | async-done | bytes 2359312 | tf_op jit(solution)/shard_map/all_gather | solution.py:83
  422.5 59.8 %all-gather.17.cloned.1.call-done = bf16[1536,768]{0,1:T(8,128)(2,1)} async-done(((bf16[1536,48]{0,1:T(8,128)(2,1)}), bf16[1536,768]{0,1:T(8,128)(2,1)}) %all-gather.17.cloned.1.call-update) | async-done | bytes 2359312 | tf_op jit(solution)/shard_map/all_gather | solution.py:84
  488.6 39.2 %all_gather.72 = bf16[384,768]{0,1:T(8,128)(2,1)} all-gather(bf16[384,48]{0,1:T(8,128)(2,1)S(1)} %get-tuple-element.229), channel_id=1, replica_groups=mesh['dp'=16,'tensor'=2] {'dp'}, dimensions={1}, use_global_device_ids=true | all-gather | bytes 626688 | tf_op jit(solution)/shard_map/all_gather | solution.py:82
  539.8 18.7 all-gather.19.cloned.1.call-done
  585.2 61.1 %all-gather.21.cloned.1.call-done = bf16[768,1536]{1,0:T(8,128)(2,1)} async-done(((bf16[48,1536]{1,0:T(8,128)(2,1)}), bf16[768,1536]{1,0:T(8,128)(2,1)}) %all-gather.21.cloned.1.call-update) | async-done | bytes 2359312 | tf_op jit(solution)/shard_map/all_gather | solution.py:83
  651.4 59.8 %all-gather.23.cloned.1.call-done = bf16[1536,768]{0,1:T(8,128)(2,1)} async-done(((bf16[1536,48]{0,1:T(8,128)(2,1)}), bf16[1536,768]{0,1:T(8,128)(2,1)}) %all-gather.23.cloned.1.call-update) | async-done | bytes 2359312 | tf_op jit(solution)/shard_map/all_gather | solution.py:84
  862.0 10.0 fusion.247
  922.6 13.2 fusion.214
  935.9 68.7 %all-reduce.3.cloned.1.call-done = f32[288,768]{1,0:T(8,128)} async-done(((f32[288,768]{1,0:T(8,128)}), f32[288,768]{1,0:T(8,128)}) %all-reduce.3.cloned.1.call-update) | async-done | bytes 884752 | tf_op jit(solution)/shard_map/psum | solution.py:378
  1009.8 121.7 %reduce-scatter.45.cloned.1.call-done = f32[384,48]{0,1:T(8,128)} async-done(((f32[384,768]{0,1:T(8,128)}), f32[384,48]{0,1:T(8,128)}) %reduce-scatter.45.cloned.1.call-update) | async-done | bytes 73744 | tf_op jit(solution)/shard_map/reduce_scatter | solution.py:341
  1131.5 128.1 %reduce-scatter.43.cloned.1.call-done = f32[384,48]{0,1:T(8,128)} async-done(((f32[384,768]{0,1:T(8,128)}), f32[384,48]{0,1:T(8,128)}) %reduce-scatter.43.cloned.1.call-update) | async-done | bytes 73744 | tf_op jit(solution)/shard_map/reduce_scatter | solution.py:341
  1263.5 134.3 %reduce-scatter.41.cloned.1.call-done = f32[48,3,384]{2,0,1:T(8,128)} async-done(((f32[768,3,384]{2,0,1:T(8,128)}), f32[48,3,384]{2,0,1:T(8,128)}) %reduce-scatter.41.cloned.1.call-update) | async-done | bytes 221200 | tf_op jit(solution)/shard_map/reduce_scatter | solution.py:340
  1397.8 138.5 %reduce-scatter.39.cloned.1.call-done = f32[48,3,384]{2,0,1:T(8,128)} async-done(((f32[768,3,384]{2,0,1:T(8,128)}), f32[48,3,384]{2,0,1:T(8,128)}) %reduce-scatter.39.cloned.1.call-update) | async-done | bytes 221200 | tf_op jit(solution)/shard_map/reduce_scatter | solution.py:340
  1541.0 136.9 %reduce-scatter.53.cloned.1.call-done = f32[1536,48]{0,1:T(8,128)} async-done(((f32[1536,768]{0,1:T(8,128)}), f32[1536,48]{0,1:T(8,128)}) %reduce-scatter.53.cloned.1.call-update) | async-done | bytes 294928 | tf_op jit(solution)/shard_map/reduce_scatter | solution.py:343
  1677.9 142.6 %reduce-scatter.51.cloned.1.call-done = f32[1536,48]{0,1:T(8,128)} async-done(((f32[1536,768]{0,1:T(8,128)}), f32[1536,48]{0,1:T(8,128)}) %reduce-scatter.51.cloned.1.call-update) | async-done | bytes 294928 | tf_op jit(solution)/shard_map/reduce_scatter | solution.py:343
  1825.6 136.7 %reduce-scatter.49.cloned.1.call-done = f32[48,1536]{1,0:T(8,128)} async-done(((f32[768,1536]{1,0:T(8,128)}), f32[48,1536]{1,0:T(8,128)}) %reduce-scatter.49.cloned.1.call-update) | async-done | bytes 294928 | tf_op jit(solution)/shard_map/reduce_scatter | solution.py:342
  1962.2 142.6 %reduce-scatter.47.cloned.1.call-done = f32[48,1536]{1,0:T(8,128)} async-done(((f32[768,1536]{1,0:T(8,128)}), f32[48,1536]{1,0:T(8,128)}) %reduce-scatter.47.cloned.1.call-update) | async-done | bytes 294928 | tf_op jit(solution)/shard_map/reduce_scatter | solution.py:342
  2109.9 140.3 %reduce-scatter.55.cloned.1.call-done = f32[48,1769]{1,0:T(8,128)} async-done(((f32[768,1769]{1,0:T(8,128)}), f32[48,1769]{1,0:T(8,128)}) %reduce-scatter.55.cloned.1.call-update) | async-done | bytes 339664
  2254.5 492.6 %reduce-scatter.37.cloned.1.call-done = f32[48,10752]{1,0:T(8,128)} async-done(((f32[768,10752]{1,0:T(8,128)}), f32[48,10752]{1,0:T(8,128)}) %reduce-scatter.37.cloned.1.call-update) | async-done | bytes 2064400 | tf_op jit(solution)/shard_map/reduce_scatter | solution.py:373
  2765.6 40.0 %all-reduce = (f32[11]{0:T(128)S(1)}, f32[11]{0:T(128)S(1)}, f32[]{:T(128)}) all-reduce(f32[11]{0:T(128)S(1)} %stack.272, f32[11]{0:T(128)S(1)} %stack.299, f32[]{:T(128)} %get-tuple-element.297), channel_id=1, replica_groups=mesh['dp'=16,'tensor'=2] {'dp','tensor'}, use_global_device_ids=true, to_apply=%region_11.0 | all-reduce | flops 23 | bytes 184 | tf_op jit(solution)/shard_map/psum | solution.py:277
  (562 shorter events, 356.9 us)
Async XLA Ops:
  7.2 73.1 %all-gather.9.cloned.1.call-start = ((), (), s32[]{:S(2)}) async-start(), calls=%async_computation.18 | async-start | bytes 2924544 | tf_op jit(solution)/shard_map/all_gather | solution.py:279
  9.1 263.5 %all-gather.11.cloned.1.call-start = ((), (), s32[]{:S(2)}) async-start(), calls=%async_computation.19 | async-start | bytes 17547264 | tf_op jit(solution)/shard_map/all_gather | solution.py:280
  11.8 320.4 %all-gather.13.cloned.1.call-start = ((), (), s32[]{:S(2)}) async-start(), calls=%async_computation.20 | async-start | bytes 1880064 | tf_op jit(solution)/shard_map/all_gather | solution.py:81
  12.6 338.8 %reduce-scatter.21.cloned.1.call-start = ((), (), s32[]{:S(2)}) async-start(), calls=%async_computation.21 | async-start | bytes 1179648 | tf_op jit(solution)/shard_map/reduce_scatter | solution.py:74
  342.6 74.9 %all-gather.15.cloned.1.call-start = ((), (), s32[]{:S(2)}) async-start(), calls=%async_computation.22 | async-start | bytes 2506752 | tf_op jit(solution)/shard_map/all_gather | solution.py:83
  344.5 137.8 %all-gather.17.cloned.1.call-start = ((), (), s32[]{:S(2)}) async-start(), calls=%async_computation.23 | async-start | bytes 2506752 | tf_op jit(solution)/shard_map/all_gather | solution.py:84
  346.3 181.6 %reduce-scatter.23.cloned.1.call-start = ((), (), s32[]{:S(2)}) async-start(), calls=%async_computation.24 | async-start | bytes 1179648 | tf_op jit(solution)/shard_map/reduce_scatter | solution.py:74
  487.8 70.7 %all-gather.19.cloned.1.call-start = ((), (), s32[]{:S(2)}) async-start(), calls=%async_computation.25 | async-start | bytes 1880064 | tf_op jit(solution)/shard_map/all_gather | solution.py:81
  488.5 91.7 %reduce-scatter.25.cloned.1.call-start = ((), (), s32[]{:S(2)}) async-start(), calls=%async_computation.26 | async-start | bytes 1179648 | tf_op jit(solution)/shard_map/reduce_scatter | solution.py:74
  571.4 74.9 %all-gather.21.cloned.1.call-start = ((), (), s32[]{:S(2)}) async-start(), calls=%async_computation.27 | async-start | bytes 2506752 | tf_op jit(solution)/shard_map/all_gather | solution.py:83
  572.0 139.2 %all-gather.23.cloned.1.call-start = ((), (), s32[]{:S(2)}) async-start(), calls=%async_computation.28 | async-start | bytes 2506752 | tf_op jit(solution)/shard_map/all_gather | solution.py:84
  572.8 152.1 %reduce-scatter.27.cloned.1.call-start = ((), (), s32[]{:S(2)}) async-start(), calls=%async_computation.29 | async-start | bytes 1179648 | tf_op jit(solution)/shard_map/reduce_scatter | solution.py:74
  740.6 50.0 %reduce-scatter.31.cloned.1.call-start = ((), (), s32[]{:S(2)}) async-start(), calls=%async_computation.31 | async-start | bytes 1179648 | tf_op jit(solution)/shard_map/reduce_scatter | solution.py:74
  840.9 163.6 %all-reduce.3.cloned.1.call-start = ((), (), s32[]{:S(2)}) async-start(), calls=%async_computation.34 | async-start | bytes 1769472 | tf_op jit(solution)/shard_map/psum | solution.py:378
  875.1 256.5 %reduce-scatter.45.cloned.1.call-start = ((), (), s32[]{:S(2)}) async-start(), calls=%async_computation.39 | async-start | bytes 1253376 | tf_op jit(solution)/shard_map/reduce_scatter | solution.py:341
  876.8 382.9 %reduce-scatter.43.cloned.1.call-start = ((), (), s32[]{:S(2)}) async-start(), calls=%async_computation.38 | async-start | bytes 1253376 | tf_op jit(solution)/shard_map/reduce_scatter | solution.py:341
  878.6 519.2 %reduce-scatter.41.cloned.1.call-start = ((), (), s32[]{:S(2)}) async-start(), calls=%async_computation.37 | async-start | bytes 3760128 | tf_op jit(solution)/shard_map/reduce_scatter | solution.py:340
  881.7 654.6 %reduce-scatter.39.cloned.1.call-start = ((), (), s32[]{:S(2)}) async-start(), calls=%async_computation.36 | async-start | bytes 3760128 | tf_op jit(solution)/shard_map/reduce_scatter | solution.py:340
  886.3 791.6 %reduce-scatter.53.cloned.1.call-start = ((), (), s32[]{:S(2)}) async-start(), calls=%async_computation.43 | async-start | bytes 5013504 | tf_op jit(solution)/shard_map/reduce_scatter | solution.py:343
  893.1 927.4 %reduce-scatter.51.cloned.1.call-start = ((), (), s32[]{:S(2)}) async-start(), calls=%async_computation.42 | async-start | bytes 5013504 | tf_op jit(solution)/shard_map/reduce_scatter | solution.py:343
  899.9 1062.4 %reduce-scatter.49.cloned.1.call-start = ((), (), s32[]{:S(2)}) async-start(), calls=%async_computation.41 | async-start | bytes 5013504 | tf_op jit(solution)/shard_map/reduce_scatter | solution.py:342
  905.1 1199.7 %reduce-scatter.47.cloned.1.call-start = ((), (), s32[]{:S(2)}) async-start(), calls=%async_computation.40 | async-start | bytes 5013504 | tf_op jit(solution)/shard_map/reduce_scatter | solution.py:342
  910.2 1340.0 %reduce-scatter.55.cloned.1.call-start = ((), (), s32[]{:S(2)}) async-start(), calls=%async_computation.44 | async-start | bytes 5849088
  921.9 1825.2 %reduce-scatter.37.cloned.1.call-start = ((), (), s32[]{:S(2)}) async-start(), calls=%async_computation.35 | async-start | bytes 35094528 | tf_op jit(solution)/shard_map/reduce_scatter | solution.py:373
  (147 other events, 7956.4 us)
Sparse Core Ops, SparseCore 0:
  11.4 68.8 all-gather.8
  83.7 188.8 all-gather.10
  275.9 56.3 all-gather.12
  342.7 8.5 reduce-scatter.20
  355.0 62.5 all-gather.14
  421.1 61.0 all-gather.16
  499.2 59.2 all-gather.18
  583.8 62.5 all-gather.20
  650.1 61.0 all-gather.22
  740.8 9.4 reduce-scatter.28
  781.2 9.3 reduce-scatter.30
  807.8 9.4 reduce-scatter.32
  841.0 9.3 reduce-scatter.34
  875.2 129.3 all-reduce.2
  1009.7 121.7 reduce-scatter.44
  1136.3 123.3 reduce-scatter.42
  1264.6 133.1 reduce-scatter.40
  1402.9 133.3 reduce-scatter.38
  1541.5 136.4 reduce-scatter.52
  1683.9 136.5 reduce-scatter.50
  1825.5 136.6 reduce-scatter.48
  1968.2 136.5 reduce-scatter.46
  2109.9 140.2 reduce-scatter.54
  2256.1 490.9 reduce-scatter.36
  (3 shorter events, 24.4 us)
where the time goes:
time: 2850 us; the launch traced here: 2840 us
  waiting for transfers between devices  2360 us (83%)
  blocking collectives  152 us (5%)
  matrix products  143 us (5%)
  other arithmetic  92 us (3%)
  local copies, waits for them, and re-layouts  58.6 us (2%)
  between operations  34.7 us (1%)
    reduce_scatter x1, waiting for transfers between devices, local(): lax.psum_scatter(grad_modw, 'dp', scatter_dimension=0, tiled=True)  493 us
    reduce_scatter x2, waiting for transfers between devices, local(): lax.psum_scatter(grads[3], 'dp', scatter_dimension=1, tiled=True)  279 us
    reduce_scatter x2, waiting for transfers between devices, local(): lax.psum_scatter(grads[2], 'dp', scatter_dimension=0, tiled=True)  279 us
    reduce_scatter x2, waiting for transfers between devices, local(): lax.psum_scatter(grads[0], 'dp', scatter_dimension=0, tiled=True)  273 us
    reduce_scatter x2, waiting for transfers between devices, local(): lax.psum_scatter(grads[1], 'dp', scatter_dimension=1, tiled=True)  250 us
    all_gather x1, waiting for transfers between devices, local(): lax.all_gather(mod_w.astype(jnp.bfloat16), 'dp', axis=0, tiled=True)  189 us
    unnamed x28, waiting for transfers between devices  143 us
    all_gather x2, waiting for transfers between devices, fetch_layer(): lax.all_gather(up_w[layer_id].astype(jnp.bfloat16), 'dp', axis=0, tiled=T...  122 us
  transfers between devices with their start and end apart: 27, of which 26 were waited for; matrix products, arithmetic and copies ran while one was open for 4% of the time, Pallas kernels for 0%

commit v1 on v0

--- a/solution.py
+++ b/solution.py
@@ -3,6 +3,8 @@
 import jax
 import jax.numpy as jnp
 from jax import lax
+from jax.experimental import pallas as pl
+from jax.experimental.pallas import tpu as pltpu
 from jax.sharding import PartitionSpec as P
 
 HDIM = 64
@@ -74,15 +76,6 @@
     return lax.psum_scatter(
         term_rows.astype(jnp.bfloat16), "tensor", scatter_dimension=1, tiled=True
     ).astype(jnp.float32)
-
-
-def fetch_layer(qkv_w, proj_w, up_w, down_w, layer_id):
-    return (
-        lax.all_gather(qkv_w[layer_id].astype(jnp.bfloat16), "dp", axis=0, tiled=True),
-        lax.all_gather(proj_w[layer_id].astype(jnp.bfloat16), "dp", axis=1, tiled=True),
-        lax.all_gather(up_w[layer_id].astype(jnp.bfloat16), "dp", axis=0, tiled=True),
-        lax.all_gather(down_w[layer_id].astype(jnp.bfloat16), "dp", axis=1, tiled=True),
-    )
 
 
 def split_heads(gathered, w_qkv):
@@ -113,7 +106,7 @@
     ).astype(jnp.bfloat16)
     attended = attended.reshape(attended.shape[0], attended.shape[1], -1)
     branch = fold_rows(
-        jnp.einsum("bne,ed->bnd", attended, w_proj, preferred_element_type=jnp.float32)
+        jnp.einsum("bne,de->bnd", attended, w_proj, preferred_element_type=jnp.float32)
     )
     middle = hidden + layer_mod[:, 2][:, None, :] * branch
     normed_two = modulated_norm(middle, layer_mod[:, 3], layer_mod[:, 4]).astype(jnp.bfloat16)
@@ -121,7 +114,7 @@
     inner_pre = jnp.einsum("bnd,df->bnf", gathered_two, w_up, preferred_element_type=jnp.float32)
     activ = gelu_tanh(inner_pre).astype(jnp.bfloat16)
     outer_out = fold_rows(
-        jnp.einsum("bnf,fd->bnd", activ, w_down, preferred_element_type=jnp.float32)
+        jnp.einsum("bnf,df->bnd", activ, w_down, preferred_element_type=jnp.float32)
     )
     output = middle + layer_mod[:, 5][:, None, :] * outer_out
     saved_state = (
@@ -160,8 +153,8 @@
     grad_gate_m = jnp.sum(grad_out * outer_out, axis=1)
     grad_outer = spread_rows((layer_mod[:, 5][:, None, :] * grad_out).astype(jnp.bfloat16))
     activ = gelu_tanh(inner_pre).astype(jnp.bfloat16)
-    grad_down = jnp.einsum("bnf,bnd->fd", activ, grad_outer, preferred_element_type=jnp.float32)
-    grad_activ = jnp.einsum("bnd,fd->bnf", grad_outer, w_down, preferred_element_type=jnp.float32)
+    grad_down = jnp.einsum("bnd,bnf->df", grad_outer, activ, preferred_element_type=jnp.float32)
+    grad_activ = jnp.einsum("bnd,df->bnf", grad_outer, w_down, preferred_element_type=jnp.float32)
     _, gelu_back = jax.vjp(gelu_tanh, inner_pre)
     grad_inner = gelu_back(grad_activ)[0].astype(jnp.bfloat16)
     grad_up = jnp.einsum(
@@ -175,9 +168,9 @@
     grad_middle = grad_middle + grad_out
     grad_gate_a = jnp.sum(grad_middle * branch, axis=1)
     grad_branch = spread_rows((layer_mod[:, 2][:, None, :] * grad_middle).astype(jnp.bfloat16))
-    grad_proj = jnp.einsum("bne,bnd->ed", attended, grad_branch, preferred_element_type=jnp.float32)
+    grad_proj = jnp.einsum("bnd,bne->de", grad_branch, attended, preferred_element_type=jnp.float32)
     grad_att = jnp.einsum(
-        "bnd,ed->bne", grad_branch, w_proj, preferred_element_type=jnp.float32
+        "bnd,de->bne", grad_branch, w_proj, preferred_element_type=jnp.float32
     ).astype(jnp.bfloat16)
     grad_att = grad_att.reshape(queries.shape)
     scores = score_block(queries, key_heads)
@@ -210,6 +203,262 @@
         [grad_shift_a, grad_scale_a, grad_gate_a, grad_shift_m, grad_scale_m, grad_gate_m], axis=1
     )
     return (grad_hidden, grad_layer_mod, (grad_qkv, grad_proj, grad_up, grad_down))
+
+
+def grid_of(dp_count):
+    if dp_count == 16:
+        return (4, 2, 2)
+    sizes = [1, 1, 1]
+    rest, prime = dp_count, 2
+    while rest > 1:
+        while rest % prime == 0:
+            sizes[sizes.index(min(sizes))] *= prime
+            rest //= prime
+        prime += 1
+    return tuple(sorted(sizes, reverse=True))
+
+
+ORDERS = ((0, 1, 2), (0, 2, 1))
+
+
+def place(sizes):
+    index = lax.axis_index("dp")
+    return (index // (sizes[1] * sizes[2]), index // sizes[2] % sizes[1], index % sizes[2])
+
+
+def peer_of(sizes, spot, axis, other):
+    moved = [other if a == axis else spot[a] for a in range(3)]
+    return (moved[0] * sizes[1] + moved[1]) * sizes[2] + moved[2], lax.axis_index("tensor")
+
+
+def entry_barrier(sizes, spot):
+    barrier = pltpu.get_barrier_semaphore()
+    count = 0
+    for axis in range(3):
+        for offset in range(1, sizes[axis]):
+            other = (spot[axis] + offset) % sizes[axis]
+            pl.semaphore_signal(
+                barrier,
+                inc=1,
+                device_id=peer_of(sizes, spot, axis, other),
+                device_id_type=pl.DeviceIdType.MESH,
+            )
+            count += 1
+    pl.semaphore_wait(barrier, count)
+
+
+def gather_kernel(sizes, blob_ref, out_ref, send_sem, recv_sem, own_sem):
+    spot = place(sizes)
+    waves, columns = out_ref.shape[0], out_ref.shape[5]
+    half = columns // 2
+    own = pltpu.make_async_copy(blob_ref, out_ref.at[:, spot[0], spot[1], spot[2]], own_sem)
+    own.start()
+    entry_barrier(sizes, spot)
+
+    def copies(wave, order_id, phase):
+        order = ORDERS[order_id]
+        axis = order[phase]
+        pick = [spot[a] for a in range(3)]
+        for earlier in order[:phase]:
+            pick[earlier] = slice(None)
+        lanes = pl.ds(order_id * half, half)
+        target = out_ref.at[wave, pick[0], pick[1], pick[2], :, lanes]
+        source = blob_ref.at[wave, :, lanes] if phase == 0 else target
+        made = []
+        for offset in range(1, sizes[axis]):
+            other = (spot[axis] + offset) % sizes[axis]
+            made.append(
+                pltpu.make_async_remote_copy(
+                    src_ref=source,
+                    dst_ref=target,
+                    send_sem=send_sem.at[wave, order_id, phase, offset],
+                    recv_sem=recv_sem.at[wave, order_id, phase, offset],
+                    device_id=peer_of(sizes, spot, axis, other),
+                    device_id_type=pl.DeviceIdType.MESH,
+                )
+            )
+        return made
+
+    started = []
+    for step in range(waves + 3):
+        for phase in reversed(range(4)):
+            wave = step - phase
+            if not 0 <= wave < waves:
+                continue
+            for order_id in range(2):
+                if phase > 0:
+                    for copy in copies(wave, order_id, phase - 1):
+                        copy.wait_recv()
+                if wave == 0 and phase == 1 and order_id == 0:
+                    own.wait()
+                if phase < 3:
+                    for copy in copies(wave, order_id, phase):
+                        copy.start()
+                        started.append(copy)
+    for copy in started:
+        copy.wait_send()
+
+
+def gather_weights(blob, dp_count):
+    sizes = grid_of(dp_count)
+    waves, rows, columns = blob.shape
+    most = max(sizes)
+    out = pl.pallas_call(
+        lambda *refs: gather_kernel(sizes, *refs),
+        out_shape=jax.ShapeDtypeStruct((waves,) + sizes + (rows, columns), blob.dtype),
+        in_specs=[pl.BlockSpec(memory_space=pl.ANY)],
+        out_specs=pl.BlockSpec(memory_space=pl.ANY),
+        scratch_shapes=[
+            pltpu.SemaphoreType.DMA((waves, 2, 3, most)),
+            pltpu.SemaphoreType.DMA((waves, 2, 3, most)),
+            pltpu.SemaphoreType.DMA,
+        ],
+        compiler_params=pltpu.CompilerParams(collective_id=0, has_side_effects=True),
+    )(blob)
+    return out.reshape(waves, dp_count * rows, columns)
+
+
+def reduce_grads_kernel(sizes, waves, *refs):
+    grads = refs[:waves]
+    out_ref = refs[waves]
+    held, got_one, got_two, got_three, send_sem, recv_sem, load_sem = refs[waves + 1 :]
+    spot = place(sizes)
+    half = out_ref.shape[2] // 2
+    loads = []
+    for wave in range(waves):
+        load = pltpu.make_async_copy(grads[wave], held.at[wave], load_sem.at[wave])
+        load.start()
+        loads.append(load)
+    entry_barrier(sizes, spot)
+    inbox = (got_one, got_two, got_three)
+
+    def copies(wave, order_id, phase):
+        order = ORDERS[order_id][::-1]
+        axis = order[phase]
+        lanes = pl.ds(order_id * half, half)
+        made = []
+        for offset in range(1, sizes[axis]):
+            other = (spot[axis] + offset) % sizes[axis]
+            pick = [slice(None)] * 3
+            for earlier in order[:phase]:
+                pick[earlier] = spot[earlier]
+            pick[axis] = other
+            source = held.at[wave, pick[0], pick[1], pick[2], :, lanes]
+            target = inbox[phase].at[wave, order_id, offset - 1]
+            made.append(
+                pltpu.make_async_remote_copy(
+                    src_ref=source,
+                    dst_ref=target,
+                    send_sem=send_sem.at[wave, order_id, phase, offset],
+                    recv_sem=recv_sem.at[wave, order_id, phase, offset],
+                    device_id=peer_of(sizes, spot, axis, other),
+                    device_id_type=pl.DeviceIdType.MESH,
+                )
+            )
+        return made
+
+    def absorb(wave, order_id, phase):
+        order = ORDERS[order_id][::-1]
+        lanes = pl.ds(order_id * half, half)
+        box = inbox[phase]
+        peers = sizes[order[phase]] - 1
+        if phase == 2:
+            total = held[wave, spot[0], spot[1], spot[2], :, lanes].astype(jnp.float32)
+            for p in range(peers):
+                total = total + box[wave, order_id, p].astype(jnp.float32)
+            out_ref[wave, :, lanes] = total
+            return
+        left = order[phase + 1 :]
+        if phase == 0:
+            first, second = left
+            first, second = max(first, second), min(first, second)
+
+            def body(step, carry):
+                low, high = step % sizes[first], step // sizes[first]
+                pick = [spot[0], spot[1], spot[2]]
+                pick[first], pick[second] = low, high
+                total = held[wave, pick[0], pick[1], pick[2], :, lanes].astype(jnp.float32)
+                for p in range(peers):
+                    total = total + box[wave, order_id, p, high, low].astype(jnp.float32)
+                held[wave, pick[0], pick[1], pick[2], :, lanes] = total.astype(held.dtype)
+                return carry
+
+            lax.fori_loop(0, sizes[first] * sizes[second], body, 0)
+        else:
+            (only,) = left
+
+            def body_one(step, carry):
+                pick = [spot[0], spot[1], spot[2]]
+                pick[only] = step
+                total = held[wave, pick[0], pick[1], pick[2], :, lanes].astype(jnp.float32)
+                for p in range(peers):
+                    total = total + box[wave, order_id, p, step].astype(jnp.float32)
+                held[wave, pick[0], pick[1], pick[2], :, lanes] = total.astype(held.dtype)
+                return carry
+
+            lax.fori_loop(0, sizes[only], body_one, 0)
+
+    started = []
+    for step in range(waves + 3):
+        for phase in reversed(range(4)):
+            wave = step - phase
+            if not 0 <= wave < waves:
+                continue
+            if phase == 0:
+                loads[wave].wait()
+            for order_id in range(2):
+                if phase > 0:
+                    for copy in copies(wave, order_id, phase - 1):
+                        copy.wait_recv()
+                    absorb(wave, order_id, phase - 1)
+                if phase < 3:
+                    for copy in copies(wave, order_id, phase):
+                        copy.start()
+                        started.append(copy)
+    for copy in started:
+        copy.wait_send()
+
+
+def reduce_grads(grads, dp_count):
+    sizes = grid_of(dp_count)
+    waves = len(grads)
+    rows, columns = grads[0].shape[0] // dp_count, grads[0].shape[1]
+    half = columns // 2
+    most = max(sizes)
+    grads = [g.reshape(sizes + (rows, columns)) for g in grads]
+    low = jnp.bfloat16
+    return pl.pallas_call(
+        lambda *refs: reduce_grads_kernel(sizes, waves, *refs),
+        out_shape=jax.ShapeDtypeStruct((waves, rows, columns), jnp.float32),
+        in_specs=[pl.BlockSpec(memory_space=pl.ANY)] * waves,
+        out_specs=pl.BlockSpec(memory_space=pltpu.VMEM),
+        scratch_shapes=[
+            pltpu.VMEM((waves,) + sizes + (rows, columns), low),
+            pltpu.VMEM((waves, 2, sizes[2] - 1, sizes[0], sizes[1], rows, half), low),
+            pltpu.VMEM((waves, 2, sizes[1] - 1, sizes[0], rows, half), low),
+            pltpu.VMEM((waves, 2, sizes[0] - 1, rows, half), low),
+            pltpu.SemaphoreType.DMA((waves, 2, 3, most)),
+            pltpu.SemaphoreType.DMA((waves, 2, 3, most)),
+            pltpu.SemaphoreType.DMA((waves,)),
+        ],
+        compiler_params=pltpu.CompilerParams(
+            collective_id=1, has_side_effects=True, vmem_limit_bytes=60 * 2**20
+        ),
+    )(*grads)
+
+
+def gather_plain(blob, dp_count):
+    waves, rows, columns = blob.shape
+    return lax.all_gather(blob, "dp", axis=1, tiled=True)
+
+
+def reduce_plain(grads, dp_count):
+    return jnp.stack(
+        [
+            lax.psum_scatter(g.astype(jnp.float32), "dp", scatter_dimension=0, tiled=True)
+            for g in grads
+        ]
+    )
 
 
 def local(
@@ -246,52 +495,49 @@
     tensor_count = lax.axis_size("tensor")
     samples = latents.shape[0]
     half_rows = latents.shape[2]
-    shares = [1.0 / (dp_count * tensor_count), 1.0 / tensor_count, 1.0 / tensor_count] + [1.0] * (
-        4 * layer_count
-    )
-    weights_list = (
-        [small_w, cond_w, mod_w]
-        + [qkv_w[i] for i in range(layer_count)]
-        + [proj_w[i] for i in range(layer_count)]
-        + [up_w[i] for i in range(layer_count)]
-        + [down_w[i] for i in range(layer_count)]
-    )
-    firsts_list = (
-        [small_m, cond_m, mod_m]
-        + [qkv_m[i] for i in range(layer_count)]
-        + [proj_m[i] for i in range(layer_count)]
-        + [up_m[i] for i in range(layer_count)]
-        + [down_m[i] for i in range(layer_count)]
-    )
-    seconds_list = (
-        [small_v, cond_v, mod_v]
-        + [qkv_v[i] for i in range(layer_count)]
-        + [proj_v[i] for i in range(layer_count)]
-        + [up_v[i] for i in range(layer_count)]
-        + [down_v[i] for i in range(layer_count)]
-    )
-
-    def squares(arrays):
-        return jnp.stack([jnp.sum(a * a) * f for a, f in zip(arrays, shares)])
-
-    weight_sq = lax.psum(squares(weights_list), ("dp", "tensor"))
-    cond_full, mod_full = (
-        lax.all_gather(cond_w.astype(jnp.bfloat16), "dp", axis=1, tiled=True),
-        lax.all_gather(mod_w.astype(jnp.bfloat16), "dp", axis=0, tiled=True),
-    )
-    small_low = small_w.astype(jnp.bfloat16)
+    rows = qkv_w.shape[1]
+    kernels = rows % 16 == 0
+    my_dp = lax.axis_index("dp")
+    low = jnp.bfloat16
+
+    parts = []
+    for i in range(layer_count):
+        parts.append(
+            jnp.concatenate(
+                [qkv_w[i, :, 0], qkv_w[i, :, 1], qkv_w[i, :, 2], proj_w[i].T], axis=1
+            ).astype(low)
+        )
+        parts.append(up_w[i].astype(low))
+        parts.append(down_w[i].T.astype(low))
+    blob = jnp.stack(parts)
+    full = (gather_weights if kernels else gather_plain)(blob, dp_count)
+    heads_wide = qkv_w.shape[3]
+
+    ids = lax.all_gather(jnp.stack([time_ids, labels]), "dp", axis=1, tiled=True)
+    all_times, all_labels = ids[0], ids[1]
+    small_low = small_w.astype(low)
     patch_rows = small_low[:PATCH]
     time_rows = small_low[PATCH : PATCH + FREQ]
     head_rows = small_low[PATCH + FREQ :]
+    moment_all = (all_times.astype(jnp.float32) + 0.5) / TSTEPS
+    features = time_features(moment_all).astype(low)
+    time_pre = jnp.dot(features, time_rows, preferred_element_type=jnp.float32)
+    time_act = jax.nn.silu(time_pre).astype(low)
+    cond_low = cond_w.astype(low)
+    mod_low = mod_w.astype(low)
+    onehot = all_labels[:, None] == jnp.arange(CLASSES)[None, :]
+    cond = jnp.dot(
+        time_act, cond_low[:model_width], preferred_element_type=jnp.float32
+    ) + jnp.dot(onehot.astype(low), cond_low[model_width:], preferred_element_type=jnp.float32)
+    cond_act = jax.nn.silu(cond).astype(low)
+    modulation = lax.psum_scatter(
+        jnp.dot(cond_act, mod_low, preferred_element_type=jnp.float32),
+        "dp",
+        scatter_dimension=0,
+        tiled=True,
+    )
+
     moment = (time_ids.astype(jnp.float32) + 0.5) / TSTEPS
-    features = time_features(moment).astype(jnp.bfloat16)
-    time_pre = jnp.dot(features, time_rows, preferred_element_type=jnp.float32)
-    time_act = jax.nn.silu(time_pre).astype(jnp.bfloat16)
-    time_emb = jnp.dot(time_act, cond_full[:model_width], preferred_element_type=jnp.float32)
-    onehot = (labels[:, None] == jnp.arange(CLASSES)[None, :]).astype(jnp.bfloat16)
-    cond = time_emb + jnp.dot(onehot, cond_full[model_width:], preferred_element_type=jnp.float32)
-    cond_act = jax.nn.silu(cond).astype(jnp.bfloat16)
-    modulation = jnp.dot(cond_act, mod_full, preferred_element_type=jnp.float32)
     blended = ((1.0 - moment)[:, None, None] * latents + moment[:, None, None] * gaussian).astype(
         jnp.bfloat16
     )
@@ -303,7 +549,13 @@
     saved_list = []
     fetched = []
     for layer_id in range(layer_count):
-        weights = fetch_layer(qkv_w, proj_w, up_w, down_w, layer_id)
+        packed = full[3 * layer_id]
+        weights = (
+            packed[:, : 3 * heads_wide].reshape(model_width, 3, heads_wide),
+            packed[:, 3 * heads_wide :],
+            full[3 * layer_id + 1],
+            full[3 * layer_id + 2],
+        )
         layer_mod = modulation[
             :, 6 * layer_id * model_width : (6 * layer_id + 6) * model_width
         ].reshape(samples, 6, model_width)
@@ -327,22 +579,28 @@
     _, final_back = jax.vjp(modulated_norm, hidden, final_mod[:, 0], final_mod[:, 1])
     grad_hidden, grad_fshift, grad_fscale = final_back(grad_final)
     mod_grads = [None] * layer_count
-    layer_grads = [None] * layer_count
+    layer_grads = [None] * (3 * layer_count)
     for layer_id in reversed(range(layer_count)):
-        weights = fetch_layer(qkv_w, proj_w, up_w, down_w, layer_id)
         layer_mod = modulation[
             :, 6 * layer_id * model_width : (6 * layer_id + 6) * model_width
         ].reshape(samples, 6, model_width)
         grad_hidden, grad_layer_mod, grads = block_backward(
-            grad_hidden, layer_mod, weights, saved_list[layer_id]
+            grad_hidden, layer_mod, fetched[layer_id], saved_list[layer_id]
         )
-        layer_grads[layer_id] = (
-            lax.psum_scatter(grads[0], "dp", scatter_dimension=0, tiled=True),
-            lax.psum_scatter(grads[1], "dp", scatter_dimension=1, tiled=True),
-            lax.psum_scatter(grads[2], "dp", scatter_dimension=0, tiled=True),
-            lax.psum_scatter(grads[3], "dp", scatter_dimension=1, tiled=True),
+        layer_grads[3 * layer_id] = jnp.concatenate(
+            [grads[0].reshape(model_width, 3 * heads_wide).astype(low), grads[1].astype(low)],
+            axis=1,
         )
+        layer_grads[3 * layer_id + 1] = grads[2].astype(low)
+        layer_grads[3 * layer_id + 2] = grads[3].astype(low)
         mod_grads[layer_id] = grad_layer_mod.reshape(samples, 6 * model_width)
+    flow = list(reversed(range(3 * layer_count)))
+    if kernels:
+        summed = reduce_grads([layer_grads[i] for i in flow], dp_count)
+    else:
+        summed = reduce_plain([layer_grads[i] for i in flow], dp_count)
+    own_grads = [summed[flow.index(i)] for i in range(3 * layer_count)]
+
     grad_patch = jnp.einsum(
         "bpn,bnd->pd", blended, grad_hidden.astype(jnp.bfloat16), preferred_element_type=jnp.float32
     )
@@ -351,61 +609,82 @@
         + [jnp.stack([grad_fshift, grad_fscale], axis=1).reshape(samples, 2 * model_width)],
         axis=1,
     )
-    grad_mods = lax.psum(all_mods.astype(jnp.bfloat16), "tensor")
-    grad_cond_act = jnp.einsum("be,de->bd", grad_mods, mod_full, preferred_element_type=jnp.float32)
+    grad_mods = lax.all_gather(
+        lax.psum(all_mods.astype(low), "tensor"), "dp", axis=0, tiled=True
+    )
+    grad_cond_act = jnp.einsum("be,de->bd", grad_mods, mod_low, preferred_element_type=jnp.float32)
     _, silu_back = jax.vjp(jax.nn.silu, cond)
     grad_cond = silu_back(grad_cond_act)[0]
-    grad_temb = grad_cond.astype(jnp.bfloat16)
+    grad_temb = grad_cond.astype(low)
     grad_time_act = jnp.einsum(
-        "be,de->bd", grad_temb, cond_full[:model_width], preferred_element_type=jnp.float32
-    )
-    _, silu_back_two = jax.vjp(jax.nn.silu, time_pre)
-    grad_pre = silu_back_two(grad_time_act)[0].astype(jnp.bfloat16)
-    grad_time_one = jnp.einsum("bf,bd->fd", features, grad_pre, preferred_element_type=jnp.float32)
-    grad_modw = jnp.einsum("bd,be->de", cond_act, grad_mods, preferred_element_type=jnp.float32)
+        "be,de->bd", grad_temb, cond_low[:model_width], preferred_element_type=jnp.float32
+    )
+    grad_mod_w = jnp.einsum("bd,be->de", cond_act, grad_mods, preferred_element_type=jnp.float32)
     grad_table = jnp.einsum(
         "bc,bd->cd", onehot.astype(jnp.float32), grad_cond, precision=HIGHEST_PREC
     )
     grad_time_two = jnp.einsum("bd,be->de", time_act, grad_temb, preferred_element_type=jnp.float32)
-    grad_cond_full = jnp.concatenate([grad_time_two, grad_table], axis=0)
-    grad_cond_w, grad_mod_w = (
-        lax.psum_scatter(grad_cond_full, "dp", scatter_dimension=1, tiled=True),
-        lax.psum_scatter(grad_modw, "dp", scatter_dimension=0, tiled=True),
-    )
-    grad_small_local = jnp.concatenate(
-        [grad_patch, grad_time_one / tensor_count, grad_head], axis=0
-    )
-    grad_small, loss_sum = lax.psum((grad_small_local, loss_part), ("dp", "tensor"))
-    grads_list = (
-        [grad_small, grad_cond_w, grad_mod_w]
-        + [layer_grads[i][0] for i in range(layer_count)]
-        + [layer_grads[i][1] for i in range(layer_count)]
-        + [layer_grads[i][2] for i in range(layer_count)]
-        + [layer_grads[i][3] for i in range(layer_count)]
-    )
+    grad_cond_w = jnp.concatenate([grad_time_two, grad_table], axis=0)
+    ends, grad_time_act, loss_sum = lax.psum(
+        (
+            jnp.concatenate([grad_patch, grad_head], axis=0),
+            grad_time_act / tensor_count,
+            loss_part,
+        ),
+        ("dp", "tensor"),
+    )
+    _, silu_back_two = jax.vjp(jax.nn.silu, time_pre)
+    grad_pre = silu_back_two(grad_time_act)[0].astype(low)
+    grad_time_one = jnp.einsum("bf,bd->fd", features, grad_pre, preferred_element_type=jnp.float32)
+    grad_small = jnp.concatenate([ends[:PATCH], grad_time_one, ends[PATCH:]], axis=0)
+
+    def stacked(kind):
+        return jnp.stack([kind(i) for i in range(layer_count)])
+
+    grads_list = [
+        grad_small,
+        grad_cond_w,
+        grad_mod_w,
+        stacked(lambda i: own_grads[3 * i][:, : 3 * heads_wide].reshape(rows, 3, heads_wide)),
+        stacked(lambda i: own_grads[3 * i][:, 3 * heads_wide :].T),
+        stacked(lambda i: own_grads[3 * i + 1]),
+        stacked(lambda i: own_grads[3 * i + 2].T),
+    ]
+    weights_list = [small_w, cond_w, mod_w, qkv_w, proj_w, up_w, down_w]
+    firsts_list = [small_m, cond_m, mod_m, qkv_m, proj_m, up_m, down_m]
+    seconds_list = [small_v, cond_v, mod_v, qkv_v, proj_v, up_v, down_v]
+    shares = [1.0 / (dp_count * tensor_count), 1.0 / tensor_count, 1.0 / tensor_count]
+    shares = shares + [1.0] * 4
+
+    def squares(arrays):
+        sums = []
+        for kind_id, a in enumerate(arrays):
+            axes = None if kind_id < 3 else tuple(range(1, a.ndim))
+            sums.append(jnp.sum(a * a, axis=axes).reshape(-1) * shares[kind_id])
+        return jnp.concatenate(sums)
+
     results = [
         lamb_parts(weights_list[i], firsts_list[i], seconds_list[i], grads_list[i])
         for i in range(len(weights_list))
     ]
     updates = [r[2] for r in results]
-    update_sq = lax.psum(squares(updates), ("dp", "tensor"))
-    weight_norm = jnp.sqrt(weight_sq + EPS_NORM)
-    update_norm = jnp.sqrt(update_sq + EPS_NORM)
-    renewed = [
-        weights_list[i] - LEARN_RATE * (weight_norm[i] / update_norm[i]) * updates[i]
-        for i in range(len(weights_list))
-    ]
-    firsts_new = [r[0] for r in results]
-    seconds_new = [r[1] for r in results]
-    span_list = [[0], [1], [2]] + [
-        [3 + kind_id * layer_count + l for l in range(layer_count)] for kind_id in range(4)
-    ]
+    total_sq = lax.psum(
+        jnp.stack([squares(weights_list), squares(updates)]), ("dp", "tensor")
+    )
+    norms = jnp.sqrt(total_sq + EPS_NORM)
+    ratio = norms[0] / norms[1]
     outputs = []
-    for kind_id, span_ids in enumerate(span_list):
-        for source in (renewed, firsts_new, seconds_new):
-            picked = [source[i] for i in span_ids]
-            outputs.append(picked[0] if kind_id < 3 else jnp.stack(picked))
-    norms = jnp.stack([weight_norm, update_norm])
+    for kind_id in range(7):
+        if kind_id < 3:
+            factor = ratio[kind_id]
+        else:
+            first = 3 + (kind_id - 3) * layer_count
+            factor = ratio[first : first + layer_count].reshape(
+                (layer_count,) + (1,) * (weights_list[kind_id].ndim - 1)
+            )
+        outputs.append(weights_list[kind_id] - LEARN_RATE * factor * updates[kind_id])
+        outputs.append(results[kind_id][0])
+        outputs.append(results[kind_id][1])
     return tuple(outputs) + (loss_sum, norms)
 
 

time: 2850 us -> 878 us (0.31)
  waiting for transfers between devices: 2360 us -> 147 us
  Pallas kernels: 0 us -> 284 us
  matrix products: 143 us -> 107 us
    reduce_scatter x9 -> x0, waiting for transfers between devices: 1570 us -> none  [the longest x1 493 us: local(): lax.psum_scatter(grad_modw, 'dp', scatter_dimension=0, tiled=True)]
    all_gather x8 -> x0, waiting for transfers between devices: 521 us -> none  [the longest x1 189 us: local(): lax.all_gather(mod_w.astype(jnp.bfloat16), 'dp', axis=0, tiled=True)]
    pallas_call x0 -> x2, Pallas kernels: none -> 284 us  [the longest x1 151 us: gather_weights(): pl.pallas_call(lambda *refs: gather_kernel(sizes, *refs), out_shape=jax.S...]
    unnamed x28 -> x11, waiting for transfers between devices: 143 us -> 0.19 us
    psum x1, waiting for transfers between devices: 68.7 us -> 114 us  [local(): lax.psum((jnp.concatenate([grad_patch, grad_head], axis=0), grad_time_act...]
    dot_general x16 -> x17, matrix products: 58.8 us -> 38.1 us  [the longest x2 8.22 us: block_backward(): jnp.einsum('bnd,bnf->df', grad_outer, activ, preferred_element_type=jnp.f...]
  transfers between devices with their start and end apart: 27 -> 10, of which waited for: 26 -> 8; matrix products, arithmetic and copies ran while one was open for 4% -> 9% of each run, Pallas kernels for 0% -> 17%
where the time goes in v1:
time: 878 us; the launch traced here: 867 us
  Pallas kernels  284 us (32%)
  blocking collectives  153 us (17%)
  waiting for transfers between devices  147 us (17%)
  matrix products  107 us (12%)
  other arithmetic  80 us (9%)
  local copies, waits for them, and re-layouts  71.3 us (8%)
  between operations  23.5 us (3%)
    pallas_call x1, Pallas kernels, gather_weights(): pl.pallas_call(lambda *refs: gather_kernel(sizes, *refs), out_shape=jax.S...  151 us
    pallas_call x1, Pallas kernels, reduce_grads(): pl.pallas_call(lambda *refs: reduce_grads_kernel(sizes, waves, *refs), ou...  133 us
    psum x1, waiting for transfers between devices, local(): lax.psum((jnp.concatenate([grad_patch, grad_head], axis=0), grad_time_act...  114 us
    psum x1, blocking collectives, local(): lax.psum(jnp.stack([squares(weights_list), squares(updates)]), ('dp', 'te...  41.6 us
    all_gather x1, blocking collectives, local(): lax.all_gather(lax.psum(all_mods.astype(low), 'tensor'), 'dp', axis=0, ti...  36.8 us
    all_gather x1, blocking collectives, local(): lax.all_gather(jnp.stack([time_ids, labels]), 'dp', axis=1, tiled=True)  34.6 us
    reduce_scatter x8, waiting for transfers between devices, fold_rows(): lax.psum_scatter(term_rows.astype(jnp.bfloat16), 'tensor', scatter_dimens...  32.8 us
    all_gather x8, blocking collectives, spread_rows(): return lax.all_gather(part_rows, 'tensor', axis=1, tiled=True)  31.3 us
  transfers between devices with their start and end apart: 10, of which 8 were waited for; matrix products, arithmetic and copies ran while one was open for 9% of the time, Pallas kernels for 17%

profile of v1, /device:TPU:1, one launch (start us, length us, event | category | flops | bytes accessed | tf_op | source)
XLA Modules:
  0.0 867.2 jit_solution(282783725372381077)
XLA Ops:
  8.2 34.6 %all-gather = s32[16,2,2]{2,1,0:T(2,128)S(1)} all-gather(s32[1,2,2]{2,1,0:T(2,128)S(1)} %bitcast.448), channel_id=1, replica_groups=mesh['dp'=16,'tensor'=2] {'dp'}, dimensions={0}, use_global_device_ids=true | all-gather | bytes 272 | tf_op jit(solution)/shard_map/all_gather | solution.py:516
  50.8 151.5 %shard_map.425 = bf16[6,4,2,2,48,1536]{5,4,3,2,1,0:T(8,128)(2,1)} custom-call(bf16[6,48,1536]{2,1,0:T(8,128)(2,1)} %copy-done.75), custom_call_target="tpu_custom_call" | custom-call | tf_op jit(solution)/shard_map/pallas_call | solution.py:306
  202.3 9.7 %fusion.138 = (bf16[1,4,2,2,48,1536]{5,4,3,2,1,0:T(8,128)(2,1)}, bf16[1,4,2,2,48,1536]{5,4,3,2,1,0:T(8,128)(2,1)}, bf16[1,4,2,2,48,1536]{5,4,3,2,1,0:T(8,128)(2,...) fusion(bf16[6,4,2,2,48,1536]{5,4,3,2,1,0:T(8,128)(2,1)} %shard_, ...), kind=kLoop, calls=%fused_computation.393 | loop fusion | bytes 28311552 | tf_op jit(solution)/shard_map/slice | solution.py:556
  224.4 13.9 %all_gather.31 = bf16[2,256,768]{2,1,0:T(8,128)(2,1)S(1)} all-gather(bf16[2,128,768]{2,1,0:T(8,128)(2,1)S(1)} %add_convert_fusion.5), channel_id=1, replica_groups=mesh['dp'=16,'tensor'=2] {'tensor'}, dimensions={1}, use_global_device_ids=true | all-gather | bytes 1179648 | tf_op jit(solution)/shard_map/all_gather | solution.py:72
  251.3 5.5 reduce-scatter.9.cloned.1.call-done
  270.9 3.9 copy.264
  295.9 9.5 %reduce-scatter.13.cloned.1.call-done = bf16[2,128,768]{2,1,0:T(8,128)(2,1)} async-done(((bf16[2,256,768]{2,1,0:T(8,128)(2,1)}), bf16[2,128,768]{2,1,0:T(8,128)(2,1)}) %reduce-scatter.13.cloned.1.call-update) | async-done | bytes 393232 | tf_op jit(solution)/shard_map/reduce_scatter | solution.py:76
  317.4 8.6 reduce-scatter.15.cloned.1.call-done
  336.4 3.0 fusion.15
  345.1 4.5 bitcast_convert_fusion.2
  366.9 3.5 convolution_convert_fusion.10
  381.8 3.9 bitcast_convert_fusion.5
  387.2 5.2 bitcast_convert_fusion.3
  416.4 3.0 fusion.8
  423.2 4.6 bitcast_convert_fusion
  455.8 3.1 bitcast_convert_fusion.4
  463.0 132.6 %shard_map.426 = f32[6,48,1536]{2,1,0:T(8,128)} custom-call(bf16[4,2,2,48,1536]{4,3,2,1,0:T(8,128)(2,1)} %bitcast.418, bf16[4,2,2,48,1536]{4,3,2,1,0:T(8,128)(2,1)} %bitcast.417, bf16[4,2,2,48,1536]{4,3,2,1,0:T(8,128)(2,1)} %bitcast.399, bf16[4,2,2,48,1536]{4,3,2,1,0:T(8,128)(2,1)} %bitcast.420, bf16[4,2,2,48,1536]{4,3,2,1,0:T(8,128)(2,1)} %bitcast.419, ...), custom_call_target="tpu_custom_call" | custom-call | tf_op jit(solution)/shard_map/pallas_call | solution.py:430
  601.7 3.1 multiply_reduce_fusion.20
  615.4 8.6 psum.36
  624.0 36.8 %all-gather.1 = bf16[16,2,10752]{2,1,0:T(2,128)(2,1)} all-gather(bf16[1,2,10752]{2,1,0:T(2,128)(2,1)S(1)} %bitcast.433), channel_id=1, replica_groups=mesh['dp'=16,'tensor'=2] {'dp'}, dimensions={0}, use_global_device_ids=true | all-gather | bytes 731136 | tf_op jit(solution)/shard_map/all_gather | solution.py:612
  668.8 7.2 multiply_reduce_fusion.5
  680.4 114.3 %all-reduce.8.cloned.1.call-done = (f32[32,768]{1,0:T(8,128)}, f32[32,768]{1,0:T(8,128)}) async-done(((f32[32,768]{1,0:T(8,128)}, f32[32,768]{1,0:T(8,128)}), (f32[32,768]{1,0:T(8,128)}, f32[32,768]{1,0:T(8,128)})) %all-reduce.8.cloned.1.call-update) | async-done | bytes 196624 | tf_op jit(solution)/shard_map/psum | solution.py:628
  796.9 4.3 multiply_reduce_fusion.7
  802.8 41.6 %all-reduce.1 = (f32[2,11]{1,0:T(2,128)S(1)}, f32[]{:T(128)}) all-reduce(f32[2,11]{1,0:T(2,128)S(1)} %pad_maximum_fusion.18, f32[]{:T(128)} %get-tuple-element.221), channel_id=1, replica_groups=mesh['dp'=16,'tensor'=2] {'dp','tensor'}, use_global_device_ids=true, to_apply=%region_66.67 | all-reduce | flops 23 | bytes 184 | tf_op jit(solution)/shard_map/psum | solution.py:671
  (612 shorter events, 227.3 us)
Async XLA Ops:
  7.2 39.8 %copy-start.10 = (f32[48,10752]{1,0:T(8,128)S(1)}, f32[48,10752]{1,0:T(8,128)}, u32[]{:S(2)}) copy-start(f32[48,10752]{1,0:T(8,128)} %param.37) | copy-start | bytes 6193156
  7.2 214.6 %all-reduce.6.cloned.1.call-start = ((), (), s32[]{:S(2)}) async-start(), calls=%async_computation.16 | async-start | bytes 2752512
  48.4 208.4 %reduce-scatter.9.cloned.1.call-start = ((), (), s32[]{:S(2)}) async-start(), calls=%async_computation.8 | async-start | bytes 1179648 | tf_op jit(solution)/shard_map/reduce_scatter | solution.py:76
  214.6 23.7 %copy-start.60 = (bf16[768,1152]{0,1:T(8,128)(2,1)}, bf16[768,1152]{0,1:T(8,128)(2,1)S(1)}, u32[]{:S(2)}) copy-start(bf16[768,1152]{0,1:T(8,128)(2,1)S(1)} %copy.256) | copy-start | bytes 5308420
  221.5 19.9 %copy-start.2 = (f32[2,128,768]{2,1,0:T(8,128)}, f32[2,128,768]{2,1,0:T(8,128)S(1)}, u32[]{:S(2)}) copy-start(f32[2,128,768]{2,1,0:T(8,128)S(1)} %get-tuple-element.211) | copy-start | bytes 2359300
  221.5 19.9 %copy-start.120 = (f32[2,128]{1,0:T(2,128)}, f32[2,128]{1,0:T(2,128)S(1)}, u32[]{:S(2)}) copy-start(f32[2,128]{1,0:T(2,128)S(1)} %broadcast_multiply_fusion.4) | copy-start | bytes 3076
  221.7 19.7 %copy-start.137 = (f32[2,128]{1,0:T(2,128)}, f32[2,128]{1,0:T(2,128)S(1)}, u32[]{:S(2)}) copy-start(f32[2,128]{1,0:T(2,128)S(1)} %fusion.105) | copy-start | bytes 3076
  251.1 26.4 %reduce-scatter.11.cloned.1.call-start = ((), (), s32[]{:S(2)}) async-start(), calls=%async_computation.9 | async-start | bytes 1179648 | tf_op jit(solution)/shard_map/reduce_scatter | solution.py:76
  268.0 37.3 %reduce-scatter.13.cloned.1.call-start = ((), (), s32[]{:S(2)}) async-start(), calls=%async_computation.10 | async-start | bytes 1179648 | tf_op jit(solution)/shard_map/reduce_scatter | solution.py:76
  295.8 30.2 %reduce-scatter.15.cloned.1.call-start = ((), (), s32[]{:S(2)}) async-start(), calls=%async_computation.11 | async-start | bytes 1179648 | tf_op jit(solution)/shard_map/reduce_scatter | solution.py:76
  316.4 36.1 %reduce-scatter.17.cloned.1.call-start = ((), (), s32[]{:S(2)}) async-start(), calls=%async_computation.12 | async-start | bytes 1179648 | tf_op jit(solution)/shard_map/reduce_scatter | solution.py:76
  342.9 59.9 %reduce-scatter.19.cloned.1.call-start = ((), (), s32[]{:S(2)}) async-start(), calls=%async_computation.13 | async-start | bytes 1179648 | tf_op jit(solution)/shard_map/reduce_scatter | solution.py:76
  385.7 46.8 %reduce-scatter.21.cloned.1.call-start = ((), (), s32[]{:S(2)}) async-start(), calls=%async_computation.14 | async-start | bytes 1179648 | tf_op jit(solution)/shard_map/reduce_scatter | solution.py:76
  423.0 187.9 %reduce-scatter.23.cloned.1.call-start = ((), (), s32[]{:S(2)}) async-start(), calls=%async_computation.15 | async-start | bytes 1179648 | tf_op jit(solution)/shard_map/reduce_scatter | solution.py:76
  597.2 197.5 %all-reduce.8.cloned.1.call-start = ((), (), s32[]{:S(2)}) async-start(), calls=%async_computation.17 | async-start | bytes 393216 | tf_op jit(solution)/shard_map/psum | solution.py:628
  609.0 54.1 %copy-start.11 = (f32[48,10752]{1,0:T(8,128)S(1)}, f32[48,10752]{1,0:T(8,128)}, u32[]{:S(2)}) copy-start(f32[48,10752]{1,0:T(8,128)} %param.37) | copy-start | bytes 6193156
  609.0 54.1 %copy-start.113 = (f32[32,48]{1,0:T(8,128)S(1)}, f32[32,48]{1,0:T(8,128)}, u32[]{:S(2)}) copy-start(f32[32,48]{1,0:T(8,128)} %copy-done.112) | copy-start | bytes 18436
  624.0 42.4 %copy-start.92 = (f32[32,768]{1,0:T(8,128)S(1)}, f32[32,768]{1,0:T(8,128)}, u32[]{:S(2)}) copy-start(f32[32,768]{1,0:T(8,128)} %copy-done.91) | copy-start | bytes 294916
  668.8 126.7 %copy-start.107 = (bf16[32,128]{1,0:T(8,128)(2,1)S(1)}, bf16[32,128]{1,0:T(8,128)(2,1)}, u32[]{:S(2)}) copy-start(bf16[32,128]{1,0:T(8,128)(2,1)} %copy-done.106) | copy-start | bytes 24580
  668.8 126.7 %copy-start.109 = (bf16[32,128]{1,0:T(8,128)(2,1)S(1)}, bf16[32,128]{1,0:T(8,128)(2,1)}, u32[]{:S(2)}) copy-start(bf16[32,128]{1,0:T(8,128)(2,1)} %copy-done.108) | copy-start | bytes 24580
  796.8 50.2 %copy-start.74 = (f32[2,384,48]{1,2,0:T(8,128)S(1)}, f32[2,384,48]{1,2,0:T(8,128)}, u32[]{:S(2)}) copy-start(f32[2,384,48]{1,2,0:T(8,128)} %param.43) | copy-start | bytes 442372
  796.8 50.2 %copy-start.88 = (f32[2,384,48]{1,2,0:T(8,128)S(1)}, f32[2,384,48]{1,2,0:T(8,128)}, u32[]{:S(2)}) copy-start(f32[2,384,48]{1,2,0:T(8,128)} %get-tuple-element.125) | copy-start | bytes 442372
  796.8 54.0 %copy-start.35 = (f32[2,48,3,384]{3,1,2,0:T(8,128)S(1)}, f32[2,48,3,384]{3,1,2,0:T(8,128)}, u32[]{:S(2)}) copy-start(f32[2,48,3,384]{3,1,2,0:T(8,128)} %param.40) | copy-start | bytes 1327108
  801.2 52.0 %copy-start.29 = (f32[2,1536,48]{1,2,0:T(8,128)S(1)}, f32[2,1536,48]{1,2,0:T(8,128)}, u32[]{:S(2)}) copy-start(f32[2,1536,48]{1,2,0:T(8,128)} %param.49) | copy-start | bytes 1769476
  (171 other events, 767.0 us)
Sparse Core Ops, SparseCore 0:
  48.5 138.8 all-reduce.5
  251.2 5.5 reduce-scatter.8
  268.1 9.3 reduce-scatter.10
  295.9 9.3 reduce-scatter.12
  316.5 9.4 reduce-scatter.14
  343.1 9.3 reduce-scatter.16
  385.8 9.3 reduce-scatter.18
  423.1 9.3 reduce-scatter.20
  597.3 13.4 reduce-scatter.22
  668.9 125.7 all-reduce.7

commit v2 on v1

--- a/solution.py
+++ b/solution.py
@@ -205,6 +205,13 @@
     return (grad_hidden, grad_layer_mod, (grad_qkv, grad_proj, grad_up, grad_down))
 
 
+ORDERS = ((0, 1, 2), (0, 2, 1))
+MESH_ID = pl.DeviceIdType.MESH
+NN = (((1,), (0,)), ((), ()))
+NT = (((1,), (1,)), ((), ()))
+TN = (((0,), (0,)), ((), ()))
+
+
 def grid_of(dp_count):
     if dp_count == 16:
         return (4, 2, 2)
@@ -218,9 +225,6 @@
     return tuple(sorted(sizes, reverse=True))
 
 
-ORDERS = ((0, 1, 2), (0, 2, 1))
-
-
 def place(sizes):
     index = lax.axis_index("dp")
     return (index // (sizes[1] * sizes[2]), index // sizes[2] % sizes[1], index % sizes[2])
@@ -231,108 +235,153 @@
     return (moved[0] * sizes[1] + moved[1]) * sizes[2] + moved[2], lax.axis_index("tensor")
 
 
-def entry_barrier(sizes, spot):
+def dot(left, right, form):
+    return lax.dot_general(left, right, form, preferred_element_type=jnp.float32)
+
+
+def greet(peers):
     barrier = pltpu.get_barrier_semaphore()
-    count = 0
+    for peer in peers:
+        pl.semaphore_signal(barrier, inc=1, device_id=peer, device_id_type=MESH_ID)
+    pl.semaphore_wait(barrier, len(peers))
+
+
+def axis_peers(sizes, spot):
+    peers = []
     for axis in range(3):
         for offset in range(1, sizes[axis]):
-            other = (spot[axis] + offset) % sizes[axis]
-            pl.semaphore_signal(
-                barrier,
-                inc=1,
-                device_id=peer_of(sizes, spot, axis, other),
-                device_id_type=pl.DeviceIdType.MESH,
-            )
-            count += 1
-    pl.semaphore_wait(barrier, count)
-
-
-def gather_kernel(sizes, blob_ref, out_ref, send_sem, recv_sem, own_sem):
+            peers.append(peer_of(sizes, spot, axis, (spot[axis] + offset) % sizes[axis]))
+    return peers
+
+
+def norm_parts(x):
+    centre = x - jnp.mean(x, axis=-1, keepdims=True)
+    spread = jnp.mean(centre * centre, axis=-1, keepdims=True)
+    rstd = lax.rsqrt(spread + EPS_LAYER)
+    return centre * rstd, rstd
+
+
+def norm_forward(x, shift, scale):
+    return (norm_parts(x)[0] * (1.0 + scale) + shift).astype(jnp.bfloat16)
+
+
+def norm_backward(x, scale, dy):
+    xh, rstd = norm_parts(x)
+    dxh = dy * (1.0 + scale)
+    dx = (
+        dxh
+        - jnp.mean(dxh, axis=-1, keepdims=True)
+        - xh * jnp.mean(dxh * xh, axis=-1, keepdims=True)
+    ) * rstd
+    return dx, jnp.sum(dy, axis=0, keepdims=True), jnp.sum(dy * xh, axis=0, keepdims=True)
+
+
+GELU_C = math.sqrt(2.0 / math.pi)
+
+
+def step_kernel(sizes, layers, total_count, *refs):
+    (
+        blob,
+        hidden_in,
+        mod,
+        velocity,
+        time_weight,
+        blended,
+        head_rows,
+        own_grads,
+        mod_grads,
+        ends,
+        loss_out,
+        full,
+        got_one,
+        got_two,
+        got_three,
+        gathered,
+        grad_spread,
+        outbox,
+        inbox,
+        qkv,
+        attended,
+        hidden,
+        middle,
+        branch,
+        outer,
+        inner,
+        act,
+        grad_inner,
+        grad_mixed,
+        resid,
+        part,
+        turned,
+        ag_send,
+        ag_recv,
+        rs_send,
+        rs_recv,
+        pair_send,
+        pair_recv,
+        own_sem,
+    ) = refs
+    low = jnp.bfloat16
     spot = place(sizes)
-    waves, columns = out_ref.shape[0], out_ref.shape[5]
+    my_dp, my_core = lax.axis_index("dp"), lax.axis_index("tensor")
+    partner = (my_dp, 1 - my_core)
+    waves, rows, columns = blob.shape
     half = columns // 2
-    own = pltpu.make_async_copy(blob_ref, out_ref.at[:, spot[0], spot[1], spot[2]], own_sem)
+    samples, half_rows, width = hidden_in.shape
+    tokens = 2 * half_rows
+    heads_wide = qkv.shape[3] // 3
+    pairs = heads_wide // (2 * HDIM)
+    mine = pl.ds(pl.multiple_of(my_core * half_rows, half_rows), half_rows)
+    theirs = pl.ds(pl.multiple_of((1 - my_core) * half_rows, half_rows), half_rows)
+    tile = 512
+
+    own = pltpu.make_async_copy(blob, full.at[:, spot[0], spot[1], spot[2]], own_sem)
     own.start()
-    entry_barrier(sizes, spot)
-
-    def copies(wave, order_id, phase):
+    greet(axis_peers(sizes, spot) + [partner])
+
+    unsent = []
+
+    def gather_copies(wave, order_id, phase):
         order = ORDERS[order_id]
         axis = order[phase]
         pick = [spot[a] for a in range(3)]
         for earlier in order[:phase]:
             pick[earlier] = slice(None)
         lanes = pl.ds(order_id * half, half)
-        target = out_ref.at[wave, pick[0], pick[1], pick[2], :, lanes]
-        source = blob_ref.at[wave, :, lanes] if phase == 0 else target
-        made = []
-        for offset in range(1, sizes[axis]):
-            other = (spot[axis] + offset) % sizes[axis]
-            made.append(
-                pltpu.make_async_remote_copy(
-                    src_ref=source,
-                    dst_ref=target,
-                    send_sem=send_sem.at[wave, order_id, phase, offset],
-                    recv_sem=recv_sem.at[wave, order_id, phase, offset],
-                    device_id=peer_of(sizes, spot, axis, other),
-                    device_id_type=pl.DeviceIdType.MESH,
-                )
+        target = full.at[wave, pick[0], pick[1], pick[2], :, lanes]
+        source = blob.at[wave, :, lanes] if phase == 0 else target
+        return [
+            pltpu.make_async_remote_copy(
+                src_ref=source,
+                dst_ref=target,
+                send_sem=ag_send.at[wave, order_id, phase, offset],
+                recv_sem=ag_recv.at[wave, order_id, phase, offset],
+                device_id=peer_of(sizes, spot, axis, (spot[axis] + offset) % sizes[axis]),
+                device_id_type=MESH_ID,
             )
-        return made
-
-    started = []
-    for step in range(waves + 3):
+            for offset in range(1, sizes[axis])
+        ]
+
+    def gather_step(step):
         for phase in reversed(range(4)):
             wave = step - phase
             if not 0 <= wave < waves:
                 continue
             for order_id in range(2):
                 if phase > 0:
-                    for copy in copies(wave, order_id, phase - 1):
+                    for copy in gather_copies(wave, order_id, phase - 1):
                         copy.wait_recv()
                 if wave == 0 and phase == 1 and order_id == 0:
                     own.wait()
                 if phase < 3:
-                    for copy in copies(wave, order_id, phase):
+                    for copy in gather_copies(wave, order_id, phase):
                         copy.start()
-                        started.append(copy)
-    for copy in started:
-        copy.wait_send()
-
-
-def gather_weights(blob, dp_count):
-    sizes = grid_of(dp_count)
-    waves, rows, columns = blob.shape
-    most = max(sizes)
-    out = pl.pallas_call(
-        lambda *refs: gather_kernel(sizes, *refs),
-        out_shape=jax.ShapeDtypeStruct((waves,) + sizes + (rows, columns), blob.dtype),
-        in_specs=[pl.BlockSpec(memory_space=pl.ANY)],
-        out_specs=pl.BlockSpec(memory_space=pl.ANY),
-        scratch_shapes=[
-            pltpu.SemaphoreType.DMA((waves, 2, 3, most)),
-            pltpu.SemaphoreType.DMA((waves, 2, 3, most)),
-            pltpu.SemaphoreType.DMA,
-        ],
-        compiler_params=pltpu.CompilerParams(collective_id=0, has_side_effects=True),
-    )(blob)
-    return out.reshape(waves, dp_count * rows, columns)
-
-
-def reduce_grads_kernel(sizes, waves, *refs):
-    grads = refs[:waves]
-    out_ref = refs[waves]
-    held, got_one, got_two, got_three, send_sem, recv_sem, load_sem = refs[waves + 1 :]
-    spot = place(sizes)
-    half = out_ref.shape[2] // 2
-    loads = []
-    for wave in range(waves):
-        load = pltpu.make_async_copy(grads[wave], held.at[wave], load_sem.at[wave])
-        load.start()
-        loads.append(load)
-    entry_barrier(sizes, spot)
-    inbox = (got_one, got_two, got_three)
-
-    def copies(wave, order_id, phase):
+                        unsent.append(copy)
+
+    inboxes = (got_one, got_two, got_three)
+    rs_unsent = []
+
+    def reduce_copies(wave, order_id, phase):
         order = ORDERS[order_id][::-1]
         axis = order[phase]
         lanes = pl.ds(order_id * half, half)
@@ -343,108 +392,476 @@
             for earlier in order[:phase]:
                 pick[earlier] = spot[earlier]
             pick[axis] = other
-            source = held.at[wave, pick[0], pick[1], pick[2], :, lanes]
-            target = inbox[phase].at[wave, order_id, offset - 1]
             made.append(
                 pltpu.make_async_remote_copy(
-                    src_ref=source,
-                    dst_ref=target,
-                    send_sem=send_sem.at[wave, order_id, phase, offset],
-                    recv_sem=recv_sem.at[wave, order_id, phase, offset],
+                    src_ref=full.at[wave, pick[0], pick[1], pick[2], :, lanes],
+                    dst_ref=inboxes[phase].at[wave, order_id, offset - 1],
+                    send_sem=rs_send.at[wave, order_id, phase, offset],
+                    recv_sem=rs_recv.at[wave, order_id, phase, offset],
                     device_id=peer_of(sizes, spot, axis, other),
-                    device_id_type=pl.DeviceIdType.MESH,
+                    device_id_type=MESH_ID,
                 )
             )
         return made
 
-    def absorb(wave, order_id, phase):
-        order = ORDERS[order_id][::-1]
-        lanes = pl.ds(order_id * half, half)
-        box = inbox[phase]
-        peers = sizes[order[phase]] - 1
-        if phase == 2:
-            total = held[wave, spot[0], spot[1], spot[2], :, lanes].astype(jnp.float32)
-            for p in range(peers):
-                total = total + box[wave, order_id, p].astype(jnp.float32)
-            out_ref[wave, :, lanes] = total
-            return
-        left = order[phase + 1 :]
-        if phase == 0:
-            first, second = left
-            first, second = max(first, second), min(first, second)
-
-            def body(step, carry):
-                low, high = step % sizes[first], step // sizes[first]
-                pick = [spot[0], spot[1], spot[2]]
-                pick[first], pick[second] = low, high
-                total = held[wave, pick[0], pick[1], pick[2], :, lanes].astype(jnp.float32)
+    def reduce_send(wave, phase):
+        for order_id in range(2):
+            for copy in reduce_copies(wave, order_id, phase):
+                copy.start()
+                rs_unsent.append(copy)
+
+    def reduce_absorb(wave, phase):
+        for order_id in range(2):
+            for copy in reduce_copies(wave, order_id, phase):
+                copy.wait_recv()
+            order = ORDERS[order_id][::-1]
+            lanes = pl.ds(order_id * half, half)
+            box = inboxes[phase]
+            peers = sizes[order[phase]] - 1
+            left = sorted(order[phase + 1 :])
+            if not left:
+                total = full[wave, spot[0], spot[1], spot[2], :, lanes].astype(jnp.float32)
                 for p in range(peers):
-                    total = total + box[wave, order_id, p, high, low].astype(jnp.float32)
-                held[wave, pick[0], pick[1], pick[2], :, lanes] = total.astype(held.dtype)
+                    total = total + box[wave, order_id, p].astype(jnp.float32)
+                own_grads[wave, :, lanes] = total
+                continue
+            span = math.prod(sizes[a] for a in left)
+
+            def body(step, carry, order_id=order_id, left=left, box=box, peers=peers, lanes=lanes):
+                index = (step,) if len(left) == 1 else (step // sizes[left[1]], step % sizes[left[1]])
+                pick = list(spot)
+                for a, i in zip(left, index):
+                    pick[a] = i
+                total = full[wave, pick[0], pick[1], pick[2], :, lanes].astype(jnp.float32)
+                for p in range(peers):
+                    total = total + box[(wave, order_id, p) + index].astype(jnp.float32)
+                full[wave, pick[0], pick[1], pick[2], :, lanes] = total.astype(low)
                 return carry
 
-            lax.fori_loop(0, sizes[first] * sizes[second], body, 0)
-        else:
-            (only,) = left
-
-            def body_one(step, carry):
-                pick = [spot[0], spot[1], spot[2]]
-                pick[only] = step
-                total = held[wave, pick[0], pick[1], pick[2], :, lanes].astype(jnp.float32)
-                for p in range(peers):
-                    total = total + box[wave, order_id, p, step].astype(jnp.float32)
-                held[wave, pick[0], pick[1], pick[2], :, lanes] = total.astype(held.dtype)
+            lax.fori_loop(0, span, body, 0)
+
+    def reduce_advance(wave, phase):
+        reduce_absorb(wave, phase - 1)
+        if phase < 3:
+            reduce_send(wave, phase)
+
+    def spread_copy(buffer, slot, stage, b):
+        return pltpu.make_async_remote_copy(
+            src_ref=buffer.at[slot, b, mine],
+            dst_ref=buffer.at[slot, b, mine],
+            send_sem=pair_send.at[stage, b],
+            recv_sem=pair_recv.at[stage, b],
+            device_id=partner,
+            device_id_type=MESH_ID,
+        )
+
+    def spread(buffer, slot, stage, b, value):
+        buffer[slot, b, mine] = value
+        spread_copy(buffer, slot, stage, b).start()
+
+    def fold_copy(slot, stage, b):
+        return pltpu.make_async_remote_copy(
+            src_ref=outbox.at[slot, b],
+            dst_ref=inbox.at[slot, b],
+            send_sem=pair_send.at[stage, b],
+            recv_sem=pair_recv.at[stage, b],
+            device_id=partner,
+            device_id_type=MESH_ID,
+        )
+
+    def fold(slot, stage, b, value):
+        part[b] = value
+        outbox[slot, b] = part[b, theirs].astype(low)
+        fold_copy(slot, stage, b).start()
+
+    def folded(slot, stage, b):
+        fold_copy(slot, stage, b).wait_recv()
+        return part[b, mine] + inbox[slot, b].astype(jnp.float32)
+
+    pair_stages = []
+
+    def each_sample(body):
+        lax.fori_loop(0, samples, lambda b, carry: (body(b), carry)[1], 0)
+
+    def weight(wave):
+        return full[wave].reshape(width, columns)
+
+    def weight_lanes(wave, lanes, count):
+        return full[wave, :, :, :, :, lanes].reshape(width, count)
+
+    def vec(b, row):
+        return mod[b, row : row + 1]
+
+    lane = lax.broadcasted_iota(jnp.int32, (1, 2 * HDIM), 1)
+    first_head = lane < HDIM
+    keep = (
+        jnp.where(first_head, 1.0, 0.0).astype(low),
+        jnp.where(first_head, 0.0, 1.0).astype(low),
+    )
+    factor = HDIM ** (-0.5)
+
+    def pair_lanes(kind, p):
+        return pl.ds(kind * heads_wide + p * 2 * HDIM, 2 * HDIM)
+
+    gather_step(0)
+    gather_step(1)
+    gather_step(2)
+    for layer in range(layers):
+        row = 6 * layer
+        sa, sb, sc, sd = (8 * layer + i for i in range(4))
+        pair_stages += [
+            (lambda b, s=sa, g=2 * layer: spread_copy(gathered, g, s, b)),
+            (lambda b, s=sb, g=4 * layer: fold_copy(g, s, b)),
+            (lambda b, s=sc, g=2 * layer + 1: spread_copy(gathered, g, s, b)),
+            (lambda b, s=sd, g=4 * layer + 1: fold_copy(g, s, b)),
+        ]
+
+        def first(b):
+            if layer == 0:
+                x = hidden_in[b]
+            else:
+                x = middle[layer - 1, b] + vec(b, row - 1) * outer[layer - 1, b]
+            hidden[layer, b] = x
+            spread(gathered, 2 * layer, sa, b, norm_forward(x, vec(b, row), vec(b, row + 1)))
+
+        each_sample(first)
+        gather_step(3 * layer + 3)
+
+        def attention(b):
+            spread_copy(gathered, 2 * layer, sa, b).wait_recv()
+            for kind in range(3):
+                lanes = pl.ds(kind * heads_wide, heads_wide)
+                qkv[layer, b, :, lanes] = dot(
+                    gathered[2 * layer, b], weight_lanes(3 * layer, lanes, heads_wide), NN
+                ).astype(low)
+            for p in range(pairs):
+                q = qkv[layer, b, :, pair_lanes(0, p)]
+                k = qkv[layer, b, :, pair_lanes(1, p)]
+                v = qkv[layer, b, :, pair_lanes(2, p)]
+                got = []
+                for h in range(2):
+                    s = dot(q, k * keep[h], NT) * factor
+                    e = jnp.exp(s - jnp.max(s, axis=-1, keepdims=True))
+                    e = e / jnp.sum(e, axis=-1, keepdims=True)
+                    got.append(dot(e.astype(low), v, NN))
+                attended[layer, b, :, pl.ds(p * 2 * HDIM, 2 * HDIM)] = jnp.where(
+                    first_head, got[0], got[1]
+                ).astype(low)
+            fold(
+                4 * layer,
+                sb,
+                b,
+                dot(
+                    attended[layer, b],
+                    weight_lanes(3 * layer, pl.ds(3 * heads_wide, heads_wide), heads_wide),
+                    NT,
+                ),
+            )
+
+        each_sample(attention)
+
+        def second(b):
+            got = folded(4 * layer, sb, b)
+            branch[layer, b] = got
+            x = hidden[layer, b] + vec(b, row + 2) * got
+            middle[layer, b] = x
+            spread(gathered, 2 * layer + 1, sc, b, norm_forward(x, vec(b, row + 3), vec(b, row + 4)))
+
+        each_sample(second)
+        gather_step(3 * layer + 4)
+
+        def widen(b):
+            spread_copy(gathered, 2 * layer + 1, sc, b).wait_recv()
+
+            def body(n, carry):
+                lanes = pl.ds(pl.multiple_of(n * tile, tile), tile)
+                x = dot(gathered[2 * layer + 1, b], weight_lanes(3 * layer + 1, lanes, tile), NN)
+                inner[b, :, lanes] = x
+                t = jnp.tanh(GELU_C * (x + 0.044715 * x * x * x))
+                act[b, :, lanes] = (0.5 * x * (1.0 + t)).astype(low)
                 return carry
 
-            lax.fori_loop(0, sizes[only], body_one, 0)
+            lax.fori_loop(0, columns // tile, body, 0)
+
+        each_sample(widen)
+        gather_step(3 * layer + 5)
+
+        def narrow(b):
+            fold(4 * layer + 1, sd, b, dot(act[b], weight(3 * layer + 2), NT))
+
+        each_sample(narrow)
+
+        def third(b):
+            outer[layer, b] = folded(4 * layer + 1, sd, b)
+
+        each_sample(third)
+
+    for copy in unsent:
+        copy.wait_send()
+
+    last = layers - 1
+    loss_out[...] = jnp.zeros_like(loss_out)
+    ends[...] = jnp.zeros_like(ends)
+    pad = pl.ds(PATCH, PATCH)
+
+    def head(b):
+        x = middle[last, b] + vec(b, 6 * layers - 1) * outer[last, b]
+        shift, scale = vec(b, 6 * layers), vec(b, 6 * layers + 1)
+        xh, _ = norm_parts(x)
+        normed = (xh * (1.0 + scale) + shift).astype(low)
+        predicted = dot(head_rows[...], normed, NT)
+        error = predicted - velocity[b]
+        weighted = time_weight[b] * error
+        loss_out[...] += jnp.sum(weighted * error, axis=0, keepdims=True)
+        grad_pred = (2.0 * weighted / total_count).astype(low)
+        ends[pad, :] += dot(grad_pred, normed, NN)
+        dx, gshift, gscale = norm_backward(x, scale, dot(grad_pred, head_rows[...], TN))
+        mod_grads[b, 6 * layers : 6 * layers + 1] = gshift
+        mod_grads[b, 6 * layers + 1 : 6 * layers + 2] = gscale
+        resid[b] = dx
+
+    each_sample(head)
+
+    def weight_grad(wave, left, right_of, spans):
+        turned[...] = left.reshape(samples * tokens, width).T
+
+        def body(n, carry):
+            start, count = spans
+            lanes = pl.ds(pl.multiple_of(start + n * count, 128), count)
+            got = dot(turned[...], right_of(pl.ds(pl.multiple_of(n * count, 128), count), count), NN)
+            full[wave, :, :, :, :, lanes] = got.astype(low).reshape(sizes + (rows, count))
+            return carry
+
+        return body
 
     started = []
-    for step in range(waves + 3):
-        for phase in reversed(range(4)):
-            wave = step - phase
-            if not 0 <= wave < waves:
-                continue
-            if phase == 0:
-                loads[wave].wait()
-            for order_id in range(2):
-                if phase > 0:
-                    for copy in copies(wave, order_id, phase - 1):
-                        copy.wait_recv()
-                    absorb(wave, order_id, phase - 1)
-                if phase < 3:
-                    for copy in copies(wave, order_id, phase):
-                        copy.start()
-                        started.append(copy)
-    for copy in started:
+
+    def pump():
+        for entry in started:
+            if entry[1] <= 3:
+                reduce_advance(entry[0], entry[1])
+                entry[1] += 1
+
+    for layer in reversed(range(layers)):
+        row = 6 * layer
+        se, sf, sg, sh = (8 * layer + 4 + i for i in range(4))
+        pair_stages += [
+            (lambda b, s=se, g=2 * layer: spread_copy(grad_spread, g, s, b)),
+            (lambda b, s=sf, g=4 * layer + 2: fold_copy(g, s, b)),
+            (lambda b, s=sg, g=2 * layer + 1: spread_copy(grad_spread, g, s, b)),
+            (lambda b, s=sh, g=4 * layer + 3: fold_copy(g, s, b)),
+        ]
+
+        def grad_first(b):
+            g = resid[b]
+            mod_grads[b, row + 5 : row + 6] = jnp.sum(g * outer[layer, b], axis=0, keepdims=True)
+            spread(grad_spread, 2 * layer, se, b, (vec(b, row + 5) * g).astype(low))
+
+        each_sample(grad_first)
+
+        def grad_wide(b):
+            spread_copy(grad_spread, 2 * layer, se, b).wait_recv()
+
+            def body(n, carry):
+                lanes = pl.ds(pl.multiple_of(n * tile, tile), tile)
+                if layer == last:
+                    x = inner[b, :, lanes]
+                else:
+                    x = dot(
+                        gathered[2 * layer + 1, b], weight_lanes(3 * layer + 1, lanes, tile), NN
+                    )
+                g = dot(grad_spread[2 * layer, b], weight_lanes(3 * layer + 2, lanes, tile), NN)
+                t = jnp.tanh(GELU_C * (x + 0.044715 * x * x * x))
+                if layer != last:
+                    act[b, :, lanes] = (0.5 * x * (1.0 + t)).astype(low)
+                slope = 0.5 * (1.0 + t) + 0.5 * x * (1.0 - t * t) * (
+                    GELU_C * (1.0 + 3.0 * 0.044715 * x * x)
+                )
+                grad_inner[b, :, lanes] = (g * slope).astype(low)
+                return carry
+
+            lax.fori_loop(0, columns // tile, body, 0)
+            fold(4 * layer + 2, sf, b, dot(grad_inner[b], weight(3 * layer + 1), NT))
+
+        each_sample(grad_wide)
+
+        def wide_of(source):
+            def right_of(lanes, count):
+                return source[:, :, lanes].reshape(samples * tokens, count)
+
+            return right_of
+
+        lax.fori_loop(
+            0,
+            columns // tile,
+            weight_grad(3 * layer + 2, grad_spread[2 * layer], wide_of(act), (0, tile)),
+            0,
+        )
+        reduce_send(3 * layer + 2, 0)
+        lax.fori_loop(
+            0,
+            columns // tile,
+            weight_grad(3 * layer + 1, gathered[2 * layer + 1], wide_of(grad_inner), (0, tile)),
+            0,
+        )
+        reduce_send(3 * layer + 1, 0)
+
+        def grad_second(b):
+            dy = folded(4 * layer + 2, sf, b)
+            dx, gshift, gscale = norm_backward(middle[layer, b], vec(b, row + 4), dy)
+            g = dx + resid[b]
+            resid[b] = g
+            mod_grads[b, row + 3 : row + 4] = gshift
+            mod_grads[b, row + 4 : row + 5] = gscale
+            mod_grads[b, row + 2 : row + 3] = jnp.sum(g * branch[layer, b], axis=0, keepdims=True)
+            spread(grad_spread, 2 * layer + 1, sg, b, (vec(b, row + 2) * g).astype(low))
+
+        each_sample(grad_second)
+        pump()
+        started.append([3 * layer + 2, 1])
+        started.append([3 * layer + 1, 1])
+
+        def grad_attention(b):
+            spread_copy(grad_spread, 2 * layer + 1, sg, b).wait_recv()
+            got_all = dot(
+                grad_spread[2 * layer + 1, b],
+                weight_lanes(3 * layer, pl.ds(3 * heads_wide, heads_wide), heads_wide),
+                NN,
+            ).astype(low)
+            for p in range(pairs):
+                ga = got_all[:, p * 2 * HDIM : (p + 1) * 2 * HDIM]
+                q = qkv[layer, b, :, pair_lanes(0, p)]
+                k = qkv[layer, b, :, pair_lanes(1, p)]
+                v = qkv[layer, b, :, pair_lanes(2, p)]
+                gq, gk, gv = [], [], []
+                for h in range(2):
+                    s = dot(k * keep[h], q, NT) * factor
+                    e = jnp.exp(s - jnp.max(s, axis=0, keepdims=True))
+                    e = e / jnp.sum(e, axis=0, keepdims=True)
+                    dp = dot(v * keep[h], ga, NT)
+                    ds = (e * (dp - jnp.sum(e * dp, axis=0, keepdims=True))).astype(low)
+                    gv.append(dot(e.astype(low), ga, NN))
+                    gk.append(dot(ds, q, NN))
+                    gq.append(dot(ds, k, TN))
+                for kind, got, scale in ((0, gq, factor), (1, gk, factor), (2, gv, 1.0)):
+                    grad_mixed[b, :, pair_lanes(kind, p)] = (
+                        jnp.where(first_head, got[0], got[1]) * scale
+                    ).astype(low)
+            fold(
+                4 * layer + 3,
+                sh,
+                b,
+                dot(
+                    grad_mixed[b],
+                    weight_lanes(3 * layer, pl.ds(0, 3 * heads_wide), 3 * heads_wide),
+                    NT,
+                ),
+            )
+
+        each_sample(grad_attention)
+        lax.fori_loop(
+            0,
+            3,
+            weight_grad(3 * layer, gathered[2 * layer], wide_of(grad_mixed), (0, heads_wide)),
+            0,
+        )
+        lax.fori_loop(
+            0,
+            1,
+            weight_grad(
+                3 * layer,
+                grad_spread[2 * layer + 1],
+                wide_of(attended.at[layer]),
+                (3 * heads_wide, heads_wide),
+            ),
+            0,
+        )
+        reduce_send(3 * layer, 0)
+        pump()
+        started.append([3 * layer, 1])
+
+        def grad_third(b):
+            dy = folded(4 * layer + 3, sh, b)
+            dx, gshift, gscale = norm_backward(hidden[layer, b], vec(b, row + 1), dy)
+            resid[b] = dx + resid[b]
+            mod_grads[b, row : row + 1] = gshift
+            mod_grads[b, row + 1 : row + 2] = gscale
+
+        each_sample(grad_third)
+
+    def patch(b):
+        ends[pl.ds(0, PATCH), :] += dot(blended[b], resid[b].astype(low), NN)
+
+    each_sample(patch)
+    for _ in range(3):
+        pump()
+    for copy in rs_unsent:
         copy.wait_send()
 
-
-def reduce_grads(grads, dp_count):
+    def finish(b):
+        for stage in pair_stages:
+            stage(b).wait_send()
+
+    each_sample(finish)
+
+
+def train_step(blob, hidden, mod, velocity, time_weight, blended, head_rows, dp_count, layers, total):
     sizes = grid_of(dp_count)
-    waves = len(grads)
-    rows, columns = grads[0].shape[0] // dp_count, grads[0].shape[1]
+    waves, rows, columns = blob.shape
+    samples, half_rows, width = hidden.shape
+    tokens = 2 * half_rows
     half = columns // 2
+    heads_wide = columns // 4
     most = max(sizes)
-    grads = [g.reshape(sizes + (rows, columns)) for g in grads]
-    low = jnp.bfloat16
+    low, wide = jnp.bfloat16, jnp.float32
+    in_vmem = pl.BlockSpec(memory_space=pltpu.VMEM)
+    stages = 8 * layers
+    resid_shape = (layers, samples, half_rows, width)
+    dma = pltpu.SemaphoreType.DMA
     return pl.pallas_call(
-        lambda *refs: reduce_grads_kernel(sizes, waves, *refs),
-        out_shape=jax.ShapeDtypeStruct((waves, rows, columns), jnp.float32),
-        in_specs=[pl.BlockSpec(memory_space=pl.ANY)] * waves,
-        out_specs=pl.BlockSpec(memory_space=pltpu.VMEM),
+        lambda *refs: step_kernel(sizes, layers, total, *refs),
+        out_shape=(
+            jax.ShapeDtypeStruct((waves, rows, columns), wide),
+            jax.ShapeDtypeStruct(mod.shape, wide),
+            jax.ShapeDtypeStruct((2 * PATCH, width), wide),
+            jax.ShapeDtypeStruct((8, half_rows), wide),
+        ),
+        in_specs=[pl.BlockSpec(memory_space=pl.ANY)] + [in_vmem] * 6,
+        out_specs=(in_vmem,) * 4,
         scratch_shapes=[
             pltpu.VMEM((waves,) + sizes + (rows, columns), low),
             pltpu.VMEM((waves, 2, sizes[2] - 1, sizes[0], sizes[1], rows, half), low),
             pltpu.VMEM((waves, 2, sizes[1] - 1, sizes[0], rows, half), low),
             pltpu.VMEM((waves, 2, sizes[0] - 1, rows, half), low),
-            pltpu.SemaphoreType.DMA((waves, 2, 3, most)),
-            pltpu.SemaphoreType.DMA((waves, 2, 3, most)),
-            pltpu.SemaphoreType.DMA((waves,)),
+            pltpu.VMEM((2 * layers, samples, tokens, width), low),
+            pltpu.VMEM((2 * layers, samples, tokens, width), low),
+            pltpu.VMEM((4 * layers, samples, half_rows, width), low),
+            pltpu.VMEM((4 * layers, samples, half_rows, width), low),
+            pltpu.VMEM((layers, samples, tokens, 3 * heads_wide), low),
+            pltpu.VMEM((layers, samples, tokens, heads_wide), low),
+            pltpu.VMEM(resid_shape, wide),
+            pltpu.VMEM(resid_shape, wide),
+            pltpu.VMEM(resid_shape, wide),
+            pltpu.VMEM(resid_shape, wide),
+            pltpu.VMEM((samples, tokens, columns), wide),
+            pltpu.VMEM((samples, tokens, columns), low),
+            pltpu.VMEM((samples, tokens, columns), low),
+            pltpu.VMEM((samples, tokens, 3 * heads_wide), low),
+            pltpu.VMEM((samples, half_rows, width), wide),
+            pltpu.VMEM((samples, tokens, width), wide),
+            pltpu.VMEM((width, samples * tokens), low),
+            dma((waves, 2, 3, most)),
+            dma((waves, 2, 3, most)),
+            dma((waves, 2, 3, most)),
+            dma((waves, 2, 3, most)),
+            dma((stages, samples)),
+            dma((stages, samples)),
+            dma,
         ],
         compiler_params=pltpu.CompilerParams(
-            collective_id=1, has_side_effects=True, vmem_limit_bytes=60 * 2**20
+            collective_id=0, has_side_effects=True, vmem_limit_bytes=64 * 2**20 - 2**17
         ),
-    )(*grads)
+    )(blob, hidden, mod, velocity, time_weight, blended, head_rows)
 
 
 def gather_plain(blob, dp_count):
@@ -510,7 +927,6 @@
         parts.append(up_w[i].astype(low))
         parts.append(down_w[i].T.astype(low))
     blob = jnp.stack(parts)
-    full = (gather_weights if kernels else gather_plain)(blob, dp_count)
     heads_wide = qkv_w.shape[3]
 
     ids = lax.all_gather(jnp.stack([time_ids, labels]), "dp", axis=1, tiled=True)
@@ -546,69 +962,82 @@
         jnp.einsum("bpn,pd->bnd", blended, patch_rows, preferred_element_type=jnp.float32)
         + position_table(token_index, model_width)[None]
     )
-    saved_list = []
-    fetched = []
-    for layer_id in range(layer_count):
-        packed = full[3 * layer_id]
-        weights = (
-            packed[:, : 3 * heads_wide].reshape(model_width, 3, heads_wide),
-            packed[:, 3 * heads_wide :],
-            full[3 * layer_id + 1],
-            full[3 * layer_id + 2],
+    time_weight = 0.5 + moment
+    total_count = samples * dp_count * half_rows * tensor_count * PATCH
+    if kernels:
+        table = modulation.reshape(samples, -1, model_width)
+        own_grads, all_mods, ends, loss_rows = train_step(
+            blob,
+            hidden,
+            jnp.pad(table, ((0, 0), (0, 2), (0, 0))),
+            velocity,
+            jnp.broadcast_to(time_weight[:, None, None], velocity.shape),
+            blended,
+            head_rows,
+            dp_count,
+            layer_count,
+            float(total_count),
         )
-        layer_mod = modulation[
-            :, 6 * layer_id * model_width : (6 * layer_id + 6) * model_width
-        ].reshape(samples, 6, model_width)
-        hidden, saved_state = block_forward(hidden, layer_mod, weights)
-        saved_list.append(saved_state)
-        fetched.append(weights)
-    final_mod = modulation[:, 6 * layer_count * model_width :].reshape(samples, 2, model_width)
-    final_normed = modulated_norm(hidden, final_mod[:, 0], final_mod[:, 1]).astype(jnp.bfloat16)
-    predicted = jnp.einsum(
-        "bnd,pd->bpn", final_normed, head_rows, preferred_element_type=jnp.float32
-    )
-    time_weight = 0.5 + moment
-    error = predicted - velocity
-    loss_part = jnp.sum(time_weight[:, None, None] * error * error)
-    total_count = samples * dp_count * half_rows * tensor_count * PATCH
-    grad_pred = (time_weight[:, None, None] * (2.0 * error) / total_count).astype(jnp.bfloat16)
-    grad_head = jnp.einsum(
-        "bpn,bnd->pd", grad_pred, final_normed, preferred_element_type=jnp.float32
-    )
-    grad_final = jnp.einsum("bpn,pd->bnd", grad_pred, head_rows, preferred_element_type=jnp.float32)
-    _, final_back = jax.vjp(modulated_norm, hidden, final_mod[:, 0], final_mod[:, 1])
-    grad_hidden, grad_fshift, grad_fscale = final_back(grad_final)
-    mod_grads = [None] * layer_count
-    layer_grads = [None] * (3 * layer_count)
-    for layer_id in reversed(range(layer_count)):
-        layer_mod = modulation[
-            :, 6 * layer_id * model_width : (6 * layer_id + 6) * model_width
-        ].reshape(samples, 6, model_width)
-        grad_hidden, grad_layer_mod, grads = block_backward(
-            grad_hidden, layer_mod, fetched[layer_id], saved_list[layer_id]
+        loss_part = jnp.sum(loss_rows[0])
+        all_mods = all_mods[:, : table.shape[1]].reshape(samples, -1)
+    else:
+        full = gather_plain(blob, dp_count)
+        saved_list = []
+        fetched = []
+        for layer_id in range(layer_count):
+            packed = full[3 * layer_id]
+            weights = (
+                packed[:, : 3 * heads_wide].reshape(model_width, 3, heads_wide),
+                packed[:, 3 * heads_wide :],
+                full[3 * layer_id + 1],
+                full[3 * layer_id + 2],
+            )
+            layer_mod = modulation[
+                :, 6 * layer_id * model_width : (6 * layer_id + 6) * model_width
+            ].reshape(samples, 6, model_width)
+            hidden, saved_state = block_forward(hidden, layer_mod, weights)
+            saved_list.append(saved_state)
+            fetched.append(weights)
+        final_mod = modulation[:, 6 * layer_count * model_width :].reshape(samples, 2, model_width)
+        final_normed = modulated_norm(hidden, final_mod[:, 0], final_mod[:, 1]).astype(jnp.bfloat16)
+        predicted = jnp.einsum(
+            "bnd,pd->bpn", final_normed, head_rows, preferred_element_type=jnp.float32
         )
-        layer_grads[3 * layer_id] = jnp.concatenate(
-            [grads[0].reshape(model_width, 3 * heads_wide).astype(low), grads[1].astype(low)],
+        error = predicted - velocity
+        loss_part = jnp.sum(time_weight[:, None, None] * error * error)
+        grad_pred = (time_weight[:, None, None] * (2.0 * error) / total_count).astype(jnp.bfloat16)
+        grad_head = jnp.einsum(
+            "bpn,bnd->pd", grad_pred, final_normed, preferred_element_type=jnp.float32
+        )
+        grad_final = jnp.einsum("bpn,pd->bnd", grad_pred, head_rows, preferred_element_type=jnp.float32)
+        _, final_back = jax.vjp(modulated_norm, hidden, final_mod[:, 0], final_mod[:, 1])
+        grad_hidden, grad_fshift, grad_fscale = final_back(grad_final)
+        mod_grads = [None] * layer_count
+        layer_grads = [None] * (3 * layer_count)
+        for layer_id in reversed(range(layer_count)):
+            layer_mod = modulation[
+                :, 6 * layer_id * model_width : (6 * layer_id + 6) * model_width
+            ].reshape(samples, 6, model_width)
+            grad_hidden, grad_layer_mod, grads = block_backward(
+                grad_hidden, layer_mod, fetched[layer_id], saved_list[layer_id]
+            )
+            layer_grads[3 * layer_id] = jnp.concatenate(
+                [grads[0].reshape(model_width, 3 * heads_wide).astype(low), grads[1].astype(low)],
+                axis=1,
+            )
+            layer_grads[3 * layer_id + 1] = grads[2].astype(low)
+            layer_grads[3 * layer_id + 2] = grads[3].astype(low)
+            mod_grads[layer_id] = grad_layer_mod.reshape(samples, 6 * model_width)
+        own_grads = reduce_plain(layer_grads, dp_count)
+        grad_patch = jnp.einsum(
+            "bpn,bnd->pd", blended, grad_hidden.astype(jnp.bfloat16), preferred_element_type=jnp.float32
+        )
+        ends = jnp.concatenate([grad_patch, grad_head], axis=0)
+        all_mods = jnp.concatenate(
+            mod_grads
+            + [jnp.stack([grad_fshift, grad_fscale], axis=1).reshape(samples, 2 * model_width)],
             axis=1,
         )
-        layer_grads[3 * layer_id + 1] = grads[2].astype(low)
-        layer_grads[3 * layer_id + 2] = grads[3].astype(low)
-        mod_grads[layer_id] = grad_layer_mod.reshape(samples, 6 * model_width)
-    flow = list(reversed(range(3 * layer_count)))
-    if kernels:
-        summed = reduce_grads([layer_grads[i] for i in flow], dp_count)
-    else:
-        summed = reduce_plain([layer_grads[i] for i in flow], dp_count)
-    own_grads = [summed[flow.index(i)] for i in range(3 * layer_count)]
-
-    grad_patch = jnp.einsum(
-        "bpn,bnd->pd", blended, grad_hidden.astype(jnp.bfloat16), preferred_element_type=jnp.float32
-    )
-    all_mods = jnp.concatenate(
-        mod_grads
-        + [jnp.stack([grad_fshift, grad_fscale], axis=1).reshape(samples, 2 * model_width)],
-        axis=1,
-    )
     grad_mods = lax.all_gather(
         lax.psum(all_mods.astype(low), "tensor"), "dp", axis=0, tiled=True
     )
@@ -627,7 +1056,7 @@
     grad_cond_w = jnp.concatenate([grad_time_two, grad_table], axis=0)
     ends, grad_time_act, loss_sum = lax.psum(
         (
-            jnp.concatenate([grad_patch, grad_head], axis=0),
+            ends,
             grad_time_act / tensor_count,
             loss_part,
         ),

time: 878 us -> 737 us (0.84)
  matrix products: 107 us -> 14 us
  waiting for transfers between devices: 147 us -> 222 us
  local copies, waits for them, and re-layouts: 71.3 us -> 21.5 us
  other arithmetic: 80 us -> 35.7 us
  blocking collectives: 153 us -> 124 us
    unnamed x11 -> x3, waiting for transfers between devices: 0.19 us -> 109 us
    dot_general x40 -> x0, matrix products: 91.5 us -> none  [the longest x2 9.04 us: block_backward(): jnp.einsum('bnd,bnf->df', gathered_two, grad_inner, preferred_element_typ...]
    reduce_scatter x8 -> x0, waiting for transfers between devices: 32.8 us -> none  [fold_rows(): lax.psum_scatter(term_rows.astype(jnp.bfloat16), 'tensor', scatter_dimens...]
    all_gather x8 -> x0, blocking collectives: 31.3 us -> none  [spread_rows(): return lax.all_gather(part_rows, 'tensor', axis=1, tiled=True)]
    reduce_sum x28 -> x1, other arithmetic: 31.5 us -> 1.29 us  [local(): loss_part = jnp.sum(loss_rows[0])]
    slice x7 -> x1, local copies, waits for them, and re-layouts: 20.1 us -> 0.61 us  [local(): head_rows = small_low[PATCH + FREQ:]]
    unnamed x397 -> x107, local copies, waits for them, and re-layouts: 27.3 us -> 8.64 us
    pallas_call x2 -> x1, Pallas kernels: 284 us -> 288 us  [train_step(): pl.pallas_call(lambda *refs: step_kernel(sizes, layers, total, *refs), ou...]
  transfers between devices with their start and end apart: 10 -> 2, of which waited for: 8 -> 2; matrix products, arithmetic and copies ran while one was open for 9% -> 3% of each run, Pallas kernels for 17% -> 0%
where the time goes in v2:
time: 737 us; the launch traced here: 727 us
  Pallas kernels  288 us (39%)
  waiting for transfers between devices  222 us (30%)
  blocking collectives  124 us (17%)
  other arithmetic  35.7 us (5%)
  between operations  21.6 us (3%)
  local copies, waits for them, and re-layouts  21.5 us (3%)
  matrix products  14 us (2%)
    pallas_call x1, Pallas kernels, train_step(): pl.pallas_call(lambda *refs: step_kernel(sizes, layers, total, *refs), ou...  288 us
    psum x1, waiting for transfers between devices, local(): lax.psum((ends, grad_time_act / tensor_count, loss_part), ('dp', 'tensor'))  113 us
    unnamed x3, waiting for transfers between devices  109 us
    psum x1, blocking collectives, local(): lax.psum(jnp.stack([squares(weights_list), squares(updates)]), ('dp', 'te...  41.5 us
    all_gather x1, blocking collectives, local(): lax.all_gather(lax.psum(all_mods.astype(low), 'tensor'), 'dp', axis=0, ti...  36.6 us
    all_gather x1, blocking collectives, local(): lax.all_gather(jnp.stack([time_ids, labels]), 'dp', axis=1, tiled=True)  34.6 us
    reduce_sum x6, other arithmetic, squares(): sums.append(jnp.sum(a * a, axis=axes).reshape(-1) * shares[kind_id])  15.5 us
  transfers between devices with their start and end apart: 2, of which 2 were waited for; matrix products, arithmetic and copies ran while one was open for 3% of the time, Pallas kernels for 0%

profile of v2, /device:TPU:1, one launch (start us, length us, event | category | flops | bytes accessed | tf_op | source)
XLA Modules:
  0.0 726.8 jit_solution(8172934783117534857)
XLA Ops:
  8.2 34.6 %all-gather = s32[16,2,2]{2,1,0:T(2,128)S(1)} all-gather(s32[1,2,2]{2,1,0:T(2,128)S(1)} %bitcast.109), channel_id=1, replica_groups=mesh['dp'=16,'tensor'=2] {'dp'}, dimensions={0}, use_global_device_ids=true | all-gather | bytes 272 | tf_op jit(solution)/shard_map/all_gather | solution.py:932
  46.4 1.4 fusion.6
  56.8 109.0 %all-reduce.7.cloned.1.call-done = f32[32,10752]{1,0:T(8,128)} async-done(((f32[32,10752]{1,0:T(8,128)}), f32[32,10752]{1,0:T(8,128)}) %all-reduce.7.cloned.1.call-update) | async-done | bytes 1376272
  168.2 287.6 %shard_map.425 = (f32[6,48,1536]{2,1,0:T(8,128)}, f32[2,16,768]{2,1,0:T(8,128)}, f32[32,768]{1,0:T(8,128)}, f32[8,128]{1,0:T(8,128)}) custom-call(bf16[6,48,1536]{2,1,0:T(8,128)(2,1)} %fusion.13.refs_0_, f32[2,128,768]{2,1,0:T(8,128)} %convolution_add_fusion.refs_1_, f32[2,16,768]{2,1,0:T(8,128)} %pad.4.refs_2_, f32[2,16,128]{2,1,0:T(8,128)} %refs_3_.1, ...), custom_call_target="tpu_custom_call" | custom-call | tf_op jit(solution)/shard_map/pallas_call | solution.py:821
  457.0 11.7 %psum.36 = bf16[2,10752]{1,0:T(2,128)(2,1)S(1)} all-reduce(bf16[2,10752]{1,0:T(2,128)(2,1)S(1)} %bitcast.106), channel_id=1, replica_groups=mesh['dp'=16,'tensor'=2] {'tensor'}, use_global_device_ids=true, to_apply=%region_9.10 | all-reduce | flops 21504 | bytes 86016 | tf_op jit(solution)/shard_map/psum | solution.py:1042
  468.7 36.6 %all-gather.1 = bf16[16,2,10752]{2,1,0:T(2,128)(2,1)} all-gather(bf16[1,2,10752]{2,1,0:T(2,128)(2,1)S(1)} %bitcast.107), channel_id=1, replica_groups=mesh['dp'=16,'tensor'=2] {'dp'}, dimensions={0}, use_global_device_ids=true | all-gather | bytes 731136 | tf_op jit(solution)/shard_map/all_gather | solution.py:1041
  505.3 1.4 reshape.303
  507.1 1.8 convolution_multiply_fusion
  512.5 1.7 multiply_reduce_fusion.11
  518.0 6.9 multiply_reduce_fusion.1
  526.4 1.8 copy_dynamic-update-slice_fusion
  528.2 3.1 multiply_reduce_fusion.9
  531.3 2.6 multiply_reduce_fusion.13
  533.9 2.1 multiply_reduce_fusion.6
  536.1 2.0 multiply_reduce_fusion.7
  539.4 112.9 %all-reduce.9.cloned.1.call-done = (f32[32,768]{1,0:T(8,128)}, f32[32,768]{1,0:T(8,128)}) async-done(((f32[32,768]{1,0:T(8,128)}, f32[32,768]{1,0:T(8,128)}), (f32[32,768]{1,0:T(8,128)}, f32[32,768]{1,0:T(8,128)})) %all-reduce.9.cloned.1.call-update) | async-done | bytes 196624 | tf_op jit(solution)/shard_map/psum | solution.py:1057
  654.3 4.0 multiply_reduce_fusion.3
  659.6 1.3 concatenate.57
  662.4 41.5 %all-reduce.2 = (f32[2,11]{1,0:T(2,128)S(1)}, f32[]{:T(128)}) all-reduce(f32[2,11]{1,0:T(2,128)S(1)} %pad_maximum_fusion.9, f32[]{:T(128)} %slice_reduce_fusion), channel_id=1, replica_groups=mesh['dp'=16,'tensor'=2] {'dp','tensor'}, use_global_device_ids=true, to_apply=%region_18.19 | all-reduce | flops 23 | bytes 184 | tf_op jit(solution)/shard_map/psum | solution.py:1100
  706.5 1.8 multiply_subtract_fusion.6
  708.3 2.1 multiply_subtract_fusion.5
  710.4 2.3 multiply_subtract_fusion.4
  715.1 1.4 multiply_subtract_fusion.1
  717.1 2.4 multiply_subtract_fusion
  (161 shorter events, 31.2 us)
Async XLA Ops:
  7.2 39.1 %copy-start = (f32[48,10752]{1,0:T(8,128)S(1)}, f32[48,10752]{1,0:T(8,128)}, u32[]{:S(2)}) copy-start(f32[48,10752]{1,0:T(8,128)} %param.37) | copy-start | bytes 6193156
  7.2 158.6 %all-reduce.7.cloned.1.call-start = ((), (), s32[]{:S(2)}) async-start(), calls=%async_computation | async-start | bytes 2752512
  47.8 604.4 %all-reduce.9.cloned.1.call-start = ((), (), s32[]{:S(2)}) async-start(), calls=%async_computation.1 | async-start | bytes 393216 | tf_op jit(solution)/shard_map/psum | solution.py:1057
  48.8 5.3 copy-start.37
  48.8 5.3 copy-start.38
  54.2 114.0 %copy-start.36 = (bf16[2,16,128]{2,1,0:T(8,128)(2,1)}, bf16[2,16,128]{2,1,0:T(8,128)(2,1)S(1)}, u32[]{:S(2)}) copy-start(bf16[2,16,128]{2,1,0:T(8,128)(2,1)S(1)} %add_convert_fusion.refs_5_) | copy-start | bytes 24580
  455.9 50.8 %copy-start.1 = (f32[48,10752]{1,0:T(8,128)S(1)}, f32[48,10752]{1,0:T(8,128)}, u32[]{:S(2)}) copy-start(f32[48,10752]{1,0:T(8,128)} %param.37) | copy-start | bytes 6193156
  518.0 10.2 %copy-start.9 = (f32[2,48,3,384]{3,1,2,0:T(8,128)S(1)}, f32[2,48,3,384]{3,1,2,0:T(8,128)}, u32[]{:S(2)}) copy-start(f32[2,48,3,384]{3,1,2,0:T(8,128)} %param.40) | copy-start | bytes 1327108
  525.0 6.3 copy-start.22
  526.3 7.6 %copy-start.4 = (f32[2,1536,48]{1,2,0:T(8,128)S(1)}, f32[2,1536,48]{1,2,0:T(8,128)}, u32[]{:S(2)}) copy-start(f32[2,1536,48]{1,2,0:T(8,128)} %param.49) | copy-start | bytes 1769476
  526.4 7.6 %copy-start.25 = (f32[1,1536,48]{1,2,0:T(8,128)S(1)}, f32[1,1536,48]{1,2,0:T(8,128)}, u32[]{:S(2)}) copy-start(f32[1,1536,48]{1,2,0:T(8,128)} %get-tuple-element.109) | copy-start | bytes 884740
  526.4 7.6 %copy-start.26 = (f32[1,1536,48]{1,2,0:T(8,128)S(1)}, f32[1,1536,48]{1,2,0:T(8,128)}, u32[]{:S(2)}) copy-start(f32[1,1536,48]{1,2,0:T(8,128)} %get-tuple-element.110) | copy-start | bytes 884740
  526.4 7.6 %copy-start.27 = (f32[2,1536,48]{1,2,0:T(8,128)S(1)}, f32[2,1536,48]{1,2,0:T(8,128)}, u32[]{:S(2)}) copy-start(f32[2,1536,48]{1,2,0:T(8,128)} %param.50) | copy-start | bytes 1769476
  526.4 7.5 %copy-start.28 = (f32[2,1536,48]{1,2,0:T(8,128)S(1)}, f32[2,1536,48]{1,2,0:T(8,128)}, u32[]{:S(2)}) copy-start(f32[2,1536,48]{1,2,0:T(8,128)} %param.51) | copy-start | bytes 1769476
  531.3 4.8 copy-start.24
  536.1 118.2 %copy-start.2 = (f32[288,768]{1,0:T(8,128)S(1)}, f32[288,768]{1,0:T(8,128)}, u32[]{:S(2)}) copy-start(f32[288,768]{1,0:T(8,128)} %param.31) | copy-start | bytes 2654212
  654.3 5.3 copy-start.41
  654.3 6.6 copy-start.39
  654.3 6.6 copy-start.40
  654.3 6.6 copy-start.42
  703.9 6.6 copy-start.10
  703.9 8.9 %copy-start.14 = (f32[2,1536,48]{1,2,0:T(8,128)S(1)}, f32[2,1536,48]{1,2,0:T(8,128)}, u32[]{:S(2)}) copy-start(f32[2,1536,48]{1,2,0:T(8,128)} %get-tuple-element.95) | copy-start | bytes 1769476
  703.9 8.9 %copy-start.15 = (f32[2,1536,48]{1,2,0:T(8,128)S(1)}, f32[2,1536,48]{1,2,0:T(8,128)}, u32[]{:S(2)}) copy-start(f32[2,1536,48]{1,2,0:T(8,128)} %get-tuple-element.96) | copy-start | bytes 1769476
  703.9 10.0 %copy-start.44 = (f32[2,11]{1,0:T(2,128)}, f32[2,11]{1,0:T(2,128)S(1)}, u32[]{:S(2)}) copy-start(f32[2,11]{1,0:T(2,128)S(1)} %add_sqrt_fusion) | copy-start | bytes 268
  (26 other events, 72.9 us)
Sparse Core Ops, SparseCore 0:
  47.9 117.8 all-reduce.6
  526.5 125.7 all-reduce.8

commit v3 on v2

--- a/solution.py
+++ b/solution.py
@@ -206,6 +206,8 @@
 
 
 ORDERS = ((0, 1, 2), (0, 2, 1))
+LAG = 2
+BURST_LAG = 3
 MESH_ID = pl.DeviceIdType.MESH
 NN = (((1,), (0,)), ((), ()))
 NT = (((1,), (1,)), ((), ()))
@@ -283,15 +285,19 @@
     (
         blob,
         hidden_in,
-        mod,
+        timing,
+        cond_cols,
+        mod_rows,
         velocity,
         time_weight,
         blended,
         head_rows,
         own_grads,
-        mod_grads,
-        ends,
-        loss_out,
+        timing_all,
+        cond_out,
+        grad_cond_out,
+        grad_mods,
+        sums,
         full,
         got_one,
         got_two,
@@ -313,6 +319,20 @@
         resid,
         part,
         turned,
+        timing_box,
+        mod_part,
+        mod_box,
+        mod,
+        mod_grads,
+        mod_grads_low,
+        mod_grads_box,
+        ends,
+        loss_row,
+        ends_box,
+        sum_part,
+        sum_box,
+        small_send,
+        small_recv,
         ag_send,
         ag_recv,
         rs_send,
@@ -326,65 +346,106 @@
     my_dp, my_core = lax.axis_index("dp"), lax.axis_index("tensor")
     partner = (my_dp, 1 - my_core)
     waves, rows, columns = blob.shape
-    half = columns // 2
     samples, half_rows, width = hidden_in.shape
     tokens = 2 * half_rows
     heads_wide = qkv.shape[3] // 3
     pairs = heads_wide // (2 * HDIM)
     mine = pl.ds(pl.multiple_of(my_core * half_rows, half_rows), half_rows)
     theirs = pl.ds(pl.multiple_of((1 - my_core) * half_rows, half_rows), half_rows)
-    tile = 512
+    tile = 384
+    per_wave = columns // tile
+    chunks = waves * per_wave
 
     own = pltpu.make_async_copy(blob, full.at[:, spot[0], spot[1], spot[2]], own_sem)
     own.start()
-    greet(axis_peers(sizes, spot) + [partner])
+    dp_peers = all_peers(sizes[0] * sizes[1] * sizes[2], False)
+    greet(dp_peers + [partner])
+
+    small_unsent = []
+
+    def small(kind, slot, source, target, device):
+        return pltpu.make_async_remote_copy(
+            src_ref=source,
+            dst_ref=target,
+            send_sem=small_send.at[kind, slot],
+            recv_sem=small_recv.at[kind, slot],
+            device_id=device,
+            device_id_type=MESH_ID,
+        )
+
+    def small_start(copies):
+        for copy in copies:
+            copy.start()
+            small_unsent.append(copy)
+
+    devices = len(dp_peers) + 1
+    mod_part[...] = jnp.zeros_like(mod_part)
+    mod_grads[...] = jnp.zeros_like(mod_grads)
+    time_copies = [
+        small(0, i, timing, timing_box.at[my_dp], peer) for i, peer in enumerate(dp_peers)
+    ]
+    small_start(time_copies)
+    timing_box[my_dp] = timing[...]
 
     unsent = []
 
-    def gather_copies(wave, order_id, phase):
-        order = ORDERS[order_id]
+    def chunk_place(chunk):
+        return chunk // per_wave, pl.ds(chunk % per_wave * tile, tile), ORDERS[chunk % 2]
+
+    def gather_copies(chunk, phase):
+        wave, lanes, order = chunk_place(chunk)
         axis = order[phase]
         pick = [spot[a] for a in range(3)]
         for earlier in order[:phase]:
             pick[earlier] = slice(None)
-        lanes = pl.ds(order_id * half, half)
         target = full.at[wave, pick[0], pick[1], pick[2], :, lanes]
         source = blob.at[wave, :, lanes] if phase == 0 else target
         return [
             pltpu.make_async_remote_copy(
                 src_ref=source,
                 dst_ref=target,
-                send_sem=ag_send.at[wave, order_id, phase, offset],
-                recv_sem=ag_recv.at[wave, order_id, phase, offset],
+                send_sem=ag_send.at[chunk, phase, offset],
+                recv_sem=ag_recv.at[chunk, phase, offset],
                 device_id=peer_of(sizes, spot, axis, (spot[axis] + offset) % sizes[axis]),
                 device_id_type=MESH_ID,
             )
             for offset in range(1, sizes[axis])
         ]
 
-    def gather_step(step):
+    gather_state = [0]
+
+    def gather_step():
+        step = gather_state[0]
+        gather_state[0] += 1
         for phase in reversed(range(4)):
-            wave = step - phase
-            if not 0 <= wave < waves:
+            chunk = step - LAG * phase
+            if not 0 <= chunk < chunks:
                 continue
-            for order_id in range(2):
-                if phase > 0:
-                    for copy in gather_copies(wave, order_id, phase - 1):
-                        copy.wait_recv()
-                if wave == 0 and phase == 1 and order_id == 0:
-                    own.wait()
-                if phase < 3:
-                    for copy in gather_copies(wave, order_id, phase):
-                        copy.start()
-                        unsent.append(copy)
+            if phase > 0:
+                for copy in gather_copies(chunk, phase - 1):
+                    copy.wait_recv()
+            if chunk == 0 and phase == 1:
+                own.wait()
+            if phase < 3:
+                for copy in gather_copies(chunk, phase):
+                    copy.start()
+                    unsent.append(copy)
+
+    def gather_until(wave):
+        while gather_state[0] <= per_wave * (wave + 1) - 1 + 3 * LAG:
+            gather_step()
+
+    def gather_more():
+        if gather_state[0] < chunks + 3 * LAG:
+            gather_step()
 
     inboxes = (got_one, got_two, got_three)
     rs_unsent = []
 
-    def reduce_copies(wave, order_id, phase):
-        order = ORDERS[order_id][::-1]
+    def reduce_copies(chunk, phase):
+        wave, lanes, order = chunk_place(chunk)
+        order = order[::-1]
         axis = order[phase]
-        lanes = pl.ds(order_id * half, half)
         made = []
         for offset in range(1, sizes[axis]):
             other = (spot[axis] + offset) % sizes[axis]
@@ -395,55 +456,71 @@
             made.append(
                 pltpu.make_async_remote_copy(
                     src_ref=full.at[wave, pick[0], pick[1], pick[2], :, lanes],
-                    dst_ref=inboxes[phase].at[wave, order_id, offset - 1],
-                    send_sem=rs_send.at[wave, order_id, phase, offset],
-                    recv_sem=rs_recv.at[wave, order_id, phase, offset],
+                    dst_ref=inboxes[phase].at[chunk, offset - 1],
+                    send_sem=rs_send.at[chunk, phase, offset],
+                    recv_sem=rs_recv.at[chunk, phase, offset],
                     device_id=peer_of(sizes, spot, axis, other),
                     device_id_type=MESH_ID,
                 )
             )
         return made
 
-    def reduce_send(wave, phase):
-        for order_id in range(2):
-            for copy in reduce_copies(wave, order_id, phase):
-                copy.start()
-                rs_unsent.append(copy)
-
-    def reduce_absorb(wave, phase):
-        for order_id in range(2):
-            for copy in reduce_copies(wave, order_id, phase):
-                copy.wait_recv()
-            order = ORDERS[order_id][::-1]
-            lanes = pl.ds(order_id * half, half)
-            box = inboxes[phase]
-            peers = sizes[order[phase]] - 1
-            left = sorted(order[phase + 1 :])
-            if not left:
-                total = full[wave, spot[0], spot[1], spot[2], :, lanes].astype(jnp.float32)
-                for p in range(peers):
-                    total = total + box[wave, order_id, p].astype(jnp.float32)
-                own_grads[wave, :, lanes] = total
-                continue
-            span = math.prod(sizes[a] for a in left)
-
-            def body(step, carry, order_id=order_id, left=left, box=box, peers=peers, lanes=lanes):
-                index = (step,) if len(left) == 1 else (step // sizes[left[1]], step % sizes[left[1]])
-                pick = list(spot)
-                for a, i in zip(left, index):
-                    pick[a] = i
-                total = full[wave, pick[0], pick[1], pick[2], :, lanes].astype(jnp.float32)
-                for p in range(peers):
-                    total = total + box[(wave, order_id, p) + index].astype(jnp.float32)
-                full[wave, pick[0], pick[1], pick[2], :, lanes] = total.astype(low)
-                return carry
-
-            lax.fori_loop(0, span, body, 0)
-
-    def reduce_advance(wave, phase):
-        reduce_absorb(wave, phase - 1)
+    def reduce_send(chunk, phase):
+        for copy in reduce_copies(chunk, phase):
+            copy.start()
+            rs_unsent.append(copy)
+
+    def reduce_absorb(chunk, phase):
+        for copy in reduce_copies(chunk, phase):
+            copy.wait_recv()
+        wave, lanes, order = chunk_place(chunk)
+        order = order[::-1]
+        box = inboxes[phase]
+        peers = sizes[order[phase]] - 1
+        left = sorted(order[phase + 1 :])
+        if not left:
+            total = full[wave, spot[0], spot[1], spot[2], :, lanes].astype(jnp.float32)
+            for p in range(peers):
+                total = total + box[chunk, p].astype(jnp.float32)
+            own_grads[wave, :, lanes] = total
+            return
+        span = math.prod(sizes[a] for a in left)
+
+        def body(step, carry):
+            index = (step,) if len(left) == 1 else (step // sizes[left[1]], step % sizes[left[1]])
+            pick = list(spot)
+            for a, i in zip(left, index):
+                pick[a] = i
+            total = full[wave, pick[0], pick[1], pick[2], :, lanes].astype(jnp.float32)
+            for p in range(peers):
+                total = total + box[(chunk, p) + index].astype(jnp.float32)
+            full[wave, pick[0], pick[1], pick[2], :, lanes] = total.astype(low)
+            return carry
+
+        lax.fori_loop(0, span, body, 0)
+
+    produced = []
+    taken = [0, 0, 0, 0]
+
+    def reduce_advance(phase):
+        chunk = produced[taken[phase]]
+        taken[phase] += 1
+        reduce_absorb(chunk, phase - 1)
         if phase < 3:
-            reduce_send(wave, phase)
+            reduce_send(chunk, phase)
+
+    def reduce_more(lag=1):
+        if taken[3] + LAG <= taken[2]:
+            reduce_advance(3)
+        if taken[2] + LAG <= taken[1]:
+            reduce_advance(2)
+        if taken[1] + lag <= len(produced):
+            reduce_advance(1)
+
+    def reduce_start(chunk):
+        produced.append(chunk)
+        reduce_send(chunk, 0)
+        reduce_more(BURST_LAG)
 
     def spread_copy(buffer, slot, stage, b):
         return pltpu.make_async_remote_copy(
@@ -455,13 +532,19 @@
             device_id_type=MESH_ID,
         )
 
+    pair_unsent = []
+    out_turn = {}
+    out_last = {}
+
     def spread(buffer, slot, stage, b, value):
         buffer[slot, b, mine] = value
-        spread_copy(buffer, slot, stage, b).start()
+        copy = spread_copy(buffer, slot, stage, b)
+        copy.start()
+        pair_unsent.append(copy)
 
     def fold_copy(slot, stage, b):
         return pltpu.make_async_remote_copy(
-            src_ref=outbox.at[slot, b],
+            src_ref=outbox.at[out_turn[slot] % 2, b],
             dst_ref=inbox.at[slot, b],
             send_sem=pair_send.at[stage, b],
             recv_sem=pair_recv.at[stage, b],
@@ -470,18 +553,23 @@
         )
 
     def fold(slot, stage, b, value):
+        turn = out_turn.setdefault(slot, len(out_turn))
         part[b] = value
-        outbox[slot, b] = part[b, theirs].astype(low)
-        fold_copy(slot, stage, b).start()
+        if (turn % 2, b) in out_last:
+            out_last[turn % 2, b].wait_send()
+        outbox[turn % 2, b] = part[b, theirs].astype(low)
+        copy = fold_copy(slot, stage, b)
+        copy.start()
+        out_last[turn % 2, b] = copy
 
     def folded(slot, stage, b):
         fold_copy(slot, stage, b).wait_recv()
         return part[b, mine] + inbox[slot, b].astype(jnp.float32)
 
-    pair_stages = []
-
-    def each_sample(body):
-        lax.fori_loop(0, samples, lambda b, carry: (body(b), carry)[1], 0)
+    def each_sample(body, between=lambda: None):
+        for b in range(samples):
+            body(b)
+            between()
 
     def weight(wave):
         return full[wave].reshape(width, columns)
@@ -489,8 +577,15 @@
     def weight_lanes(wave, lanes, count):
         return full[wave, :, :, :, :, lanes].reshape(width, count)
 
+    def layer_input(layer, b):
+        return hidden_in[b] if layer == 0 else hidden[layer - 1, b]
+
+    vectors = mod_rows.shape[1] // width
+    per_core = vectors // 2
+
     def vec(b, row):
-        return mod[b, row : row + 1]
+        at = b * per_core + row % per_core
+        return mod[row // per_core, at : at + 1]
 
     lane = lax.broadcasted_iota(jnp.int32, (1, 2 * HDIM), 1)
     first_head = lane < HDIM
@@ -503,29 +598,62 @@
     def pair_lanes(kind, p):
         return pl.ds(kind * heads_wide + p * 2 * HDIM, 2 * HDIM)
 
-    gather_step(0)
-    gather_step(1)
-    gather_step(2)
+    gather_more()
+    gather_more()
+
+    for copy in time_copies:
+        copy.wait_recv()
+    for j in range(devices):
+        for b in range(samples):
+            timing_all[b * devices + j : b * devices + j + 1] = timing_box[j, b : b + 1]
+    everyone = samples * devices
+    time_act = timing_all[:, :width]
+    time_act = (time_act * jax.nn.sigmoid(time_act)).astype(low)
+    classes = cond_cols.shape[1] - width
+    label = timing_all[:, width + FREQ : width + FREQ + 1]
+    onehot = lax.broadcasted_iota(jnp.int32, (everyone, classes), 1) == label.astype(jnp.int32)
+    cond = dot(time_act, cond_cols[:, :width], NT) + dot(
+        jnp.where(onehot, 1.0, 0.0).astype(low), cond_cols[:, width:], NT
+    )
+    cond_out[...] = cond
+    cond_act = (cond * jax.nn.sigmoid(cond)).astype(low)
+    for i in range(per_core):
+        lanes = pl.ds(pl.multiple_of((my_core * per_core + i) * width, 128), width)
+        got = dot(cond_act, mod_rows[:, lanes], NN)
+        for j in range(devices):
+            for b in range(samples):
+                at = b * per_core + i
+                mod_part[j, at : at + 1] = got[b * devices + j : b * devices + j + 1]
+    mod_copies = [
+        small(1, i, mod_part.at[peer[0]], mod_box.at[i], peer) for i, peer in enumerate(dp_peers)
+    ]
+    small_start(mod_copies)
+    for _ in range(2 * LAG - 2):
+        gather_more()
+    total_mod = mod_part[my_dp]
+    for i, copy in enumerate(mod_copies):
+        copy.wait_recv()
+        total_mod = total_mod + mod_box[i]
+    mod[my_core] = total_mod
+    mod_pair = small(2, 0, mod.at[my_core], mod.at[my_core], partner)
+    small_start([mod_pair])
+    gather_more()
+    mod_pair.wait_recv()
     for layer in range(layers):
         row = 6 * layer
         sa, sb, sc, sd = (8 * layer + i for i in range(4))
-        pair_stages += [
-            (lambda b, s=sa, g=2 * layer: spread_copy(gathered, g, s, b)),
-            (lambda b, s=sb, g=4 * layer: fold_copy(g, s, b)),
-            (lambda b, s=sc, g=2 * layer + 1: spread_copy(gathered, g, s, b)),
-            (lambda b, s=sd, g=4 * layer + 1: fold_copy(g, s, b)),
-        ]
 
         def first(b):
             if layer == 0:
                 x = hidden_in[b]
             else:
                 x = middle[layer - 1, b] + vec(b, row - 1) * outer[layer - 1, b]
-            hidden[layer, b] = x
+            if layer > 0:
+                hidden[layer - 1, b] = x
             spread(gathered, 2 * layer, sa, b, norm_forward(x, vec(b, row), vec(b, row + 1)))
 
-        each_sample(first)
-        gather_step(3 * layer + 3)
+        each_sample(first, gather_more)
+        gather_until(3 * layer)
 
         def attention(b):
             spread_copy(gathered, 2 * layer, sa, b).wait_recv()
@@ -558,17 +686,17 @@
                 ),
             )
 
-        each_sample(attention)
+        each_sample(attention, gather_more)
 
         def second(b):
             got = folded(4 * layer, sb, b)
             branch[layer, b] = got
-            x = hidden[layer, b] + vec(b, row + 2) * got
+            x = layer_input(layer, b) + vec(b, row + 2) * got
             middle[layer, b] = x
             spread(gathered, 2 * layer + 1, sc, b, norm_forward(x, vec(b, row + 3), vec(b, row + 4)))
 
-        each_sample(second)
-        gather_step(3 * layer + 4)
+        each_sample(second, gather_more)
+        gather_until(3 * layer + 1)
 
         def widen(b):
             spread_copy(gathered, 2 * layer + 1, sc, b).wait_recv()
@@ -583,13 +711,13 @@
 
             lax.fori_loop(0, columns // tile, body, 0)
 
-        each_sample(widen)
-        gather_step(3 * layer + 5)
+        each_sample(widen, gather_more)
+        gather_until(3 * layer + 2)
 
         def narrow(b):
             fold(4 * layer + 1, sd, b, dot(act[b], weight(3 * layer + 2), NT))
 
-        each_sample(narrow)
+        each_sample(narrow, gather_more)
 
         def third(b):
             outer[layer, b] = folded(4 * layer + 1, sd, b)
@@ -600,7 +728,7 @@
         copy.wait_send()
 
     last = layers - 1
-    loss_out[...] = jnp.zeros_like(loss_out)
+    loss_row[...] = jnp.zeros_like(loss_row)
     ends[...] = jnp.zeros_like(ends)
     pad = pl.ds(PATCH, PATCH)
 
@@ -612,9 +740,9 @@
         predicted = dot(head_rows[...], normed, NT)
         error = predicted - velocity[b]
         weighted = time_weight[b] * error
-        loss_out[...] += jnp.sum(weighted * error, axis=0, keepdims=True)
+        loss_row[...] += jnp.sum(weighted * error, axis=0, keepdims=True)
         grad_pred = (2.0 * weighted / total_count).astype(low)
-        ends[pad, :] += dot(grad_pred, normed, NN)
+        ends[pad, :width] += dot(grad_pred, normed, NN)
         dx, gshift, gscale = norm_backward(x, scale, dot(grad_pred, head_rows[...], TN))
         mod_grads[b, 6 * layers : 6 * layers + 1] = gshift
         mod_grads[b, 6 * layers + 1 : 6 * layers + 2] = gscale
@@ -622,42 +750,24 @@
 
     each_sample(head)
 
-    def weight_grad(wave, left, right_of, spans):
+    def weight_grad(wave, left, right_of, first_tile, count):
         turned[...] = left.reshape(samples * tokens, width).T
-
-        def body(n, carry):
-            start, count = spans
-            lanes = pl.ds(pl.multiple_of(start + n * count, 128), count)
-            got = dot(turned[...], right_of(pl.ds(pl.multiple_of(n * count, 128), count), count), NN)
-            full[wave, :, :, :, :, lanes] = got.astype(low).reshape(sizes + (rows, count))
-            return carry
-
-        return body
-
-    started = []
-
-    def pump():
-        for entry in started:
-            if entry[1] <= 3:
-                reduce_advance(entry[0], entry[1])
-                entry[1] += 1
+        for n in range(count):
+            got = dot(turned[...], right_of(pl.ds(n * tile, tile)), NN)
+            lanes = pl.ds((first_tile + n) * tile, tile)
+            full[wave, :, :, :, :, lanes] = got.astype(low).reshape(sizes + (rows, tile))
+            reduce_start(wave * per_wave + first_tile + n)
 
     for layer in reversed(range(layers)):
         row = 6 * layer
         se, sf, sg, sh = (8 * layer + 4 + i for i in range(4))
-        pair_stages += [
-            (lambda b, s=se, g=2 * layer: spread_copy(grad_spread, g, s, b)),
-            (lambda b, s=sf, g=4 * layer + 2: fold_copy(g, s, b)),
-            (lambda b, s=sg, g=2 * layer + 1: spread_copy(grad_spread, g, s, b)),
-            (lambda b, s=sh, g=4 * layer + 3: fold_copy(g, s, b)),
-        ]
 
         def grad_first(b):
             g = resid[b]
             mod_grads[b, row + 5 : row + 6] = jnp.sum(g * outer[layer, b], axis=0, keepdims=True)
             spread(grad_spread, 2 * layer, se, b, (vec(b, row + 5) * g).astype(low))
 
-        each_sample(grad_first)
+        each_sample(grad_first, reduce_more)
 
         def grad_wide(b):
             spread_copy(grad_spread, 2 * layer, se, b).wait_recv()
@@ -683,28 +793,13 @@
             lax.fori_loop(0, columns // tile, body, 0)
             fold(4 * layer + 2, sf, b, dot(grad_inner[b], weight(3 * layer + 1), NT))
 
-        each_sample(grad_wide)
+        each_sample(grad_wide, reduce_more)
 
         def wide_of(source):
-            def right_of(lanes, count):
-                return source[:, :, lanes].reshape(samples * tokens, count)
-
-            return right_of
-
-        lax.fori_loop(
-            0,
-            columns // tile,
-            weight_grad(3 * layer + 2, grad_spread[2 * layer], wide_of(act), (0, tile)),
-            0,
-        )
-        reduce_send(3 * layer + 2, 0)
-        lax.fori_loop(
-            0,
-            columns // tile,
-            weight_grad(3 * layer + 1, gathered[2 * layer + 1], wide_of(grad_inner), (0, tile)),
-            0,
-        )
-        reduce_send(3 * layer + 1, 0)
+            return lambda lanes: source[:, :, lanes].reshape(samples * tokens, tile)
+
+        weight_grad(3 * layer + 2, grad_spread[2 * layer], wide_of(act), 0, per_wave)
+        weight_grad(3 * layer + 1, gathered[2 * layer + 1], wide_of(grad_inner), 0, per_wave)
 
         def grad_second(b):
             dy = folded(4 * layer + 2, sf, b)
@@ -716,10 +811,7 @@
             mod_grads[b, row + 2 : row + 3] = jnp.sum(g * branch[layer, b], axis=0, keepdims=True)
             spread(grad_spread, 2 * layer + 1, sg, b, (vec(b, row + 2) * g).astype(low))
 
-        each_sample(grad_second)
-        pump()
-        started.append([3 * layer + 2, 1])
-        started.append([3 * layer + 1, 1])
+        each_sample(grad_second, reduce_more)
 
         def grad_attention(b):
             spread_copy(grad_spread, 2 * layer + 1, sg, b).wait_recv()
@@ -758,88 +850,163 @@
                 ),
             )
 
-        each_sample(grad_attention)
-        lax.fori_loop(
-            0,
-            3,
-            weight_grad(3 * layer, gathered[2 * layer], wide_of(grad_mixed), (0, heads_wide)),
-            0,
-        )
-        lax.fori_loop(
-            0,
-            1,
-            weight_grad(
-                3 * layer,
-                grad_spread[2 * layer + 1],
-                wide_of(attended.at[layer]),
-                (3 * heads_wide, heads_wide),
-            ),
-            0,
-        )
-        reduce_send(3 * layer, 0)
-        pump()
-        started.append([3 * layer, 1])
+        each_sample(grad_attention, reduce_more)
+        weight_grad(3 * layer, gathered[2 * layer], wide_of(grad_mixed), 0, 3)
+        weight_grad(3 * layer, grad_spread[2 * layer + 1], wide_of(attended.at[layer]), 3, 1)
 
         def grad_third(b):
             dy = folded(4 * layer + 3, sh, b)
-            dx, gshift, gscale = norm_backward(hidden[layer, b], vec(b, row + 1), dy)
+            dx, gshift, gscale = norm_backward(layer_input(layer, b), vec(b, row + 1), dy)
             resid[b] = dx + resid[b]
             mod_grads[b, row : row + 1] = gshift
             mod_grads[b, row + 1 : row + 2] = gscale
 
-        each_sample(grad_third)
+        each_sample(grad_third, reduce_more)
 
     def patch(b):
-        ends[pl.ds(0, PATCH), :] += dot(blended[b], resid[b].astype(low), NN)
+        ends[pl.ds(0, PATCH), :width] += dot(blended[b], resid[b].astype(low), NN)
 
     each_sample(patch)
+    ends[0:1, width:] = loss_row[0:1]
+    for b in range(samples):
+        mod_grads_low[b] = mod_grads[b].astype(low)
+    first_pair = small(2, 1, mod_grads_low.at[1 - my_core], mod_grads_box, partner)
+    ends_pair = small(2, 2, ends, ends_box, partner)
+    small_start([first_pair, ends_pair])
+    reduce_more()
+    first_pair.wait_recv()
+    grad_mods[my_core, my_dp] = (
+        mod_grads_low[my_core].astype(jnp.float32) + mod_grads_box[...].astype(jnp.float32)
+    ).astype(low)
+    share_copies = [
+        small(3, i, grad_mods.at[my_core, my_dp], grad_mods.at[my_core, my_dp], peer)
+        for i, peer in enumerate(dp_peers)
+    ]
+    small_start(share_copies)
     for _ in range(3):
-        pump()
+        reduce_more()
+    for copy in share_copies:
+        copy.wait_recv()
+    share_pair = small(2, 3, grad_mods.at[my_core], grad_mods.at[my_core], partner)
+    small_start([share_pair])
+    reduce_more()
+    share_pair.wait_recv()
+    slots = grad_mods.shape[2]
+    every_row = grad_mods[...].reshape(everyone * slots, width)
+    slot = lax.broadcasted_iota(jnp.int32, (everyone * slots, 1), 0) % slots
+    grad_cond_act = jnp.zeros((everyone * slots, rows), jnp.float32)
+    for i in range(vectors):
+        got = dot(every_row, mod_rows[:, pl.ds(i * width, width)], NT)
+        grad_cond_act = grad_cond_act + jnp.where(slot == i, got, 0.0)
+    grad_cond_act = jnp.sum(grad_cond_act.reshape(everyone, slots, rows), axis=1)
+    reduce_more()
+    cond = cond_out[...]
+    gate = jax.nn.sigmoid(cond)
+    grad_cond = grad_cond_act * gate * (1.0 + cond * (1.0 - gate))
+    grad_cond_out[...] = grad_cond
+    grad_time_act = dot(grad_cond.astype(low), cond_cols[:, :width], NN)
+    ends_pair.wait_recv()
+    ends_sum = ends[...] + ends_box[...]
+    is_first = my_core == 0
+    picked = jnp.where(is_first, ends_sum[:everyone, :width], grad_time_act)
+    extra = jnp.where(is_first, ends_sum[0:1, width:], 0.0)
+    for j in range(devices):
+        for b in range(samples):
+            sum_part[j, b : b + 1, :width] = picked[b * devices + j : b * devices + j + 1]
+            sum_part[j, b : b + 1, width:] = extra
+    sum_copies = [
+        small(4, i, sum_part.at[peer[0]], sum_box.at[i], peer) for i, peer in enumerate(dp_peers)
+    ]
+    small_start(sum_copies)
+    for _ in range(3):
+        reduce_more()
+    total_sum = sum_part[my_dp]
+    for i, copy in enumerate(sum_copies):
+        copy.wait_recv()
+        total_sum = total_sum + sum_box[i]
+    sums[my_core, my_dp] = total_sum
+    back_copies = [
+        small(5, i, sums.at[my_core, my_dp], sums.at[my_core, my_dp], peer)
+        for i, peer in enumerate(dp_peers)
+    ]
+    small_start(back_copies)
+    for _ in range(3):
+        reduce_more()
+    for copy in back_copies:
+        copy.wait_recv()
+    sums_pair = small(2, 4, sums.at[my_core], sums.at[my_core], partner)
+    small_start([sums_pair])
+    while taken[3] < chunks:
+        before = list(taken)
+        reduce_more()
+        if taken == before:
+            for phase in (3, 2):
+                if taken[phase] < taken[phase - 1]:
+                    reduce_advance(phase)
+                    break
+    sums_pair.wait_recv()
+    for copy in small_unsent:
+        copy.wait_send()
     for copy in rs_unsent:
         copy.wait_send()
 
-    def finish(b):
-        for stage in pair_stages:
-            stage(b).wait_send()
-
-    each_sample(finish)
-
-
-def train_step(blob, hidden, mod, velocity, time_weight, blended, head_rows, dp_count, layers, total):
+    for copy in pair_unsent + list(out_last.values()):
+        copy.wait_send()
+
+
+def train_step(
+    blob,
+    hidden,
+    timing,
+    cond_cols,
+    mod_rows,
+    velocity,
+    time_weight,
+    blended,
+    head_rows,
+    dp_count,
+    layers,
+    total,
+):
     sizes = grid_of(dp_count)
     waves, rows, columns = blob.shape
     samples, half_rows, width = hidden.shape
     tokens = 2 * half_rows
-    half = columns // 2
+    tile = columns // 4
+    chunks = 4 * waves
     heads_wide = columns // 4
     most = max(sizes)
+    slots = 16
     low, wide = jnp.bfloat16, jnp.float32
     in_vmem = pl.BlockSpec(memory_space=pltpu.VMEM)
     stages = 8 * layers
     resid_shape = (layers, samples, half_rows, width)
     dma = pltpu.SemaphoreType.DMA
+    everyone = samples * dp_count
     return pl.pallas_call(
         lambda *refs: step_kernel(sizes, layers, total, *refs),
         out_shape=(
             jax.ShapeDtypeStruct((waves, rows, columns), wide),
-            jax.ShapeDtypeStruct(mod.shape, wide),
-            jax.ShapeDtypeStruct((2 * PATCH, width), wide),
-            jax.ShapeDtypeStruct((8, half_rows), wide),
+            jax.ShapeDtypeStruct((everyone, timing.shape[1]), wide),
+            jax.ShapeDtypeStruct((everyone, rows), wide),
+            jax.ShapeDtypeStruct((everyone, rows), wide),
+            jax.ShapeDtypeStruct((2, dp_count, slots, width), low),
+            jax.ShapeDtypeStruct((2, dp_count, samples, width + 128), wide),
         ),
-        in_specs=[pl.BlockSpec(memory_space=pl.ANY)] + [in_vmem] * 6,
-        out_specs=(in_vmem,) * 4,
+        in_specs=[pl.BlockSpec(memory_space=pl.ANY)] + [in_vmem] * 8,
+        out_specs=(in_vmem,) * 6,
         scratch_shapes=[
             pltpu.VMEM((waves,) + sizes + (rows, columns), low),
-            pltpu.VMEM((waves, 2, sizes[2] - 1, sizes[0], sizes[1], rows, half), low),
-            pltpu.VMEM((waves, 2, sizes[1] - 1, sizes[0], rows, half), low),
-            pltpu.VMEM((waves, 2, sizes[0] - 1, rows, half), low),
+            pltpu.VMEM((chunks, sizes[2] - 1, sizes[0], sizes[1], rows, tile), low),
+            pltpu.VMEM((chunks, sizes[1] - 1, sizes[0], rows, tile), low),
+            pltpu.VMEM((chunks, sizes[0] - 1, rows, tile), low),
             pltpu.VMEM((2 * layers, samples, tokens, width), low),
             pltpu.VMEM((2 * layers, samples, tokens, width), low),
-            pltpu.VMEM((4 * layers, samples, half_rows, width), low),
+            pltpu.VMEM((2, samples, half_rows, width), low),
             pltpu.VMEM((4 * layers, samples, half_rows, width), low),
             pltpu.VMEM((layers, samples, tokens, 3 * heads_wide), low),
             pltpu.VMEM((layers, samples, tokens, heads_wide), low),
-            pltpu.VMEM(resid_shape, wide),
+            pltpu.VMEM((max(layers - 1, 1),) + resid_shape[1:], wide),
             pltpu.VMEM(resid_shape, wide),
             pltpu.VMEM(resid_shape, wide),
             pltpu.VMEM(resid_shape, wide),
@@ -850,10 +1017,24 @@
             pltpu.VMEM((samples, half_rows, width), wide),
             pltpu.VMEM((samples, tokens, width), wide),
             pltpu.VMEM((width, samples * tokens), low),
-            dma((waves, 2, 3, most)),
-            dma((waves, 2, 3, most)),
-            dma((waves, 2, 3, most)),
-            dma((waves, 2, 3, most)),
+            pltpu.VMEM((dp_count,) + timing.shape, wide),
+            pltpu.VMEM((dp_count, slots, width), wide),
+            pltpu.VMEM((dp_count - 1, slots, width), wide),
+            pltpu.VMEM((2, slots, width), wide),
+            pltpu.VMEM((samples, slots, width), wide),
+            pltpu.VMEM((samples, slots, width), low),
+            pltpu.VMEM((slots, width), low),
+            pltpu.VMEM((2 * PATCH, width + 128), wide),
+            pltpu.VMEM((8, half_rows), wide),
+            pltpu.VMEM((2 * PATCH, width + 128), wide),
+            pltpu.VMEM((dp_count, samples, width + 128), wide),
+            pltpu.VMEM((dp_count - 1, samples, width + 128), wide),
+            dma((6, max(dp_count, 8))),
+            dma((6, max(dp_count, 8))),
+            dma((chunks, 3, most)),
+            dma((chunks, 3, most)),
+            dma((chunks, 3, most)),
+            dma((chunks, 3, most)),
             dma((stages, samples)),
             dma((stages, samples)),
             dma,
@@ -861,7 +1042,57 @@
         compiler_params=pltpu.CompilerParams(
             collective_id=0, has_side_effects=True, vmem_limit_bytes=64 * 2**20 - 2**17
         ),
-    )(blob, hidden, mod, velocity, time_weight, blended, head_rows)
+    )(blob, hidden, timing, cond_cols, mod_rows, velocity, time_weight, blended, head_rows)
+
+
+def all_peers(dp_count, with_cores):
+    me, core = lax.axis_index("dp"), lax.axis_index("tensor")
+    peers = []
+    for offset in range(1, dp_count):
+        peers.append(((me + offset) % dp_count, core))
+    if with_cores:
+        for offset in range(dp_count):
+            peers.append(((me + offset) % dp_count, 1 - core))
+    return peers
+
+
+def push(source, target, sems, slot, device):
+    return pltpu.make_async_remote_copy(
+        src_ref=source,
+        dst_ref=target,
+        send_sem=sems[0].at[slot],
+        recv_sem=sems[1].at[slot],
+        device_id=device,
+        device_id_type=MESH_ID,
+    )
+
+
+def norm_kernel(dp_count, x, out, box, send, recv):
+    peers = all_peers(dp_count, True)
+    greet(peers)
+    copies = [push(x, box.at[i], (send, recv), i, p) for i, p in enumerate(peers)]
+    for copy in copies:
+        copy.start()
+    total = x[...]
+    for i, copy in enumerate(copies):
+        copy.wait_recv()
+        total = total + box[i]
+    out[...] = total
+    for copy in copies:
+        copy.wait_send()
+
+
+def sum_norms(x, dp_count):
+    dma = pltpu.SemaphoreType.DMA
+    count = 2 * dp_count - 1
+    return pl.pallas_call(
+        lambda *refs: norm_kernel(dp_count, *refs),
+        out_shape=jax.ShapeDtypeStruct(x.shape, x.dtype),
+        in_specs=[pl.BlockSpec(memory_space=pltpu.VMEM)],
+        out_specs=pl.BlockSpec(memory_space=pltpu.VMEM),
+        scratch_shapes=[pltpu.VMEM((count,) + x.shape, x.dtype), dma((count,)), dma((count,))],
+        compiler_params=pltpu.CompilerParams(collective_id=5, has_side_effects=True),
+    )(x)
 
 
 def gather_plain(blob, dp_count):
@@ -929,29 +1160,11 @@
     blob = jnp.stack(parts)
     heads_wide = qkv_w.shape[3]
 
-    ids = lax.all_gather(jnp.stack([time_ids, labels]), "dp", axis=1, tiled=True)
-    all_times, all_labels = ids[0], ids[1]
     small_low = small_w.astype(low)
     patch_rows = small_low[:PATCH]
     time_rows = small_low[PATCH : PATCH + FREQ]
     head_rows = small_low[PATCH + FREQ :]
-    moment_all = (all_times.astype(jnp.float32) + 0.5) / TSTEPS
-    features = time_features(moment_all).astype(low)
-    time_pre = jnp.dot(features, time_rows, preferred_element_type=jnp.float32)
-    time_act = jax.nn.silu(time_pre).astype(low)
-    cond_low = cond_w.astype(low)
     mod_low = mod_w.astype(low)
-    onehot = all_labels[:, None] == jnp.arange(CLASSES)[None, :]
-    cond = jnp.dot(
-        time_act, cond_low[:model_width], preferred_element_type=jnp.float32
-    ) + jnp.dot(onehot.astype(low), cond_low[model_width:], preferred_element_type=jnp.float32)
-    cond_act = jax.nn.silu(cond).astype(low)
-    modulation = lax.psum_scatter(
-        jnp.dot(cond_act, mod_low, preferred_element_type=jnp.float32),
-        "dp",
-        scatter_dimension=0,
-        tiled=True,
-    )
 
     moment = (time_ids.astype(jnp.float32) + 0.5) / TSTEPS
     blended = ((1.0 - moment)[:, None, None] * latents + moment[:, None, None] * gaussian).astype(
@@ -964,12 +1177,24 @@
     )
     time_weight = 0.5 + moment
     total_count = samples * dp_count * half_rows * tensor_count * PATCH
+    features = time_features(moment).astype(low)
+    time_pre = jnp.dot(features, time_rows, preferred_element_type=jnp.float32)
+    timing = jnp.concatenate(
+        [
+            time_pre,
+            features.astype(jnp.float32),
+            jnp.broadcast_to(labels.astype(jnp.float32)[:, None], (samples, 128)),
+        ],
+        axis=1,
+    )
     if kernels:
-        table = modulation.reshape(samples, -1, model_width)
-        own_grads, all_mods, ends, loss_rows = train_step(
+        spare = -cond_w.shape[0] % 128
+        own_grads, timing_all, cond, grad_cond, shared, sums = train_step(
             blob,
             hidden,
-            jnp.pad(table, ((0, 0), (0, 2), (0, 0))),
+            timing,
+            jnp.pad(cond_w.T.astype(low), ((0, 0), (0, spare))),
+            mod_low,
             velocity,
             jnp.broadcast_to(time_weight[:, None, None], velocity.shape),
             blended,
@@ -978,9 +1203,25 @@
             layer_count,
             float(total_count),
         )
-        loss_part = jnp.sum(loss_rows[0])
-        all_mods = all_mods[:, : table.shape[1]].reshape(samples, -1)
+        vectors = 6 * layer_count + 2
+        grad_mods = shared[:, :, :vectors].reshape(samples * dp_count, -1)
+        loss_sum = jnp.sum(sums[0, 0, 0, model_width:])
+        sums = sums.transpose(0, 2, 1, 3)[..., :model_width].reshape(2, -1, model_width)
+        ends, grad_time_act = sums[0], sums[1]
     else:
+        timing_all = lax.all_gather(timing, "dp", axis=1, tiled=False)
+        timing_all = timing_all.reshape(samples * dp_count, -1)
+        time_act = jax.nn.silu(timing_all[:, :model_width]).astype(low)
+        all_labels = timing_all[:, model_width + FREQ].astype(jnp.int32)
+        onehot = (all_labels[:, None] == jnp.arange(CLASSES)[None, :]).astype(low)
+        cond_low = cond_w.astype(low)
+        cond = jnp.dot(
+            time_act, cond_low[:model_width], preferred_element_type=jnp.float32
+        ) + jnp.dot(onehot, cond_low[model_width:], preferred_element_type=jnp.float32)
+        modulation = jnp.dot(
+            jax.nn.silu(cond).astype(low), mod_low, preferred_element_type=jnp.float32
+        ).reshape(samples, dp_count, -1)
+        modulation = lax.psum_scatter(modulation, "dp", scatter_dimension=1, tiled=True)[:, 0]
         full = gather_plain(blob, dp_count)
         saved_list = []
         fetched = []
@@ -1038,30 +1279,35 @@
             + [jnp.stack([grad_fshift, grad_fscale], axis=1).reshape(samples, 2 * model_width)],
             axis=1,
         )
-    grad_mods = lax.all_gather(
-        lax.psum(all_mods.astype(low), "tensor"), "dp", axis=0, tiled=True
-    )
-    grad_cond_act = jnp.einsum("be,de->bd", grad_mods, mod_low, preferred_element_type=jnp.float32)
-    _, silu_back = jax.vjp(jax.nn.silu, cond)
-    grad_cond = silu_back(grad_cond_act)[0]
+        grad_mods = lax.all_gather(lax.psum(all_mods.astype(low), "tensor"), "dp", axis=1)
+        grad_mods = grad_mods.reshape(samples * dp_count, -1)
+        grad_cond_act = jnp.einsum(
+            "be,de->bd", grad_mods, mod_low, preferred_element_type=jnp.float32
+        )
+        _, silu_back = jax.vjp(jax.nn.silu, cond)
+        grad_cond = silu_back(grad_cond_act)[0]
+        grad_time_act = jnp.einsum(
+            "be,de->bd",
+            grad_cond.astype(low),
+            cond_low[:model_width],
+            preferred_element_type=jnp.float32,
+        )
+        ends, grad_time_act, loss_sum = lax.psum(
+            (ends, grad_time_act / tensor_count, loss_part), ("dp", "tensor")
+        )
+    time_pre = timing_all[:, :model_width]
+    features = timing_all[:, model_width : model_width + FREQ].astype(low)
+    all_labels = timing_all[:, model_width + FREQ].astype(jnp.int32)
+    onehot = all_labels[:, None] == jnp.arange(CLASSES)[None, :]
+    time_act = jax.nn.silu(time_pre).astype(low)
+    cond_act = jax.nn.silu(cond).astype(low)
     grad_temb = grad_cond.astype(low)
-    grad_time_act = jnp.einsum(
-        "be,de->bd", grad_temb, cond_low[:model_width], preferred_element_type=jnp.float32
-    )
     grad_mod_w = jnp.einsum("bd,be->de", cond_act, grad_mods, preferred_element_type=jnp.float32)
     grad_table = jnp.einsum(
         "bc,bd->cd", onehot.astype(jnp.float32), grad_cond, precision=HIGHEST_PREC
     )
     grad_time_two = jnp.einsum("bd,be->de", time_act, grad_temb, preferred_element_type=jnp.float32)
     grad_cond_w = jnp.concatenate([grad_time_two, grad_table], axis=0)
-    ends, grad_time_act, loss_sum = lax.psum(
-        (
-            ends,
-            grad_time_act / tensor_count,
-            loss_part,
-        ),
-        ("dp", "tensor"),
-    )
     _, silu_back_two = jax.vjp(jax.nn.silu, time_pre)
     grad_pre = silu_back_two(grad_time_act)[0].astype(low)
     grad_time_one = jnp.einsum("bf,bd->fd", features, grad_pre, preferred_element_type=jnp.float32)
@@ -1097,9 +1343,12 @@
         for i in range(len(weights_list))
     ]
     updates = [r[2] for r in results]
-    total_sq = lax.psum(
-        jnp.stack([squares(weights_list), squares(updates)]), ("dp", "tensor")
-    )
+    total_sq = jnp.stack([squares(weights_list), squares(updates)])
+    if kernels:
+        kinds = total_sq.shape[1]
+        total_sq = sum_norms(jnp.pad(total_sq, ((0, 6), (0, 128 - kinds))), dp_count)[:2, :kinds]
+    else:
+        total_sq = lax.psum(total_sq, ("dp", "tensor"))
     norms = jnp.sqrt(total_sq + EPS_NORM)
     ratio = norms[0] / norms[1]
     outputs = []

time: 737 us -> 438 us (0.59)
  waiting for transfers between devices: 222 us -> 0 us
  blocking collectives: 124 us -> 0 us
  Pallas kernels: 288 us -> 358 us
  between operations: 21.6 us -> 7.21 us
    psum x1 -> x0, waiting for transfers between devices: 113 us -> none  [local(): lax.psum((ends, grad_time_act / tensor_count, loss_part), ('dp', 'tensor'))]
    unnamed x3 -> x0, waiting for transfers between devices: 109 us -> none
    all_gather x2 -> x0, blocking collectives: 71.2 us -> none  [the longest x1 36.6 us: local(): lax.all_gather(lax.psum(all_mods.astype(low), 'tensor'), 'dp', axis=0, ti...]
    pallas_call x1, Pallas kernels: 288 us -> 347 us  [train_step(): pl.pallas_call(lambda *refs: step_kernel(sizes, layers, total, *refs), ou...]
    psum x2 -> x0, blocking collectives: 53.2 us -> none  [the longest x1 41.5 us: local(): lax.psum(jnp.stack([squares(weights_list), squares(updates)]), ('dp', 'te...]
    pallas_call x0 -> x1, Pallas kernels: none -> 11.5 us  [sum_norms(): pl.pallas_call(lambda *refs: norm_kernel(dp_count, *refs), out_shape=jax....]
  transfers between devices with their start and end apart: 2 -> 0, of which waited for: 2 -> 0; matrix products, arithmetic and copies ran while one was open for 3% -> 0% of each run, Pallas kernels for 0% -> 0%
where the time goes in v3:
time: 438 us; the launch traced here: 431 us
  Pallas kernels  358 us (82%)
  other arithmetic  41 us (9%)
  local copies, waits for them, and re-layouts  16.2 us (4%)
  matrix products  8.42 us (2%)
  between operations  7.21 us (2%)
    pallas_call x1, Pallas kernels, train_step(): pl.pallas_call(lambda *refs: step_kernel(sizes, layers, total, *refs), ou...  347 us
    reduce_sum x6, other arithmetic, squares(): sums.append(jnp.sum(a * a, axis=axes).reshape(-1) * shares[kind_id])  14.8 us
    sub x7, other arithmetic, local(): weights_list[kind_id] - LEARN_RATE * factor * updates[kind_id]  12.3 us
    pallas_call x1, Pallas kernels, sum_norms(): pl.pallas_call(lambda *refs: norm_kernel(dp_count, *refs), out_shape=jax....  11.5 us

profile of v3, /device:TPU:1, one launch (start us, length us, event | category | flops | bytes accessed | tf_op | source)
XLA Modules:
  0.0 431.1 jit_solution(17460524566054056076)
XLA Ops:
  6.5 1.0 convert.49
  10.3 1.2 convolution_add_fusion.refs_1_
  15.5 1.1 convert_element_type.126.refs_4_
  16.5 346.8 %shard_map.425 = (f32[6,48,1536]{2,1,0:T(8,128)}, f32[32,1152]{1,0:T(8,128)}, f32[32,48]{1,0:T(8,128)}, f32[32,48]{1,0:T(8,128)}, bf16[2,16,16,768]{3,2,1,0:T(8,128)(2,1)}, /*index=5*/f32[2,16,2,896]{3,2,1,0:T(2,128)}) custom-call(bf16[6,48,1536]{2,1,0:T(8,128)(2,1)} %fusion.9.refs_0_, f32[2,128,768]{2,1,0:T(8,128)} %convolution_add_fusion.refs_1_, ...), custom_call_target="tpu_custom_call" | custom-call | tf_op jit(solution)/shard_map/pallas_call | solution.py:986
  363.4 1.3 slice_reduce_fusion
  364.7 2.2 copy.64
  368.6 1.1 fusion.35
  371.6 1.7 multiply_reduce_fusion.11
  374.9 3.9 multiply_reduce_fusion.3
  382.7 2.0 multiply_reduce_fusion.13
  384.7 3.1 multiply_reduce_fusion.9
  387.8 2.1 multiply_reduce_fusion.6
  389.9 2.0 multiply_reduce_fusion.7
  392.0 6.3 %multiply_reduce_fusion.1 = (f32[]{:T(128)}, f32[]{:T(128)}, f32[48,10752]{1,0:T(8,128)}, f32[48,10752]{1,0:T(8,128)}) fusion(f32[48,10752]{1,0:T(8,128)S(1)} %copy-done.1, f32[48,10752]{1,0:T(8,128)S(1)} %copy-done.36, f32[48,10752]{1,0:T(8,128)} %param.39, bf16[32,10752]{1,0:T(8,128)(2,1)S(1)} %bitcast.111, f32[32,48]{1,0:T(8,128)S(1)} %copy-done.37), kind=kOutput, calls=%fused_computation.6 | convolution fusion | flops 41811456 | bytes 11016200 | tf_op jit(solution)/shard_map/bd,be->de/dot_general | solution.py:1305
  399.6 1.3 concatenate.60
  401.6 1.3 select_maximum_fusion.refs_0_
  402.9 11.5 %shard_map.426 = f32[8,128]{1,0:T(8,128)} custom-call(f32[8,128]{1,0:T(8,128)} %select_maximum_fusion.refs_0_), custom_call_target="tpu_custom_call" | custom-call | tf_op jit(solution)/shard_map/pallas_call | solution.py:1088
  417.9 1.8 multiply_subtract_fusion.6
  419.7 2.1 multiply_subtract_fusion.5
  421.8 2.3 multiply_subtract_fusion.4
  424.1 1.1 multiply_subtract_fusion.2
  425.3 1.2 multiply_subtract_fusion.3
  426.5 1.4 multiply_subtract_fusion.1
  428.5 2.4 multiply_subtract_fusion
  (128 shorter events, 21.9 us)
Async XLA Ops:
  0.7 6.9 %copy-start.4 = (f32[2,1536,48]{1,2,0:T(8,128)S(1)}, f32[2,1536,48]{1,2,0:T(8,128)}, u32[]{:S(2)}) copy-start(f32[2,1536,48]{1,2,0:T(8,128)} %param.49) | copy-start | bytes 1769476
  0.7 6.9 %copy-start.6 = (f32[2,48,1536]{2,1,0:T(8,128)S(1)}, f32[2,48,1536]{2,1,0:T(8,128)}, u32[]{:S(2)}) copy-start(f32[2,48,1536]{2,1,0:T(8,128)} %param.46) | copy-start | bytes 1769476
  3.1 7.1 %copy-start.33 = (bf16[2,16,128]{2,1,0:T(8,128)(2,1)}, bf16[2,16,128]{2,1,0:T(8,128)(2,1)S(1)}, u32[]{:S(2)}) copy-start(bf16[2,16,128]{2,1,0:T(8,128)(2,1)S(1)} %add_convert_fusion.refs_7_) | copy-start | bytes 24580
  3.1 4.5 %copy-start.2 = (f32[288,768]{1,0:T(8,128)S(1)}, f32[288,768]{1,0:T(8,128)}, u32[]{:S(2)}) copy-start(f32[288,768]{1,0:T(8,128)} %param.31) | copy-start | bytes 2654212
  10.1 5.4 %copy-start = (f32[48,10752]{1,0:T(8,128)S(1)}, f32[48,10752]{1,0:T(8,128)}, u32[]{:S(2)}) copy-start(f32[48,10752]{1,0:T(8,128)} %param.37) | copy-start | bytes 6193156
  363.3 7.0 %copy-start.32 = (f32[32,1152]{1,0:T(8,128)S(1)}, f32[32,1152]{1,0:T(8,128)}, u32[]{:S(2)}) copy-start(f32[32,1152]{1,0:T(8,128)} %get-tuple-element.30) | copy-start | bytes 442372
  363.3 7.7 %copy-start.34 = (f32[32,48]{1,0:T(8,128)S(1)}, f32[32,48]{1,0:T(8,128)}, u32[]{:S(2)}) copy-start(f32[32,48]{1,0:T(8,128)} %get-tuple-element.31) | copy-start | bytes 18436
  363.3 8.2 %copy-start.13 = (f32[1769,48]{0,1:T(8,128)S(1)}, f32[1769,48]{0,1:T(8,128)}, u32[]{:S(2)}) copy-start(f32[1769,48]{0,1:T(8,128)} %param.34) | copy-start | bytes 1018948
  363.3 8.2 %copy-start.30 = (f32[1769,48]{0,1:T(8,128)S(1)}, f32[1769,48]{0,1:T(8,128)}, u32[]{:S(2)}) copy-start(f32[1769,48]{0,1:T(8,128)} %param.35) | copy-start | bytes 1018948
  363.4 8.2 %copy-start.31 = (f32[1769,48]{0,1:T(8,128)S(1)}, f32[1769,48]{0,1:T(8,128)}, u32[]{:S(2)}) copy-start(f32[1769,48]{0,1:T(8,128)} %param.36) | copy-start | bytes 1018948
  370.3 4.6 %copy-start.3 = (f32[288,768]{1,0:T(8,128)S(1)}, f32[288,768]{1,0:T(8,128)}, u32[]{:S(2)}) copy-start(f32[288,768]{1,0:T(8,128)} %param.31) | copy-start | bytes 2654212
  370.3 4.6 %copy-start.24 = (f32[288,768]{1,0:T(8,128)S(1)}, f32[288,768]{1,0:T(8,128)}, u32[]{:S(2)}) copy-start(f32[288,768]{1,0:T(8,128)} %param.32) | copy-start | bytes 2654212
  374.9 5.2 %copy-start.20 = (f32[6,48,1536]{2,1,0:T(8,128)S(1)}, f32[6,48,1536]{2,1,0:T(8,128)}, u32[]{:S(2)}) copy-start(f32[6,48,1536]{2,1,0:T(8,128)} %get-tuple-element.34) | copy-start | bytes 5308420
  381.0 3.6 copy-start.9
  382.6 5.2 %copy-start.5 = (f32[2,1536,48]{1,2,0:T(8,128)S(1)}, f32[2,1536,48]{1,2,0:T(8,128)}, u32[]{:S(2)}) copy-start(f32[2,1536,48]{1,2,0:T(8,128)} %param.49) | copy-start | bytes 1769476
  382.6 5.2 %copy-start.26 = (f32[2,1536,48]{1,2,0:T(8,128)S(1)}, f32[2,1536,48]{1,2,0:T(8,128)}, u32[]{:S(2)}) copy-start(f32[2,1536,48]{1,2,0:T(8,128)} %param.50) | copy-start | bytes 1769476
  382.6 5.2 %copy-start.27 = (f32[2,1536,48]{1,2,0:T(8,128)S(1)}, f32[2,1536,48]{1,2,0:T(8,128)}, u32[]{:S(2)}) copy-start(f32[2,1536,48]{1,2,0:T(8,128)} %param.51) | copy-start | bytes 1769476
  384.7 7.3 %copy-start.36 = (f32[48,10752]{1,0:T(8,128)S(1)}, f32[48,10752]{1,0:T(8,128)}, u32[]{:S(2)}) copy-start(f32[48,10752]{1,0:T(8,128)} %param.38) | copy-start | bytes 6193156
  414.4 7.4 %copy-start.10 = (f32[2,48,3,384]{3,1,2,0:T(8,128)S(1)}, f32[2,48,3,384]{3,1,2,0:T(8,128)}, u32[]{:S(2)}) copy-start(f32[2,48,3,384]{3,1,2,0:T(8,128)} %param.40) | copy-start | bytes 1327108
  414.4 9.7 %copy-start.14 = (f32[2,1536,48]{1,2,0:T(8,128)S(1)}, f32[2,1536,48]{1,2,0:T(8,128)}, u32[]{:S(2)}) copy-start(f32[2,1536,48]{1,2,0:T(8,128)} %get-tuple-element.72) | copy-start | bytes 1769476
  414.4 9.7 %copy-start.15 = (f32[2,1536,48]{1,2,0:T(8,128)S(1)}, f32[2,1536,48]{1,2,0:T(8,128)}, u32[]{:S(2)}) copy-start(f32[2,1536,48]{1,2,0:T(8,128)} %get-tuple-element.73) | copy-start | bytes 1769476
  415.3 10.0 %copy-start.35 = (f32[2,11]{1,0:T(2,128)}, f32[2,11]{1,0:T(2,128)S(1)}, u32[]{:S(2)}) copy-start(f32[2,11]{1,0:T(2,128)S(1)} %add_sqrt_fusion) | copy-start | bytes 268
  421.8 3.5 copy-start.16
  421.8 3.5 copy-start.17
  (14 other events, 31.5 us)

commit v4 on v3

--- a/solution.py
+++ b/solution.py
@@ -207,7 +207,6 @@
 
 ORDERS = ((0, 1, 2), (0, 2, 1))
 LAG = 2
-BURST_LAG = 3
 MESH_ID = pl.DeviceIdType.MESH
 NN = (((1,), (0,)), ((), ()))
 NT = (((1,), (1,)), ((), ()))
@@ -283,7 +282,10 @@
 
 def step_kernel(sizes, layers, total_count, *refs):
     (
-        blob,
+        qkv_own,
+        proj_own,
+        up_own,
+        down_own,
         hidden_in,
         timing,
         cond_cols,
@@ -296,8 +298,8 @@
         timing_all,
         cond_out,
         grad_cond_out,
-        grad_mods,
-        sums,
+        grad_mod_out,
+        sums_out,
         full,
         got_one,
         got_two,
@@ -321,6 +323,7 @@
         turned,
         timing_box,
         mod_part,
+        mod_low,
         mod_box,
         mod,
         mod_grads,
@@ -331,6 +334,8 @@
         ends_box,
         sum_part,
         sum_box,
+        grad_mods,
+        sums,
         small_send,
         small_recv,
         ag_send,
@@ -339,13 +344,13 @@
         rs_recv,
         pair_send,
         pair_recv,
-        own_sem,
+        load_sem,
     ) = refs
     low = jnp.bfloat16
     spot = place(sizes)
     my_dp, my_core = lax.axis_index("dp"), lax.axis_index("tensor")
     partner = (my_dp, 1 - my_core)
-    waves, rows, columns = blob.shape
+    waves, rows, columns = 3 * layers, up_own.shape[1], up_own.shape[2]
     samples, half_rows, width = hidden_in.shape
     tokens = 2 * half_rows
     heads_wide = qkv.shape[3] // 3
@@ -356,8 +361,24 @@
     per_wave = columns // tile
     chunks = waves * per_wave
 
-    own = pltpu.make_async_copy(blob, full.at[:, spot[0], spot[1], spot[2]], own_sem)
-    own.start()
+    loads = []
+
+    def load(source, row, start, count, where):
+        copy = pltpu.make_async_copy(
+            source,
+            inner.at[where, pl.ds(row * rows, rows), pl.ds(start, count)],
+            load_sem.at[len(loads)],
+        )
+        copy.start()
+        loads.append(copy)
+
+    narrow_wide = qkv_own.shape[3]
+    for layer in range(layers):
+        for kind in range(3):
+            load(qkv_own.at[layer, kind], layer, kind * narrow_wide, narrow_wide, 1)
+        load(proj_own.at[layer], layer, 3 * narrow_wide, narrow_wide, 1)
+        load(up_own.at[layer], 2 * layer, 0, columns, 0)
+        load(down_own.at[layer], 2 * layer + 1, 0, columns, 0)
     dp_peers = all_peers(sizes[0] * sizes[1] * sizes[2], False)
     greet(dp_peers + [partner])
 
@@ -387,6 +408,14 @@
     small_start(time_copies)
     timing_box[my_dp] = timing[...]
 
+    for copy in loads:
+        copy.wait()
+    for wave in range(waves):
+        layer, which = wave // 3, wave % 3
+        start = layer * rows if which == 0 else (2 * layer + which - 1) * rows
+        got = inner[1 if which == 0 else 0, start : start + rows]
+        full[wave, spot[0], spot[1], spot[2]] = got.astype(low)
+
     unsent = []
 
     def chunk_place(chunk):
@@ -399,10 +428,9 @@
         for earlier in order[:phase]:
             pick[earlier] = slice(None)
         target = full.at[wave, pick[0], pick[1], pick[2], :, lanes]
-        source = blob.at[wave, :, lanes] if phase == 0 else target
         return [
             pltpu.make_async_remote_copy(
-                src_ref=source,
+                src_ref=target,
                 dst_ref=target,
                 send_sem=ag_send.at[chunk, phase, offset],
                 recv_sem=ag_recv.at[chunk, phase, offset],
@@ -424,8 +452,6 @@
             if phase > 0:
                 for copy in gather_copies(chunk, phase - 1):
                     copy.wait_recv()
-            if chunk == 0 and phase == 1:
-                own.wait()
             if phase < 3:
                 for copy in gather_copies(chunk, phase):
                     copy.start()
@@ -500,27 +526,26 @@
         lax.fori_loop(0, span, body, 0)
 
     produced = []
-    taken = [0, 0, 0, 0]
-
-    def reduce_advance(phase):
-        chunk = produced[taken[phase]]
-        taken[phase] += 1
-        reduce_absorb(chunk, phase - 1)
-        if phase < 3:
-            reduce_send(chunk, phase)
-
-    def reduce_more(lag=1):
-        if taken[3] + LAG <= taken[2]:
-            reduce_advance(3)
-        if taken[2] + LAG <= taken[1]:
-            reduce_advance(2)
-        if taken[1] + lag <= len(produced):
-            reduce_advance(1)
-
-    def reduce_start(chunk):
-        produced.append(chunk)
-        reduce_send(chunk, 0)
-        reduce_more(BURST_LAG)
+    reduce_state = [0]
+
+    def reduce_step():
+        step = reduce_state[0]
+        if step >= chunks + 3 * LAG or (step < chunks and step >= len(produced)):
+            return False
+        reduce_state[0] += 1
+        for phase in (3, 2, 1):
+            at = step - phase * LAG
+            if 0 <= at < chunks:
+                reduce_absorb(produced[at], phase - 1)
+                if phase < 3:
+                    reduce_send(produced[at], phase)
+        if step < chunks:
+            reduce_send(produced[step], 0)
+        return True
+
+    def reduce_more(count=1):
+        for _ in range(count):
+            reduce_step()
 
     def spread_copy(buffer, slot, stage, b):
         return pltpu.make_async_remote_copy(
@@ -624,16 +649,20 @@
             for b in range(samples):
                 at = b * per_core + i
                 mod_part[j, at : at + 1] = got[b * devices + j : b * devices + j + 1]
+        if i == per_core // 2:
+            gather_more()
+    gather_more()
+    mod_low[...] = mod_part[...].astype(low)
     mod_copies = [
-        small(1, i, mod_part.at[peer[0]], mod_box.at[i], peer) for i, peer in enumerate(dp_peers)
+        small(1, i, mod_low.at[peer[0]], mod_box.at[i], peer) for i, peer in enumerate(dp_peers)
     ]
     small_start(mod_copies)
-    for _ in range(2 * LAG - 2):
+    for _ in range(4):
         gather_more()
     total_mod = mod_part[my_dp]
     for i, copy in enumerate(mod_copies):
         copy.wait_recv()
-        total_mod = total_mod + mod_box[i]
+        total_mod = total_mod + mod_box[i].astype(jnp.float32)
     mod[my_core] = total_mod
     mod_pair = small(2, 0, mod.at[my_core], mod.at[my_core], partner)
     small_start([mod_pair])
@@ -756,7 +785,9 @@
             got = dot(turned[...], right_of(pl.ds(n * tile, tile)), NN)
             lanes = pl.ds((first_tile + n) * tile, tile)
             full[wave, :, :, :, :, lanes] = got.astype(low).reshape(sizes + (rows, tile))
-            reduce_start(wave * per_wave + first_tile + n)
+            produced.append(wave * per_wave + first_tile + n)
+            if len(produced) <= LAG:
+                reduce_step()
 
     for layer in reversed(range(layers)):
         row = 6 * layer
@@ -767,7 +798,7 @@
             mod_grads[b, row + 5 : row + 6] = jnp.sum(g * outer[layer, b], axis=0, keepdims=True)
             spread(grad_spread, 2 * layer, se, b, (vec(b, row + 5) * g).astype(low))
 
-        each_sample(grad_first, reduce_more)
+        each_sample(grad_first)
 
         def grad_wide(b):
             spread_copy(grad_spread, 2 * layer, se, b).wait_recv()
@@ -799,7 +830,9 @@
             return lambda lanes: source[:, :, lanes].reshape(samples * tokens, tile)
 
         weight_grad(3 * layer + 2, grad_spread[2 * layer], wide_of(act), 0, per_wave)
+        reduce_more()
         weight_grad(3 * layer + 1, gathered[2 * layer + 1], wide_of(grad_inner), 0, per_wave)
+        reduce_more()
 
         def grad_second(b):
             dy = folded(4 * layer + 2, sf, b)
@@ -811,7 +844,7 @@
             mod_grads[b, row + 2 : row + 3] = jnp.sum(g * branch[layer, b], axis=0, keepdims=True)
             spread(grad_spread, 2 * layer + 1, sg, b, (vec(b, row + 2) * g).astype(low))
 
-        each_sample(grad_second, reduce_more)
+        each_sample(grad_second)
 
         def grad_attention(b):
             spread_copy(grad_spread, 2 * layer + 1, sg, b).wait_recv()
@@ -861,7 +894,8 @@
             mod_grads[b, row : row + 1] = gshift
             mod_grads[b, row + 1 : row + 2] = gscale
 
-        each_sample(grad_third, reduce_more)
+        reduce_more()
+        each_sample(grad_third)
 
     def patch(b):
         ends[pl.ds(0, PATCH), :width] += dot(blended[b], resid[b].astype(low), NN)
@@ -883,8 +917,7 @@
         for i, peer in enumerate(dp_peers)
     ]
     small_start(share_copies)
-    for _ in range(3):
-        reduce_more()
+    reduce_more(2)
     for copy in share_copies:
         copy.wait_recv()
     share_pair = small(2, 3, grad_mods.at[my_core], grad_mods.at[my_core], partner)
@@ -918,8 +951,7 @@
         small(4, i, sum_part.at[peer[0]], sum_box.at[i], peer) for i, peer in enumerate(dp_peers)
     ]
     small_start(sum_copies)
-    for _ in range(3):
-        reduce_more()
+    reduce_more(2)
     total_sum = sum_part[my_dp]
     for i, copy in enumerate(sum_copies):
         copy.wait_recv()
@@ -930,21 +962,41 @@
         for i, peer in enumerate(dp_peers)
     ]
     small_start(back_copies)
-    for _ in range(3):
-        reduce_more()
+    reduce_more(2)
     for copy in back_copies:
         copy.wait_recv()
     sums_pair = small(2, 4, sums.at[my_core], sums.at[my_core], partner)
     small_start([sums_pair])
-    while taken[3] < chunks:
-        before = list(taken)
-        reduce_more()
-        if taken == before:
-            for phase in (3, 2):
-                if taken[phase] < taken[phase - 1]:
-                    reduce_advance(phase)
-                    break
+    spread_act = jnp.broadcast_to(
+        (cond * gate)[:, None, :], (everyone, slots, rows)
+    ).reshape(everyone * slots, rows)
+    stores = []
+    per_line = columns // width
+    for i in range(vectors):
+        left = jnp.where(slot == i, spread_act, 0.0).astype(low)
+        line, at = i // per_line, i % per_line * width
+        where, start = line % 2, line // 2 * rows
+        inner[where, start : start + rows, at : at + width] = dot(left, every_row, TN)
+    for line in range(vectors // per_line):
+        where, start = line % 2, line // 2 * rows
+        copy = pltpu.make_async_copy(
+            inner.at[where, pl.ds(start, rows)],
+            grad_mod_out.at[:, pl.ds(line * columns, columns)],
+            load_sem.at[line],
+        )
+        copy.start()
+        stores.append(copy)
+    reduce_more(2)
     sums_pair.wait_recv()
+    for core in range(2):
+        for j in range(devices):
+            for b in range(samples):
+                at = b * devices + j
+                sums_out[core, at : at + 1] = sums[core, j, b : b + 1]
+    while reduce_step():
+        pass
+    for copy in stores:
+        copy.wait()
     for copy in small_unsent:
         copy.wait_send()
     for copy in rs_unsent:
@@ -955,7 +1007,7 @@
 
 
 def train_step(
-    blob,
+    own_weights,
     hidden,
     timing,
     cond_cols,
@@ -969,7 +1021,8 @@
     total,
 ):
     sizes = grid_of(dp_count)
-    waves, rows, columns = blob.shape
+    rows, columns = own_weights[2].shape[1:]
+    waves = 3 * layers
     samples, half_rows, width = hidden.shape
     tokens = 2 * half_rows
     tile = columns // 4
@@ -979,6 +1032,7 @@
     slots = 16
     low, wide = jnp.bfloat16, jnp.float32
     in_vmem = pl.BlockSpec(memory_space=pltpu.VMEM)
+    in_hbm = pl.BlockSpec(memory_space=pl.ANY)
     stages = 8 * layers
     resid_shape = (layers, samples, half_rows, width)
     dma = pltpu.SemaphoreType.DMA
@@ -990,11 +1044,11 @@
             jax.ShapeDtypeStruct((everyone, timing.shape[1]), wide),
             jax.ShapeDtypeStruct((everyone, rows), wide),
             jax.ShapeDtypeStruct((everyone, rows), wide),
-            jax.ShapeDtypeStruct((2, dp_count, slots, width), low),
-            jax.ShapeDtypeStruct((2, dp_count, samples, width + 128), wide),
+            jax.ShapeDtypeStruct((rows, mod_rows.shape[1]), wide),
+            jax.ShapeDtypeStruct((2, everyone, width + 128), wide),
         ),
-        in_specs=[pl.BlockSpec(memory_space=pl.ANY)] + [in_vmem] * 8,
-        out_specs=(in_vmem,) * 6,
+        in_specs=[in_hbm] * 4 + [in_vmem] * 8,
+        out_specs=(in_vmem,) * 4 + (in_hbm, in_vmem),
         scratch_shapes=[
             pltpu.VMEM((waves,) + sizes + (rows, columns), low),
             pltpu.VMEM((chunks, sizes[2] - 1, sizes[0], sizes[1], rows, tile), low),
@@ -1019,7 +1073,8 @@
             pltpu.VMEM((width, samples * tokens), low),
             pltpu.VMEM((dp_count,) + timing.shape, wide),
             pltpu.VMEM((dp_count, slots, width), wide),
-            pltpu.VMEM((dp_count - 1, slots, width), wide),
+            pltpu.VMEM((dp_count, slots, width), low),
+            pltpu.VMEM((dp_count - 1, slots, width), low),
             pltpu.VMEM((2, slots, width), wide),
             pltpu.VMEM((samples, slots, width), wide),
             pltpu.VMEM((samples, slots, width), low),
@@ -1029,6 +1084,8 @@
             pltpu.VMEM((2 * PATCH, width + 128), wide),
             pltpu.VMEM((dp_count, samples, width + 128), wide),
             pltpu.VMEM((dp_count - 1, samples, width + 128), wide),
+            pltpu.VMEM((2, dp_count, slots, width), low),
+            pltpu.VMEM((2, dp_count, samples, width + 128), wide),
             dma((6, max(dp_count, 8))),
             dma((6, max(dp_count, 8))),
             dma((chunks, 3, most)),
@@ -1037,12 +1094,22 @@
             dma((chunks, 3, most)),
             dma((stages, samples)),
             dma((stages, samples)),
-            dma,
+            dma((6 * layers,)),
         ],
         compiler_params=pltpu.CompilerParams(
             collective_id=0, has_side_effects=True, vmem_limit_bytes=64 * 2**20 - 2**17
         ),
-    )(blob, hidden, timing, cond_cols, mod_rows, velocity, time_weight, blended, head_rows)
+    )(
+        *own_weights,
+        hidden,
+        timing,
+        cond_cols,
+        mod_rows,
+        velocity,
+        time_weight,
+        blended,
+        head_rows,
+    )
 
 
 def all_peers(dp_count, with_cores):
@@ -1144,20 +1211,10 @@
     samples = latents.shape[0]
     half_rows = latents.shape[2]
     rows = qkv_w.shape[1]
-    kernels = rows % 16 == 0
+    kernels = rows % 16 == 0 and 2 * layer_count * rows <= 2 * half_rows
     my_dp = lax.axis_index("dp")
     low = jnp.bfloat16
 
-    parts = []
-    for i in range(layer_count):
-        parts.append(
-            jnp.concatenate(
-                [qkv_w[i, :, 0], qkv_w[i, :, 1], qkv_w[i, :, 2], proj_w[i].T], axis=1
-            ).astype(low)
-        )
-        parts.append(up_w[i].astype(low))
-        parts.append(down_w[i].T.astype(low))
-    blob = jnp.stack(parts)
     heads_wide = qkv_w.shape[3]
 
     small_low = small_w.astype(low)
@@ -1189,8 +1246,13 @@
     )
     if kernels:
         spare = -cond_w.shape[0] % 128
-        own_grads, timing_all, cond, grad_cond, shared, sums = train_step(
-            blob,
+        own_grads, timing_all, cond, grad_cond, grad_mod_w, sums = train_step(
+            (
+                qkv_w.transpose(0, 2, 1, 3),
+                proj_w.transpose(0, 2, 1),
+                up_w,
+                down_w.transpose(0, 2, 1),
+            ),
             hidden,
             timing,
             jnp.pad(cond_w.T.astype(low), ((0, 0), (0, spare))),
@@ -1203,11 +1265,8 @@
             layer_count,
             float(total_count),
         )
-        vectors = 6 * layer_count + 2
-        grad_mods = shared[:, :, :vectors].reshape(samples * dp_count, -1)
-        loss_sum = jnp.sum(sums[0, 0, 0, model_width:])
-        sums = sums.transpose(0, 2, 1, 3)[..., :model_width].reshape(2, -1, model_width)
-        ends, grad_time_act = sums[0], sums[1]
+        loss_sum = jnp.sum(sums[0, 0, model_width:])
+        ends, grad_time_act = sums[0, :, :model_width], sums[1, :, :model_width]
     else:
         timing_all = lax.all_gather(timing, "dp", axis=1, tiled=False)
         timing_all = timing_all.reshape(samples * dp_count, -1)
@@ -1222,6 +1281,16 @@
             jax.nn.silu(cond).astype(low), mod_low, preferred_element_type=jnp.float32
         ).reshape(samples, dp_count, -1)
         modulation = lax.psum_scatter(modulation, "dp", scatter_dimension=1, tiled=True)[:, 0]
+        parts = []
+        for i in range(layer_count):
+            parts.append(
+                jnp.concatenate(
+                    [qkv_w[i, :, 0], qkv_w[i, :, 1], qkv_w[i, :, 2], proj_w[i].T], axis=1
+                ).astype(low)
+            )
+            parts.append(up_w[i].astype(low))
+            parts.append(down_w[i].T.astype(low))
+        blob = jnp.stack(parts)
         full = gather_plain(blob, dp_count)
         saved_list = []
         fetched = []
@@ -1284,7 +1353,10 @@
         grad_cond_act = jnp.einsum(
             "be,de->bd", grad_mods, mod_low, preferred_element_type=jnp.float32
         )
-        _, silu_back = jax.vjp(jax.nn.silu, cond)
+        cond_act, silu_back = jax.vjp(jax.nn.silu, cond)
+        grad_mod_w = jnp.einsum(
+            "bd,be->de", cond_act.astype(low), grad_mods, preferred_element_type=jnp.float32
+        )
         grad_cond = silu_back(grad_cond_act)[0]
         grad_time_act = jnp.einsum(
             "be,de->bd",
@@ -1300,9 +1372,7 @@
     all_labels = timing_all[:, model_width + FREQ].astype(jnp.int32)
     onehot = all_labels[:, None] == jnp.arange(CLASSES)[None, :]
     time_act = jax.nn.silu(time_pre).astype(low)
-    cond_act = jax.nn.silu(cond).astype(low)
     grad_temb = grad_cond.astype(low)
-    grad_mod_w = jnp.einsum("bd,be->de", cond_act, grad_mods, preferred_element_type=jnp.float32)
     grad_table = jnp.einsum(
         "bc,bd->cd", onehot.astype(jnp.float32), grad_cond, precision=HIGHEST_PREC
     )

time: 438 us -> 383 us (0.87)
  Pallas kernels: 358 us -> 309 us
  local copies, waits for them, and re-layouts: 16.2 us -> 8.85 us
  other arithmetic: 41 us -> 47 us
    pallas_call x1, Pallas kernels: 347 us -> 297 us  [train_step(): pl.pallas_call(lambda *refs: step_kernel(sizes, layers, total, *refs), ou...]
    reduce_sum x6 -> x7, other arithmetic: 14.8 us -> 23 us  [squares(): sums.append(jnp.sum(a * a, axis=axes).reshape(-1) * shares[kind_id])]
    dot_general x1 -> x0, matrix products: 6.28 us -> none  [local(): jnp.einsum('bd,be->de', cond_act, grad_mods, preferred_element_type=jnp.f...]
    unnamed x83 -> x59, local copies, waits for them, and re-layouts: 6.38 us -> 0.83 us
where the time goes in v4:
time: 383 us; the launch traced here: 376 us
  Pallas kernels  309 us (81%)
  other arithmetic  47 us (12%)
  local copies, waits for them, and re-layouts  8.85 us (2%)
  between operations  7.28 us (2%)
  matrix products  4.64 us (1%)
    pallas_call x1, Pallas kernels, train_step(): pl.pallas_call(lambda *refs: step_kernel(sizes, layers, total, *refs), ou...  297 us
    reduce_sum x7, other arithmetic, squares(): sums.append(jnp.sum(a * a, axis=axes).reshape(-1) * shares[kind_id])  23 us
    sub x7, other arithmetic, local(): weights_list[kind_id] - LEARN_RATE * factor * updates[kind_id]  12.2 us
    pallas_call x1, Pallas kernels, sum_norms(): pl.pallas_call(lambda *refs: norm_kernel(dp_count, *refs), out_shape=jax....  11.4 us

profile of v4, /device:TPU:1, one launch (start us, length us, event | category | flops | bytes accessed | tf_op | source)
XLA Modules:
  0.0 376.4 jit_solution(2320574009798293985)
XLA Ops:
  5.4 1.4 convert_element_type.76
  9.3 1.2 convolution_add_fusion.refs_4_
  10.5 1.1 convert_element_type.85.refs_7_
  11.6 297.2 %shard_map.425 = (f32[6,48,1536]{2,1,0:T(8,128)}, f32[32,1152]{1,0:T(8,128)}, f32[32,48]{1,0:T(8,128)}, f32[32,48]{1,0:T(8,128)}, f32[48,10752]{1,0:T(8,128)}, /*index=5*/f32[2,32,896]{2,1,0:T(8,128)}) custom-call(f32[2,3,48,384]{3,2,1,0:T(8,128)} %bitcast.66, f32[2,48,384]{2,1,0:T(8,128)} %bitcast.67, f32[2,48,1536]{2,1,0:T(8,128)} %refs_2_.1, ...), custom_call_target="tpu_custom_call" | custom-call | tf_op jit(solution)/shard_map/pallas_call | solution.py:1040
  308.8 1.4 slice_reduce_fusion
  311.8 1.1 fusion.17
  314.0 2.9 multiply_reduce_fusion.11
  318.2 1.2 fusion.14
  319.4 4.1 %multiply_reduce_fusion.3 = (f32[]{:T(128)}, f32[]{:T(128)}, f32[288,768]{1,0:T(8,128)}, f32[288,768]{1,0:T(8,128)}) fusion(f32[288,768]{1,0:T(8,128)S(1)} %copy-done.4, f32[16,768]{1,0:T(8,128)S(1)} %get-tuple-element.91, f32[256,768]{1,0:T(8,128)S(1)} %fusion.14, f32[16,768]{1,0:T(8,128)S(1)} %get-tuple-element.90, f32[288,768]{1,0:T(8,128)} %param.32, ...), kind=kLoop, calls=%fused_computation.15 | loop fusion | flops 4202494 | bytes 5308424 | tf_op jit(solution)/shard_map/reduce_sum | solution.py:1408
  327.5 2.0 multiply_reduce_fusion.13
  329.5 3.1 multiply_reduce_fusion.9
  332.6 3.2 multiply_reduce_fusion.6
  335.9 3.4 multiply_reduce_fusion.7
  339.3 4.2 %multiply_reduce_fusion.1 = (f32[]{:T(128)}, f32[]{:T(128)}, f32[48,10752]{1,0:T(8,128)}, f32[48,10752]{1,0:T(8,128)}) fusion(f32[48,10752]{1,0:T(8,128)S(1)} %copy-done.1, f32[48,10752]{1,0:T(8,128)S(1)} %copy-done.18, f32[48,10752]{1,0:T(8,128)S(1)} %copy-done.16, f32[48,10752]{1,0:T(8,128)S(1)} %copy-done.17), kind=kLoop, calls=%fused_computation.6 | loop fusion | flops 8773630 | bytes 12386312 | tf_op jit(solution)/shard_map/reduce_sum | solution.py:1408
  344.9 1.3 concatenate.22
  346.9 1.3 select_maximum_fusion.refs_0_
  348.1 11.4 %shard_map.426 = f32[8,128]{1,0:T(8,128)} custom-call(f32[8,128]{1,0:T(8,128)} %select_maximum_fusion.refs_0_), custom_call_target="tpu_custom_call" | custom-call | tf_op jit(solution)/shard_map/pallas_call | solution.py:1155
  363.0 1.8 multiply_subtract_fusion.6
  364.8 2.1 multiply_subtract_fusion.5
  366.9 2.3 multiply_subtract_fusion.4
  369.3 1.1 multiply_subtract_fusion.2
  370.4 1.1 multiply_subtract_fusion.3
  371.6 1.4 multiply_subtract_fusion.1
  373.6 2.4 multiply_subtract_fusion
  (92 shorter events, 15.5 us)
Async XLA Ops:
  3.0 7.5 %copy-start.27 = (bf16[2,16,128]{2,1,0:T(8,128)(2,1)}, bf16[2,16,128]{2,1,0:T(8,128)(2,1)S(1)}, u32[]{:S(2)}) copy-start(bf16[2,16,128]{2,1,0:T(8,128)(2,1)S(1)} %add_convert_fusion.refs_10_) | copy-start | bytes 24580
  5.4 5.1 %copy-start = (f32[48,10752]{1,0:T(8,128)S(1)}, f32[48,10752]{1,0:T(8,128)}, u32[]{:S(2)}) copy-start(f32[48,10752]{1,0:T(8,128)} %param.37) | copy-start | bytes 6193156
  308.8 9.4 %copy-start.26 = (f32[32,1152]{1,0:T(8,128)S(1)}, f32[32,1152]{1,0:T(8,128)}, u32[]{:S(2)}) copy-start(f32[32,1152]{1,0:T(8,128)} %get-tuple-element.29) | copy-start | bytes 442372
  308.8 10.6 %copy-start.4 = (f32[288,768]{1,0:T(8,128)S(1)}, f32[288,768]{1,0:T(8,128)}, u32[]{:S(2)}) copy-start(f32[288,768]{1,0:T(8,128)} %param.31) | copy-start | bytes 2654212
  319.4 5.4 %copy-start.19 = (f32[6,48,1536]{2,1,0:T(8,128)S(1)}, f32[6,48,1536]{2,1,0:T(8,128)}, u32[]{:S(2)}) copy-start(f32[6,48,1536]{2,1,0:T(8,128)} %get-tuple-element.32) | copy-start | bytes 5308420
  325.9 3.6 copy-start.8
  327.4 5.2 %copy-start.25 = (f32[2,1536,48]{1,2,0:T(8,128)S(1)}, f32[2,1536,48]{1,2,0:T(8,128)}, u32[]{:S(2)}) copy-start(f32[2,1536,48]{1,2,0:T(8,128)} %param.50) | copy-start | bytes 1769476
  327.4 5.2 %copy-start.5 = (f32[2,1536,48]{1,2,0:T(8,128)S(1)}, f32[2,1536,48]{1,2,0:T(8,128)}, u32[]{:S(2)}) copy-start(f32[2,1536,48]{1,2,0:T(8,128)} %param.49) | copy-start | bytes 1769476
  327.4 5.2 %copy-start.23 = (f32[1,1536,48]{1,2,0:T(8,128)S(1)}, f32[1,1536,48]{1,2,0:T(8,128)}, u32[]{:S(2)}) copy-start(f32[1,1536,48]{1,2,0:T(8,128)} %get-tuple-element.84) | copy-start | bytes 884740
  327.4 5.2 %copy-start.24 = (f32[1,1536,48]{1,2,0:T(8,128)S(1)}, f32[1,1536,48]{1,2,0:T(8,128)}, u32[]{:S(2)}) copy-start(f32[1,1536,48]{1,2,0:T(8,128)} %get-tuple-element.85) | copy-start | bytes 884740
  329.5 6.4 %copy-start.22 = (f32[1,48,1536]{2,1,0:T(8,128)S(1)}, f32[1,48,1536]{2,1,0:T(8,128)}, u32[]{:S(2)}) copy-start(f32[1,48,1536]{2,1,0:T(8,128)} %get-tuple-element.87) | copy-start | bytes 884740
  329.5 9.8 %copy-start.18 = (f32[48,10752]{1,0:T(8,128)S(1)}, f32[48,10752]{1,0:T(8,128)}, u32[]{:S(2)}) copy-start(f32[48,10752]{1,0:T(8,128)} %get-tuple-element.31) | copy-start | bytes 6193156
  332.6 3.3 copy-start.6
  332.6 3.3 copy-start.21
  332.6 6.7 %copy-start.16 = (f32[48,10752]{1,0:T(8,128)S(1)}, f32[48,10752]{1,0:T(8,128)}, u32[]{:S(2)}) copy-start(f32[48,10752]{1,0:T(8,128)} %param.38) | copy-start | bytes 6193156
  332.6 6.7 %copy-start.17 = (f32[48,10752]{1,0:T(8,128)S(1)}, f32[48,10752]{1,0:T(8,128)}, u32[]{:S(2)}) copy-start(f32[48,10752]{1,0:T(8,128)} %param.39) | copy-start | bytes 6193156
  335.9 3.4 copy-start.1
  359.5 7.4 %copy-start.9 = (f32[2,48,3,384]{3,1,2,0:T(8,128)S(1)}, f32[2,48,3,384]{3,1,2,0:T(8,128)}, u32[]{:S(2)}) copy-start(f32[2,48,3,384]{3,1,2,0:T(8,128)} %param.40) | copy-start | bytes 1327108
  359.5 9.7 %copy-start.12 = (f32[2,1536,48]{1,2,0:T(8,128)S(1)}, f32[2,1536,48]{1,2,0:T(8,128)}, u32[]{:S(2)}) copy-start(f32[2,1536,48]{1,2,0:T(8,128)} %get-tuple-element.70) | copy-start | bytes 1769476
  359.6 9.7 %copy-start.13 = (f32[2,1536,48]{1,2,0:T(8,128)S(1)}, f32[2,1536,48]{1,2,0:T(8,128)}, u32[]{:S(2)}) copy-start(f32[2,1536,48]{1,2,0:T(8,128)} %get-tuple-element.71) | copy-start | bytes 1769476
  360.4 10.0 %copy-start.28 = (f32[2,11]{1,0:T(2,128)}, f32[2,11]{1,0:T(2,128)S(1)}, u32[]{:S(2)}) copy-start(f32[2,11]{1,0:T(2,128)S(1)} %add_sqrt_fusion) | copy-start | bytes 268
  366.9 3.5 copy-start.7
  366.9 3.5 copy-start.14
  366.9 3.5 copy-start.15
  (5 other events, 10.9 us)

commit v5 on v4

--- a/solution.py
+++ b/solution.py
@@ -1176,6 +1176,204 @@
     )
 
 
+KINDS = 7
+
+
+def pieces_of(kind, shape, layers):
+    if kind == 0:
+        return [((pl.ds(r, 48), slice(None)), 0) for r in range(0, shape[0], 48)]
+    if kind == 1:
+        split = [0] + list(range(768, shape[1], 512)) + [shape[1]]
+        return [((slice(None), pl.ds(a, b - a)), 1) for a, b in zip(split, split[1:])]
+    if kind == 2:
+        return [((slice(None), pl.ds(c, 768)), 2) for c in range(0, shape[1], 768)]
+    found = []
+    for layer in range(layers):
+        column = 3 + (kind - 3) * layers + layer
+        if kind == 3:
+            found += [((layer, part), column) for part in range(3)]
+        else:
+            found.append(((layer,), column))
+    return found
+
+
+def lamb_kernel(layers, shares, *refs):
+    weights, firsts, seconds = refs[:7], refs[7:14], refs[14:21]
+    own_grads, grad_mod, timing_all, grad_cond, sums = refs[21:26]
+    first_out, second_out, update_out = refs[26:33], refs[33:40], refs[40:47]
+    norms_out = refs[47]
+    w_buf, m_buf, v_buf = refs[48:55], refs[55:62], refs[62:69]
+    block_grads, mod_buf, small_buf, cond_buf, in_sem, out_sem, grad_sem = refs[69:]
+    low = jnp.bfloat16
+    width = small_buf.shape[1]
+    heads_wide = w_buf[3].shape[3]
+    sequence = (5, 6, 3, 4, 2, 1, 0)
+    loads = {}
+    block_load = pltpu.make_async_copy(own_grads, block_grads, grad_sem.at[0])
+    block_load.start()
+    mod_load = pltpu.make_async_copy(grad_mod, mod_buf, grad_sem.at[1])
+    for kind in sequence:
+        loads[kind] = [
+            pltpu.make_async_copy(source[kind], target[kind], in_sem.at[kind, i])
+            for i, (source, target) in enumerate(
+                ((weights, w_buf), (firsts, m_buf), (seconds, v_buf))
+            )
+        ]
+        for copy in loads[kind]:
+            copy.start()
+        if kind == 2:
+            mod_load.start()
+
+    time_pre = timing_all[:, :width]
+    gate = jax.nn.sigmoid(time_pre)
+    time_act = (time_pre * gate).astype(low)
+    grad_time_act = sums[1, :, :width]
+    grad_pre = (grad_time_act * gate * (1.0 + time_pre * (1.0 - gate))).astype(low)
+    small_buf[:PATCH] = sums[0, :PATCH, :width]
+    small_buf[PATCH : PATCH + FREQ] = dot(
+        timing_all[:, width : width + FREQ].astype(low), grad_pre, TN
+    )
+    small_buf[PATCH + FREQ :] = sums[0, PATCH:, :width]
+    label = timing_all[:, width + FREQ : width + FREQ + 1].astype(jnp.int32)
+    classes = cond_buf.shape[1] - width
+    onehot = lax.broadcasted_iota(jnp.int32, (timing_all.shape[0], classes), 1) == label
+    cond_buf[:, :width] = dot(grad_cond[...].astype(low), time_act, TN)
+    cond_buf[:, width:] = lax.dot_general(
+        grad_cond[...],
+        jnp.where(onehot, 1.0, 0.0),
+        TN,
+        precision=HIGHEST_PREC,
+        preferred_element_type=jnp.float32,
+    )
+
+    def gradient(kind, index):
+        if kind < 3:
+            return (small_buf, cond_buf, mod_buf)[kind][index]
+        layer = index[0]
+        if kind == 3:
+            return block_grads[3 * layer, :, pl.ds(index[1] * heads_wide, heads_wide)]
+        if kind == 4:
+            return block_grads[3 * layer, :, pl.ds(3 * heads_wide, heads_wide)]
+        return block_grads[3 * layer + kind - 4]
+
+    lane = lax.broadcasted_iota(jnp.int32, (1, 128), 1)
+    norm_rows = [jnp.zeros((1, 128), jnp.float32), jnp.zeros((1, 128), jnp.float32)]
+    stores = []
+    block_load.wait()
+    for kind in sequence:
+        for copy in loads[kind]:
+            copy.wait()
+        if kind == 2:
+            mod_load.wait()
+        share = shares[kind]
+        for index, column in pieces_of(kind, w_buf[kind].shape, layers):
+            g = gradient(kind, index)
+            weight = w_buf[kind][index]
+            first, second, update = lamb_parts(weight, m_buf[kind][index], v_buf[kind][index], g)
+            m_buf[kind][index] = first
+            v_buf[kind][index] = second
+            w_buf[kind][index] = update
+            for row, value in enumerate((weight, update)):
+                norm_rows[row] = norm_rows[row] + jnp.where(
+                    lane == column, share * jnp.sum(value * value), 0.0
+                )
+        for i, (source, target) in enumerate(
+            ((m_buf, first_out), (v_buf, second_out), (w_buf, update_out))
+        ):
+            copy = pltpu.make_async_copy(source[kind], target[kind], out_sem.at[kind, i])
+            copy.start()
+            stores.append(copy)
+    norms_out[...] = jnp.zeros_like(norms_out)
+    norms_out[0:1] = norm_rows[0]
+    norms_out[1:2] = norm_rows[1]
+    for copy in stores:
+        copy.wait()
+
+
+def lamb_first(weights, firsts, seconds, own_grads, grad_mod, timing_all, grad_cond, sums, shares):
+    layers = weights[3].shape[0]
+    in_hbm = pl.BlockSpec(memory_space=pl.ANY)
+    in_vmem = pl.BlockSpec(memory_space=pltpu.VMEM)
+    wide = jnp.float32
+    like = [jax.ShapeDtypeStruct(w.shape, wide) for w in weights]
+    held = [pltpu.VMEM(w.shape, wide) for w in weights]
+    dma = pltpu.SemaphoreType.DMA
+    out = pl.pallas_call(
+        lambda *refs: lamb_kernel(layers, shares, *refs),
+        out_shape=tuple(like * 3 + [jax.ShapeDtypeStruct((8, 128), wide)]),
+        in_specs=[in_hbm] * 23 + [in_vmem] * 3,
+        out_specs=tuple([in_hbm] * 21 + [in_vmem]),
+        scratch_shapes=held * 3
+        + [
+            pltpu.VMEM(own_grads.shape, wide),
+            pltpu.VMEM(grad_mod.shape, wide),
+            held[0],
+            held[1],
+            dma((KINDS, 3)),
+            dma((KINDS, 3)),
+            dma((2,)),
+        ],
+        compiler_params=pltpu.CompilerParams(vmem_limit_bytes=64 * 2**20 - 2**17),
+    )(*weights, *firsts, *seconds, own_grads, grad_mod, timing_all, grad_cond, sums)
+    return out[:7], out[7:14], out[14:21], out[21]
+
+
+def apply_kernel(layers, *refs):
+    norms, weights, updates = refs[0], refs[1:8], refs[8:15]
+    outs, w_buf, u_buf, in_sem, out_sem = refs[15:22], refs[22:29], refs[29:36], refs[36], refs[37]
+    sequence = (5, 6, 3, 4, 1, 0, 2)
+    loads = {}
+    for kind in sequence:
+        loads[kind] = [
+            pltpu.make_async_copy(source[kind], target[kind], in_sem.at[kind, i])
+            for i, (source, target) in enumerate(((weights, w_buf), (updates, u_buf)))
+        ]
+        for copy in loads[kind]:
+            copy.start()
+    lane = lax.broadcasted_iota(jnp.int32, (1, 128), 1)
+    ratio = jnp.sqrt(norms[0:1] + EPS_NORM) / jnp.sqrt(norms[1:2] + EPS_NORM)
+    stores = []
+    for kind in sequence:
+        for copy in loads[kind]:
+            copy.wait()
+        for index, column in pieces_of(kind, w_buf[kind].shape, layers):
+            factor = LEARN_RATE * jnp.sum(jnp.where(lane == column, ratio, 0.0))
+            w_buf[kind][index] = w_buf[kind][index] - factor * u_buf[kind][index]
+        copy = pltpu.make_async_copy(w_buf[kind], outs[kind], out_sem.at[kind])
+        copy.start()
+        stores.append(copy)
+    for copy in stores:
+        copy.wait()
+
+
+def lamb_last(norms, weights, updates):
+    layers = weights[3].shape[0]
+    in_hbm = pl.BlockSpec(memory_space=pl.ANY)
+    wide = jnp.float32
+    held = [pltpu.VMEM(w.shape, wide) for w in weights]
+    dma = pltpu.SemaphoreType.DMA
+    return pl.pallas_call(
+        lambda *refs: apply_kernel(layers, *refs),
+        out_shape=tuple(jax.ShapeDtypeStruct(w.shape, wide) for w in weights),
+        in_specs=[pl.BlockSpec(memory_space=pltpu.VMEM)] + [in_hbm] * 14,
+        out_specs=(in_hbm,) * 7,
+        scratch_shapes=held * 2 + [dma((KINDS, 2)), dma((KINDS,))],
+        compiler_params=pltpu.CompilerParams(vmem_limit_bytes=64 * 2**20 - 2**17),
+    )(norms, *weights, *updates)
+
+
+def turned_views(small, cond, mod, qkv, proj, up, down):
+    return [
+        small,
+        cond.T,
+        mod,
+        qkv.transpose(0, 2, 1, 3),
+        proj.transpose(0, 2, 1),
+        up,
+        down.transpose(0, 2, 1),
+    ]
+
+
 def local(
     latents,
     gaussian,
@@ -1266,7 +1464,26 @@
             float(total_count),
         )
         loss_sum = jnp.sum(sums[0, 0, model_width:])
-        ends, grad_time_act = sums[0, :, :model_width], sums[1, :, :model_width]
+        shares = [1.0 / (dp_count * tensor_count), 1.0 / tensor_count, 1.0 / tensor_count]
+        weights = turned_views(small_w, cond_w, mod_w, qkv_w, proj_w, up_w, down_w)
+        firsts, seconds, updates, squares_sum = lamb_first(
+            weights,
+            turned_views(small_m, cond_m, mod_m, qkv_m, proj_m, up_m, down_m),
+            turned_views(small_v, cond_v, mod_v, qkv_v, proj_v, up_v, down_v),
+            own_grads,
+            grad_mod_w,
+            timing_all,
+            grad_cond,
+            sums,
+            shares + [1.0] * 4,
+        )
+        squares_sum = sum_norms(squares_sum, dp_count)
+        renewed = lamb_last(squares_sum, weights, updates)
+        outputs = []
+        for triple in zip(*(turned_views(*kind) for kind in (renewed, firsts, seconds))):
+            outputs += list(triple)
+        norms = jnp.sqrt(squares_sum[:2, : 3 + 4 * layer_count] + EPS_NORM)
+        return tuple(outputs) + (loss_sum, norms)
     else:
         timing_all = lax.all_gather(timing, "dp", axis=1, tiled=False)
         timing_all = timing_all.reshape(samples * dp_count, -1)
@@ -1414,11 +1631,7 @@
     ]
     updates = [r[2] for r in results]
     total_sq = jnp.stack([squares(weights_list), squares(updates)])
-    if kernels:
-        kinds = total_sq.shape[1]
-        total_sq = sum_norms(jnp.pad(total_sq, ((0, 6), (0, 128 - kinds))), dp_count)[:2, :kinds]
-    else:
-        total_sq = lax.psum(total_sq, ("dp", "tensor"))
+    total_sq = lax.psum(total_sq, ("dp", "tensor"))
     norms = jnp.sqrt(total_sq + EPS_NORM)
     ratio = norms[0] / norms[1]
     outputs = []

time: 383 us -> 354 us (0.924)
  other arithmetic: 47 us -> 9.99 us
  Pallas kernels: 309 us -> 333 us
  local copies, waits for them, and re-layouts: 8.85 us -> 2.05 us
  between operations: 7.28 us -> 1.17 us
    pallas_call x0 -> x2, Pallas kernels: none -> 24.3 us  [the longest x1 16.8 us: lamb_first(): pl.pallas_call(lambda *refs: lamb_kernel(layers, shares, *refs), out_shap...]
    reduce_sum x7 -> x0, other arithmetic: 23 us -> none  [squares(): sums.append(jnp.sum(a * a, axis=axes).reshape(-1) * shares[kind_id])]
    sub x7 -> x0, other arithmetic: 12.2 us -> none  [local(): weights_list[kind_id] - LEARN_RATE * factor * updates[kind_id]]
where the time goes in v5:
time: 354 us; the launch traced here: 348 us
  Pallas kernels  333 us (94%)
  other arithmetic  9.99 us (3%)
    pallas_call x1, Pallas kernels, train_step(): pl.pallas_call(lambda *refs: step_kernel(sizes, layers, total, *refs), ou...  297 us
    pallas_call x1, Pallas kernels, lamb_first(): pl.pallas_call(lambda *refs: lamb_kernel(layers, shares, *refs), out_shap...  16.8 us
    pallas_call x1, Pallas kernels, sum_norms(): pl.pallas_call(lambda *refs: norm_kernel(dp_count, *refs), out_shape=jax....  11.4 us
    pallas_call x1, Pallas kernels, lamb_last(): pl.pallas_call(lambda *refs: apply_kernel(layers, *refs), out_shape=tuple...  7.48 us

profile of v5, /device:TPU:1, one launch (start us, length us, event | category | flops | bytes accessed | tf_op | source)
XLA Modules:
  0.0 347.6 jit_solution(16720028895871467436)
XLA Ops:
  0.7 0.7 convert_element_type.62
  1.3 0.1 broadcast_in_dim.4
  1.4 0.7 broadcast_add_fusion
  2.1 0.1 fusion.2
  2.2 0.8 add_convert_fusion.refs_10_
  3.0 0.7 broadcast_in_dim.5.refs_9_
  3.7 1.0 bitcast_convert_fusion
  4.7 0.7 pad.4.refs_6_
  5.4 1.4 convert_element_type.56
  6.8 0.2 fusion
  6.9 0.6 pad_maximum_fusion.1.refs_5_
  7.6 0.6 slice.22.refs_11_
  8.2 1.0 multiply_sine_fusion.1
  9.2 0.2 pad_maximum_fusion
  9.3 1.2 convolution_add_fusion.refs_4_
  10.5 0.0 copy-done.1
  10.5 0.0 copy-done
  10.5 1.1 convert_element_type.64.refs_7_
  11.6 297.3 %shard_map.425 = (f32[6,48,1536]{2,1,0:T(8,128)}, f32[32,1152]{1,0:T(8,128)}, f32[32,48]{1,0:T(8,128)}, f32[32,48]{1,0:T(8,128)}, f32[48,10752]{1,0:T(8,128)}, /*index=5*/f32[2,32,896]{2,1,0:T(8,128)}) custom-call(f32[2,3,48,384]{3,2,1,0:T(8,128)} %bitcast.32, f32[2,48,384]{2,1,0:T(8,128)} %bitcast.37, f32[2,48,1536]{2,1,0:T(8,128)} %refs_6_.1, ...), custom_call_target="tpu_custom_call" | custom-call | tf_op jit(solution)/shard_map/pallas_call | solution.py:1040
  308.9 1.3 slice_reduce_fusion
  310.2 16.8 %shard_map.426 = (f32[288,768]{1,0:T(8,128)}, f32[48,1769]{1,0:T(8,128)}, f32[48,10752]{1,0:T(8,128)}, f32[2,3,48,384]{3,2,1,0:T(8,128)}, f32[2,48,384]{2,1,0:T(...) custom-call(f32[288,768]{1,0:T(8,128)} %refs_1_.1, ...), custom_call_target="tpu_custom_call" | custom-call | tf_op jit(solution)/shard_map/pallas_call | solution.py:1301
  326.9 11.4 %shard_map.427.refs_0_ = f32[8,128]{1,0:T(8,128)} custom-call(f32[8,128]{1,0:T(8,128)} %get-tuple-element.62.refs_0_), custom_call_target="tpu_custom_call" | custom-call | tf_op jit(solution)/shard_map/pallas_call | solution.py:1155
  338.4 7.5 %shard_map.428 = (f32[288,768]{1,0:T(8,128)}, f32[48,1769]{1,0:T(8,128)}, f32[48,10752]{1,0:T(8,128)}, f32[2,3,48,384]{3,2,1,0:T(8,128)}, f32[2,48,384]{2,1,0:T(...) custom-call(f32[8,128]{1,0:T(8,128)} %shard_map.427.refs_0_, f32[288,768]{1,0:T(8,128)} %refs_1_.1, ...), custom_call_target="tpu_custom_call" | custom-call | tf_op jit(solution)/shard_map/pallas_call | solution.py:1355
  345.9 1.3 add_sqrt_fusion
  (6 shorter events, 0.0 us)
Async XLA Ops:
  3.0 7.5 %copy-start.1 = (bf16[2,16,128]{2,1,0:T(8,128)(2,1)}, bf16[2,16,128]{2,1,0:T(8,128)(2,1)S(1)}, u32[]{:S(2)}) copy-start(bf16[2,16,128]{2,1,0:T(8,128)(2,1)S(1)} %add_convert_fusion.refs_10_) | copy-start | bytes 24580
  5.4 5.1 %copy-start = (f32[48,10752]{1,0:T(8,128)S(1)}, f32[48,10752]{1,0:T(8,128)}, u32[]{:S(2)}) copy-start(f32[48,10752]{1,0:T(8,128)} %refs_3_.1) | copy-start | bytes 6193156

commit v6 on v5

--- a/solution.py
+++ b/solution.py
@@ -207,6 +207,15 @@
 
 ORDERS = ((0, 1, 2), (0, 2, 1))
 LAG = 2
+GATHER_PLAN = (
+    (3, (0, 1, 2)),
+    (3, (0, 2, 1)),
+    (1, (2, 1, 0)),
+    (2, (0, 1, 2)),
+    (2, (0, 2, 1)),
+    (1, (1, 2, 0)),
+)
+GATHER_LAG = 3
 MESH_ID = pl.DeviceIdType.MESH
 NN = (((1,), (0,)), ((), ()))
 NT = (((1,), (1,)), ((), ()))
@@ -286,14 +295,15 @@
         proj_own,
         up_own,
         down_own,
-        hidden_in,
+        small_own,
+        places,
+        latents,
+        gaussian,
+        moments,
         timing,
-        cond_cols,
+        cond_own,
         mod_rows,
         velocity,
-        time_weight,
-        blended,
-        head_rows,
         own_grads,
         timing_all,
         cond_out,
@@ -321,8 +331,10 @@
         resid,
         part,
         turned,
+        cond_cols,
+        end_rows,
+        blended,
         timing_box,
-        mod_part,
         mod_low,
         mod_box,
         mod,
@@ -351,7 +363,7 @@
     my_dp, my_core = lax.axis_index("dp"), lax.axis_index("tensor")
     partner = (my_dp, 1 - my_core)
     waves, rows, columns = 3 * layers, up_own.shape[1], up_own.shape[2]
-    samples, half_rows, width = hidden_in.shape
+    samples, half_rows, width = latents.shape[0], places.shape[0], places.shape[1]
     tokens = 2 * half_rows
     heads_wide = qkv.shape[3] // 3
     pairs = heads_wide // (2 * HDIM)
@@ -379,6 +391,14 @@
         load(proj_own.at[layer], layer, 3 * narrow_wide, narrow_wide, 1)
         load(up_own.at[layer], 2 * layer, 0, columns, 0)
         load(down_own.at[layer], 2 * layer + 1, 0, columns, 0)
+    for row, source in ((0, 0), (PATCH, PATCH + FREQ)):
+        copy = pltpu.make_async_copy(
+            small_own.at[pl.ds(source, PATCH)],
+            end_rows.at[pl.ds(row, PATCH)],
+            load_sem.at[len(loads)],
+        )
+        copy.start()
+        loads.append(copy)
     dp_peers = all_peers(sizes[0] * sizes[1] * sizes[2], False)
     greet(dp_peers + [partner])
 
@@ -400,7 +420,8 @@
             small_unsent.append(copy)
 
     devices = len(dp_peers) + 1
-    mod_part[...] = jnp.zeros_like(mod_part)
+    mod_slots = mod_low.shape[1]
+    part[0] = jnp.zeros((devices * mod_slots, width), jnp.float32)
     mod_grads[...] = jnp.zeros_like(mod_grads)
     time_copies = [
         small(0, i, timing, timing_box.at[my_dp], peer) for i, peer in enumerate(dp_peers)
@@ -421,49 +442,92 @@
     def chunk_place(chunk):
         return chunk // per_wave, pl.ds(chunk % per_wave * tile, tile), ORDERS[chunk % 2]
 
-    def gather_copies(chunk, phase):
-        wave, lanes, order = chunk_place(chunk)
-        axis = order[phase]
-        pick = [spot[a] for a in range(3)]
-        for earlier in order[:phase]:
-            pick[earlier] = slice(None)
-        target = full.at[wave, pick[0], pick[1], pick[2], :, lanes]
-        return [
-            pltpu.make_async_remote_copy(
+    plan = []
+    for wave in range(waves):
+        start = 0
+        for count, order in GATHER_PLAN:
+            plan.append((wave, start, count * (columns // 12), order))
+            start += count * (columns // 12)
+    relay = sizes[0] == 4
+    stage_count = 4 if relay else 3
+
+    def gather_stages(chunk):
+        found = []
+        for position, axis in enumerate(plan[chunk][3]):
+            if axis == 0 and relay:
+                found += [(position, axis, "direct"), (position, axis, "passed")]
+            else:
+                found.append((position, axis, "all"))
+        return found
+
+    def gather_copies(chunk, stage):
+        wave, start, count, order = plan[chunk]
+        position, axis, how = gather_stages(chunk)[stage]
+        line = spot[0]
+
+        def made(slot, source, device):
+            pick = [spot[a] for a in range(3)]
+            for earlier in order[:position]:
+                pick[earlier] = slice(None)
+            pick[axis] = source
+            target = full.at[wave, pick[0], pick[1], pick[2], :, pl.ds(start, count)]
+            return pltpu.make_async_remote_copy(
                 src_ref=target,
                 dst_ref=target,
-                send_sem=ag_send.at[chunk, phase, offset],
-                recv_sem=ag_recv.at[chunk, phase, offset],
-                device_id=peer_of(sizes, spot, axis, (spot[axis] + offset) % sizes[axis]),
+                send_sem=ag_send.at[chunk, position, slot],
+                recv_sem=ag_recv.at[chunk, position, slot],
+                device_id=peer_of(sizes, spot, axis, device),
                 device_id_type=MESH_ID,
             )
-            for offset in range(1, sizes[axis])
-        ]
+
+        if how == "passed":
+            end = jnp.where(line >= 2, 3, 0)
+            inside = (line == 1) | (line == 2)
+            return [(made(0, 3 - end, end), inside, (line == 0) | (line == 3))]
+        found = []
+        for offset in range(1, sizes[axis]):
+            copy = made(offset, spot[axis], (spot[axis] + offset) % sizes[axis])
+            if how == "direct" and offset == 1:
+                found.append((copy, line < 3, line > 0))
+            elif how == "direct" and offset == 3:
+                found.append((copy, line > 0, line < 3))
+            else:
+                found.append((copy, None, None))
+        return found
+
+    def when(condition, action):
+        if condition is None:
+            action()
+        else:
+            pl.when(condition)(action)
 
     gather_state = [0]
+    gather_end = len(plan) + stage_count * GATHER_LAG
 
     def gather_step():
         step = gather_state[0]
         gather_state[0] += 1
-        for phase in reversed(range(4)):
-            chunk = step - LAG * phase
-            if not 0 <= chunk < chunks:
+        for stage in reversed(range(stage_count + 1)):
+            chunk = step - GATHER_LAG * stage
+            if not 0 <= chunk < len(plan):
                 continue
-            if phase > 0:
-                for copy in gather_copies(chunk, phase - 1):
-                    copy.wait_recv()
-            if phase < 3:
-                for copy in gather_copies(chunk, phase):
-                    copy.start()
-                    unsent.append(copy)
+            if stage > 0:
+                for copy, _, here in gather_copies(chunk, stage - 1):
+                    when(here, copy.wait_recv)
+            if stage < stage_count:
+                for copy, there, _ in gather_copies(chunk, stage):
+                    when(there, copy.start)
+                    unsent.append((copy, there))
 
     def gather_until(wave):
-        while gather_state[0] <= per_wave * (wave + 1) - 1 + 3 * LAG:
+        last_chunk = len(GATHER_PLAN) * (wave + 1) - 1
+        while gather_state[0] <= last_chunk + stage_count * GATHER_LAG:
             gather_step()
 
-    def gather_more():
-        if gather_state[0] < chunks + 3 * LAG:
-            gather_step()
+    def gather_more(count=1):
+        for _ in range(count):
+            if gather_state[0] < gather_end:
+                gather_step()
 
     inboxes = (got_one, got_two, got_three)
     rs_unsent = []
@@ -603,7 +667,7 @@
         return full[wave, :, :, :, :, lanes].reshape(width, count)
 
     def layer_input(layer, b):
-        return hidden_in[b] if layer == 0 else hidden[layer - 1, b]
+        return hidden[layer, b]
 
     vectors = mod_rows.shape[1] // width
     per_core = vectors // 2
@@ -623,8 +687,17 @@
     def pair_lanes(kind, p):
         return pl.ds(kind * heads_wide + p * 2 * HDIM, 2 * HDIM)
 
-    gather_more()
-    gather_more()
+    gather_more(GATHER_LAG)
+
+    patch_rows = end_rows[:PATCH].astype(low)
+    head_rows = end_rows[PATCH:].astype(low)
+    for b in range(samples):
+        moment = moments[b]
+        blended[b] = ((1.0 - moment) * latents[b] + moment * gaussian[b]).astype(low)
+        hidden[0, b] = dot(blended[b], patch_rows, TN) + places[...]
+    cond_count = cond_own.shape[1]
+    cond_cols[...] = jnp.zeros_like(cond_cols)
+    cond_cols[:, :cond_count] = cond_own[...].astype(low)
 
     for copy in time_copies:
         copy.wait_recv()
@@ -647,19 +720,18 @@
         got = dot(cond_act, mod_rows[:, lanes], NN)
         for j in range(devices):
             for b in range(samples):
-                at = b * per_core + i
-                mod_part[j, at : at + 1] = got[b * devices + j : b * devices + j + 1]
+                at = j * mod_slots + b * per_core + i
+                part[0, at : at + 1] = got[b * devices + j : b * devices + j + 1]
         if i == per_core // 2:
-            gather_more()
-    gather_more()
-    mod_low[...] = mod_part[...].astype(low)
+            gather_more(1)
+    gather_more(1)
+    mod_low[...] = part[0].reshape(devices, mod_slots, width).astype(low)
     mod_copies = [
         small(1, i, mod_low.at[peer[0]], mod_box.at[i], peer) for i, peer in enumerate(dp_peers)
     ]
     small_start(mod_copies)
-    for _ in range(4):
-        gather_more()
-    total_mod = mod_part[my_dp]
+    gather_more(6)
+    total_mod = part[0, pl.ds(pl.multiple_of(my_dp * mod_slots, mod_slots), mod_slots)]
     for i, copy in enumerate(mod_copies):
         copy.wait_recv()
         total_mod = total_mod + mod_box[i].astype(jnp.float32)
@@ -674,11 +746,11 @@
 
         def first(b):
             if layer == 0:
-                x = hidden_in[b]
+                x = hidden[0, b]
             else:
                 x = middle[layer - 1, b] + vec(b, row - 1) * outer[layer - 1, b]
             if layer > 0:
-                hidden[layer - 1, b] = x
+                hidden[layer, b] = x
             spread(gathered, 2 * layer, sa, b, norm_forward(x, vec(b, row), vec(b, row + 1)))
 
         each_sample(first, gather_more)
@@ -753,8 +825,8 @@
 
         each_sample(third)
 
-    for copy in unsent:
-        copy.wait_send()
+    for copy, there in unsent:
+        when(there, copy.wait_send)
 
     last = layers - 1
     loss_row[...] = jnp.zeros_like(loss_row)
@@ -766,13 +838,13 @@
         shift, scale = vec(b, 6 * layers), vec(b, 6 * layers + 1)
         xh, _ = norm_parts(x)
         normed = (xh * (1.0 + scale) + shift).astype(low)
-        predicted = dot(head_rows[...], normed, NT)
+        predicted = dot(head_rows, normed, NT)
         error = predicted - velocity[b]
-        weighted = time_weight[b] * error
+        weighted = (0.5 + moments[b]) * error
         loss_row[...] += jnp.sum(weighted * error, axis=0, keepdims=True)
         grad_pred = (2.0 * weighted / total_count).astype(low)
         ends[pad, :width] += dot(grad_pred, normed, NN)
-        dx, gshift, gscale = norm_backward(x, scale, dot(grad_pred, head_rows[...], TN))
+        dx, gshift, gscale = norm_backward(x, scale, dot(grad_pred, head_rows, TN))
         mod_grads[b, 6 * layers : 6 * layers + 1] = gshift
         mod_grads[b, 6 * layers + 1 : 6 * layers + 2] = gscale
         resid[b] = dx
@@ -798,7 +870,7 @@
             mod_grads[b, row + 5 : row + 6] = jnp.sum(g * outer[layer, b], axis=0, keepdims=True)
             spread(grad_spread, 2 * layer, se, b, (vec(b, row + 5) * g).astype(low))
 
-        each_sample(grad_first)
+        each_sample(grad_first, reduce_more)
 
         def grad_wide(b):
             spread_copy(grad_spread, 2 * layer, se, b).wait_recv()
@@ -844,7 +916,7 @@
             mod_grads[b, row + 2 : row + 3] = jnp.sum(g * branch[layer, b], axis=0, keepdims=True)
             spread(grad_spread, 2 * layer + 1, sg, b, (vec(b, row + 2) * g).astype(low))
 
-        each_sample(grad_second)
+        each_sample(grad_second, reduce_more)
 
         def grad_attention(b):
             spread_copy(grad_spread, 2 * layer + 1, sg, b).wait_recv()
@@ -1008,14 +1080,14 @@
 
 def train_step(
     own_weights,
-    hidden,
+    places,
+    latents,
+    gaussian,
+    moments,
     timing,
-    cond_cols,
+    cond_own,
     mod_rows,
     velocity,
-    time_weight,
-    blended,
-    head_rows,
     dp_count,
     layers,
     total,
@@ -1023,7 +1095,7 @@
     sizes = grid_of(dp_count)
     rows, columns = own_weights[2].shape[1:]
     waves = 3 * layers
-    samples, half_rows, width = hidden.shape
+    samples, (half_rows, width) = latents.shape[0], places.shape
     tokens = 2 * half_rows
     tile = columns // 4
     chunks = 4 * waves
@@ -1047,7 +1119,7 @@
             jax.ShapeDtypeStruct((rows, mod_rows.shape[1]), wide),
             jax.ShapeDtypeStruct((2, everyone, width + 128), wide),
         ),
-        in_specs=[in_hbm] * 4 + [in_vmem] * 8,
+        in_specs=[in_hbm] * 5 + [in_vmem] * 8,
         out_specs=(in_vmem,) * 4 + (in_hbm, in_vmem),
         scratch_shapes=[
             pltpu.VMEM((waves,) + sizes + (rows, columns), low),
@@ -1060,7 +1132,7 @@
             pltpu.VMEM((4 * layers, samples, half_rows, width), low),
             pltpu.VMEM((layers, samples, tokens, 3 * heads_wide), low),
             pltpu.VMEM((layers, samples, tokens, heads_wide), low),
-            pltpu.VMEM((max(layers - 1, 1),) + resid_shape[1:], wide),
+            pltpu.VMEM(resid_shape, wide),
             pltpu.VMEM(resid_shape, wide),
             pltpu.VMEM(resid_shape, wide),
             pltpu.VMEM(resid_shape, wide),
@@ -1071,8 +1143,10 @@
             pltpu.VMEM((samples, half_rows, width), wide),
             pltpu.VMEM((samples, tokens, width), wide),
             pltpu.VMEM((width, samples * tokens), low),
+            pltpu.VMEM((rows, cond_own.shape[1] + -cond_own.shape[1] % 128), low),
+            pltpu.VMEM((2 * PATCH, width), wide),
+            pltpu.VMEM(latents.shape, low),
             pltpu.VMEM((dp_count,) + timing.shape, wide),
-            pltpu.VMEM((dp_count, slots, width), wide),
             pltpu.VMEM((dp_count, slots, width), low),
             pltpu.VMEM((dp_count - 1, slots, width), low),
             pltpu.VMEM((2, slots, width), wide),
@@ -1088,27 +1162,27 @@
             pltpu.VMEM((2, dp_count, samples, width + 128), wide),
             dma((6, max(dp_count, 8))),
             dma((6, max(dp_count, 8))),
-            dma((chunks, 3, most)),
-            dma((chunks, 3, most)),
+            dma((waves * len(GATHER_PLAN), 3, most)),
+            dma((waves * len(GATHER_PLAN), 3, most)),
             dma((chunks, 3, most)),
             dma((chunks, 3, most)),
             dma((stages, samples)),
             dma((stages, samples)),
-            dma((6 * layers,)),
+            dma((6 * layers + 2,)),
         ],
         compiler_params=pltpu.CompilerParams(
             collective_id=0, has_side_effects=True, vmem_limit_bytes=64 * 2**20 - 2**17
         ),
     )(
         *own_weights,
-        hidden,
+        places,
+        latents,
+        gaussian,
+        moments,
         timing,
-        cond_cols,
+        cond_own,
         mod_rows,
         velocity,
-        time_weight,
-        blended,
-        head_rows,
     )
 
 
@@ -1410,6 +1484,7 @@
     half_rows = latents.shape[2]
     rows = qkv_w.shape[1]
     kernels = rows % 16 == 0 and 2 * layer_count * rows <= 2 * half_rows
+    kernels = kernels and dp_count * 16 == 2 * half_rows
     my_dp = lax.axis_index("dp")
     low = jnp.bfloat16
 
@@ -1422,14 +1497,7 @@
     mod_low = mod_w.astype(low)
 
     moment = (time_ids.astype(jnp.float32) + 0.5) / TSTEPS
-    blended = ((1.0 - moment)[:, None, None] * latents + moment[:, None, None] * gaussian).astype(
-        jnp.bfloat16
-    )
     token_index = lax.axis_index("tensor") * half_rows + jnp.arange(half_rows)
-    hidden = (
-        jnp.einsum("bpn,pd->bnd", blended, patch_rows, preferred_element_type=jnp.float32)
-        + position_table(token_index, model_width)[None]
-    )
     time_weight = 0.5 + moment
     total_count = samples * dp_count * half_rows * tensor_count * PATCH
     features = time_features(moment).astype(low)
@@ -1443,22 +1511,22 @@
         axis=1,
     )
     if kernels:
-        spare = -cond_w.shape[0] % 128
         own_grads, timing_all, cond, grad_cond, grad_mod_w, sums = train_step(
             (
                 qkv_w.transpose(0, 2, 1, 3),
                 proj_w.transpose(0, 2, 1),
                 up_w,
                 down_w.transpose(0, 2, 1),
+                small_w,
             ),
-            hidden,
+            position_table(token_index, model_width),
+            latents,
+            gaussian,
+            jnp.broadcast_to(moment[:, None, None], latents.shape),
             timing,
-            jnp.pad(cond_w.T.astype(low), ((0, 0), (0, spare))),
+            cond_w.T,
             mod_low,
             velocity,
-            jnp.broadcast_to(time_weight[:, None, None], velocity.shape),
-            blended,
-            head_rows,
             dp_count,
             layer_count,
             float(total_count),
@@ -1485,6 +1553,13 @@
         norms = jnp.sqrt(squares_sum[:2, : 3 + 4 * layer_count] + EPS_NORM)
         return tuple(outputs) + (loss_sum, norms)
     else:
+        blended = ((1.0 - moment)[:, None, None] * latents + moment[:, None, None] * gaussian).astype(
+            jnp.bfloat16
+        )
+        hidden = (
+            jnp.einsum("bpn,pd->bnd", blended, patch_rows, preferred_element_type=jnp.float32)
+            + position_table(token_index, model_width)[None]
+        )
         timing_all = lax.all_gather(timing, "dp", axis=1, tiled=False)
         timing_all = timing_all.reshape(samples * dp_count, -1)
         time_act = jax.nn.silu(timing_all[:, :model_width]).astype(low)

time: 354 us -> 340 us (0.960)
  Pallas kernels: 333 us -> 323 us
    pallas_call x1, Pallas kernels: 297 us -> 287 us  [train_step(): pl.pallas_call(lambda *refs: step_kernel(sizes, layers, total, *refs), ou...]
where the time goes in v6:
time: 340 us; the launch traced here: 334 us
  Pallas kernels  323 us (95%)
  other arithmetic  7.71 us (2%)
    pallas_call x1, Pallas kernels, train_step(): pl.pallas_call(lambda *refs: step_kernel(sizes, layers, total, *refs), ou...  287 us
    pallas_call x1, Pallas kernels, lamb_first(): pl.pallas_call(lambda *refs: lamb_kernel(layers, shares, *refs), out_shap...  16.8 us
    pallas_call x1, Pallas kernels, sum_norms(): pl.pallas_call(lambda *refs: norm_kernel(dp_count, *refs), out_shape=jax....  12.6 us
    pallas_call x1, Pallas kernels, lamb_last(): pl.pallas_call(lambda *refs: apply_kernel(layers, *refs), out_shape=tuple...  7.48 us

profile of v6, /device:TPU:1, one launch (start us, length us, event | category | flops | bytes accessed | tf_op | source)
XLA Modules:
  0.0 334.4 jit_solution(17363426961355484890)
XLA Ops:
  0.7 0.0 copy-start
  0.7 0.8 convert_element_type.53
  1.5 0.1 broadcast_in_dim.5
  1.6 0.7 convert_add_fusion
  2.3 0.1 fusion.1
  2.4 1.3 fusion
  3.7 0.6 pad_maximum_fusion.1.refs_9_
  4.3 0.7 broadcast_in_dim.4.refs_8_
  5.0 1.0 multiply_sine_fusion.1
  6.0 0.9 pad_maximum_fusion.refs_5_
  6.9 0.0 copy-done
  6.9 1.1 convert_element_type.54.refs_11_
  7.9 286.6 %shard_map.425 = (f32[6,48,1536]{2,1,0:T(8,128)}, f32[32,1152]{1,0:T(8,128)}, f32[32,48]{1,0:T(8,128)}, f32[32,48]{1,0:T(8,128)}, f32[48,10752]{1,0:T(8,128)}, /*index=5*/f32[2,32,896]{2,1,0:T(8,128)}) custom-call(f32[2,3,48,384]{3,2,1,0:T(8,128)} %bitcast.27, f32[2,48,384]{2,1,0:T(8,128)} %bitcast.33, f32[2,48,1536]{2,1,0:T(8,128)} %refs_6_.3, ...), custom_call_target="tpu_custom_call" | custom-call | tf_op jit(solution)/shard_map/pallas_call | solution.py:1112
  294.5 1.3 slice_reduce_fusion
  295.8 16.8 %shard_map.426 = (f32[288,768]{1,0:T(8,128)}, f32[48,1769]{1,0:T(8,128)}, f32[48,10752]{1,0:T(8,128)}, f32[2,3,48,384]{3,2,1,0:T(8,128)}, f32[2,48,384]{2,1,0:T(...) custom-call(f32[288,768]{1,0:T(8,128)} %refs_1_.1, ...), custom_call_target="tpu_custom_call" | custom-call | tf_op jit(solution)/shard_map/pallas_call | solution.py:1375
  312.6 12.6 %shard_map.427.refs_0_ = f32[8,128]{1,0:T(8,128)} custom-call(f32[8,128]{1,0:T(8,128)} %get-tuple-element.62.refs_0_), custom_call_target="tpu_custom_call" | custom-call | tf_op jit(solution)/shard_map/pallas_call | solution.py:1229
  325.2 7.5 %shard_map.428 = (f32[288,768]{1,0:T(8,128)}, f32[48,1769]{1,0:T(8,128)}, f32[48,10752]{1,0:T(8,128)}, f32[2,3,48,384]{3,2,1,0:T(8,128)}, f32[2,48,384]{2,1,0:T(...) custom-call(f32[8,128]{1,0:T(8,128)} %shard_map.427.refs_0_, f32[288,768]{1,0:T(8,128)} %refs_1_.1, ...), custom_call_target="tpu_custom_call" | custom-call | tf_op jit(solution)/shard_map/pallas_call | solution.py:1429
  332.7 1.3 add_sqrt_fusion
  (4 shorter events, 0.0 us)
Async XLA Ops:
  0.7 6.2 %copy-start = (f32[48,10752]{1,0:T(8,128)S(1)}, f32[48,10752]{1,0:T(8,128)}, u32[]{:S(2)}) copy-start(f32[48,10752]{1,0:T(8,128)} %refs_3_.1) | copy-start | bytes 6193156
